TPU v7x, 512 devices: a whole 4x4x16 slice. The times are simulated.
512 devices in a mesh: seq: 64 (over z, y), head: 2 (over core), base: 4 (over x).
Axes of the slice: x: 4, y: 4, z: 16, core: 2. Of those that a mesh axis runs over, the one named last changes fastest.
Arguments:
- queries: bfloat16 [8192, 2048], P('seq', 'head'), may hold values from -8 to 8
- key_rows: bfloat16 [8192, 2048], P('seq', 'head'), may hold values from -8 to 8
- values: bfloat16 [8192, 2048], P('seq', 'head'), may hold values from -6 to 6
- cotangent: bfloat16 [8192, 2048], P('seq', 'head'), may hold values from -6 to 6
- reference_set: bfloat16 [3, 64, 2048], P(None, None, 'head'), may hold values from -6 to 6
- sample_ids: int32 [4, 8192], P('base'), may hold values from 0 to 63
- mix_weight: float32 [4], P('base'), may hold values from 0.3 to 1
- global_block: int32 [1], replicated, may hold values from 0 to 127
- random_blocks: int32 [16, 128, 2], P('head'), may hold values from 0 to 127, as said below
Outputs:
- attribution: bfloat16 [8192, 2048], P('seq', ('head', 'base'))
Inputs may be any that keep to these rules, and one draw needn't show every extreme that they name: `random_blocks`: for the heads of one index of head, at most 1 random entries of the query blocks of one index of seq fall on the key blocks of any one index of seq, and exactly 1 on some.
All inputs are finite; a program needn't handle non-finite values.
Results may differ from a plain program's by a relative error of at most 0.015.
Values may be sent and summed in bfloat16 or wider, within the bound.
No kernel may reach another device: no remote copies, remote signals or barrier semaphores. Data moves between devices by JAX's collectives and lax.ppermute only.
A program may use at most 64 MiB of HBM per device.

v0:
```python
import math

import jax
import jax.numpy as jnp
from jax import lax
from jax.sharding import PartitionSpec as P

HEAD_DIM = 128
BLOCK = 64
RAND = 2


def extended(cells, sides, width):
    for axis, dim in sides:
        count = lax.axis_size(axis)
        ends = count - 1
        head = lax.slice_in_dim(cells, 0, width, axis=dim)
        tail = lax.slice_in_dim(cells, cells.shape[dim] - width, cells.shape[dim], axis=dim)
        cells = jnp.concatenate(
            [
                lax.ppermute(tail, axis, [(i, (i + 1) % count) for i in range(ends)]),
                cells,
                lax.ppermute(head, axis, [((i + 1) % count, i) for i in range(ends)]),
            ],
            axis=dim,
        )
    return cells


def spread(array, axis, root):
    mine = lax.axis_index(axis) == root
    return lax.psum(jnp.where(mine, array, jnp.zeros_like(array)), axis)


def shifted(value, axis, steps):
    count = lax.axis_size(axis)
    initial, last = (max(0, -steps), min(count, count - steps))
    return lax.ppermute(value, axis, [(source, source + steps) for source in range(initial, last)])


def live_slots(slot_list, block_total):
    inside = (slot_list >= 0) & (slot_list < block_total)
    slot_count = slot_list.shape[-1]
    earlier = slot_list[..., :, None] == slot_list[..., None, :]
    lower_mask = jnp.arange(slot_count)[:, None] > jnp.arange(slot_count)[None, :]
    repeated = jnp.any(earlier & lower_mask, axis=-1)
    return inside & jnp.logical_not(repeated)


def per_device(
    queries,
    key_rows,
    values,
    cotangent,
    reference_set,
    sample_ids,
    mix_weight,
    global_block,
    random_blocks,
):
    seq_count = lax.axis_size("seq")
    seq_rank = lax.axis_index("seq")
    base_count = lax.axis_size("base")
    base_rank = lax.axis_index("base")
    tok_dev, feat_dev = queries.shape
    per_dev = tok_dev // BLOCK
    head_count = feat_dev // HEAD_DIM
    block_total = per_dev * seq_count
    requests = head_count * per_dev * RAND
    capacity = -(-requests // seq_count)
    inv_root = 1.0 / math.sqrt(HEAD_DIM)
    tok_ids = sample_ids[0]
    token_total = tok_ids.shape[0]
    weight = mix_weight[0]
    first_tok = seq_rank * tok_dev
    global_id = global_block[0]
    head_index = jnp.arange(head_count)
    kv_pair = jnp.stack([key_rows, values])
    widened = extended(kv_pair, (("seq", 1),), BLOCK)
    wide_blocks = widened.reshape(2, per_dev + 2, BLOCK, feat_dev)
    wide_pos = jnp.clip(first_tok - BLOCK + jnp.arange(tok_dev + 2 * BLOCK), 0, token_total - 1)
    wide_ids = tok_ids[wide_pos].reshape(per_dev + 2, BLOCK)
    window_raw = jnp.stack(
        [
            wide_blocks[:, 0:per_dev],
            wide_blocks[:, 1 : per_dev + 1],
            wide_blocks[:, 2 : per_dev + 2],
        ],
        axis=2,
    )
    window_ids = jnp.stack(
        [wide_ids[0:per_dev], wide_ids[1 : per_dev + 1], wide_ids[2 : per_dev + 2]], axis=1
    )
    owner_glob = global_id // per_dev
    local_glob = global_id % per_dev
    own_blocks = kv_pair.reshape(2, per_dev, BLOCK, feat_dev)
    glob_local = lax.dynamic_index_in_dim(own_blocks, local_glob, axis=1, keepdims=False)
    glob_kv = spread(glob_local, "seq", owner_glob)
    glob_ids = lax.dynamic_slice_in_dim(tok_ids, global_id * BLOCK, BLOCK)
    request_table = jnp.transpose(
        random_blocks.reshape(head_count, seq_count, per_dev, RAND), (1, 0, 2, 3)
    ).reshape(seq_count, requests)
    head_of = jnp.arange(requests) // (per_dev * RAND)
    owner_table = request_table // per_dev
    order_index = jnp.arange(requests)
    same_owner = owner_table[:, :, None] == owner_table[:, None, :]
    before = order_index[None, :] < order_index[:, None]
    rank_table = jnp.sum(same_owner & before[None], axis=2)
    my_requests = lax.dynamic_index_in_dim(request_table, seq_rank, 0, keepdims=False)
    my_owner = lax.dynamic_index_in_dim(owner_table, seq_rank, 0, keepdims=False)
    my_rank = lax.dynamic_index_in_dim(rank_table, seq_rank, 0, keepdims=False)
    my_slot = my_owner * capacity + my_rank
    wanted = (owner_table == seq_rank)[:, :, None] & (
        rank_table[:, :, None] == jnp.arange(capacity)[None, None, :]
    )
    has_slot = jnp.any(wanted, axis=1).reshape(-1)
    slot_block = jnp.sum(
        jnp.where(wanted, (request_table % per_dev)[:, :, None], 0), axis=1
    ).reshape(-1)
    slot_head = jnp.sum(jnp.where(wanted, head_of[None, :, None], 0), axis=1).reshape(-1)
    slot_pick = slot_block * head_count + slot_head
    own_heads = own_blocks.reshape(2, per_dev, BLOCK, head_count, HEAD_DIM)
    part_rows = BLOCK // base_count
    own_part = lax.dynamic_slice_in_dim(own_heads, base_rank * part_rows, part_rows, axis=2)
    part_shape = (own_part.shape[2], own_part.shape[4])
    own_flat = jnp.transpose(own_part, (0, 1, 3, 2, 4)).reshape(
        (2, per_dev * head_count) + part_shape
    )
    outgoing = jnp.take(own_flat, slot_pick, axis=1)
    outgoing = jnp.where(has_slot[None, :, None, None], outgoing, jnp.zeros_like(outgoing))
    incoming = lax.all_to_all(outgoing, "seq", split_axis=1, concat_axis=1, tiled=True)
    fetched_part = jnp.take(incoming, my_slot, axis=1)
    fetched = lax.all_gather(fetched_part, "base", axis=2, tiled=True)
    random_raw = jnp.transpose(
        fetched.reshape(2, head_count, per_dev, RAND, BLOCK, HEAD_DIM), (0, 2, 1, 3, 4, 5)
    )
    my_lists = my_requests.reshape(head_count, per_dev, RAND)
    random_pos = my_lists[..., None] * BLOCK + jnp.arange(BLOCK)
    random_ids = jnp.transpose(tok_ids[random_pos], (1, 0, 2, 3))
    glob_wide = jnp.broadcast_to(glob_kv[:, None, None], (2, per_dev, 1, BLOCK, feat_dev))
    near_raw = jnp.concatenate([window_raw, glob_wide], axis=2).reshape(
        2, per_dev, 4, BLOCK, head_count, HEAD_DIM
    )
    near_raw = jnp.transpose(near_raw, (0, 1, 4, 2, 3, 5))
    slot_raw = jnp.concatenate([near_raw, random_raw], axis=3)
    key_raw = slot_raw[0]
    value_raw = slot_raw[1]
    near_ids = jnp.concatenate(
        [window_ids, jnp.broadcast_to(glob_ids[None, None], (per_dev, 1, BLOCK))], axis=1
    )
    slot_ids = jnp.concatenate(
        [jnp.broadcast_to(near_ids[:, None], (per_dev, head_count, 4, BLOCK)), random_ids], axis=2
    )
    ref_heads = reference_set.reshape(3, reference_set.shape[1], head_count, HEAD_DIM)
    pick_head = head_index[None, :, None, None]
    base_k = ref_heads[1][slot_ids, pick_head]
    base_v = ref_heads[2][slot_ids, pick_head]
    query_ids = lax.dynamic_slice_in_dim(tok_ids, first_tok, tok_dev).reshape(per_dev, BLOCK)
    q_raw = queries.reshape(per_dev, BLOCK, feat_dev)
    base_q = reference_set[0][query_ids].astype(jnp.float32)
    q_mix = (base_q + weight * (q_raw.astype(jnp.float32) - base_q)).astype(jnp.bfloat16)
    k_mix = (
        base_k.astype(jnp.float32)
        + weight * (key_raw.astype(jnp.float32) - base_k.astype(jnp.float32))
    ).astype(jnp.bfloat16)
    v_mix = (
        base_v.astype(jnp.float32)
        + weight * (value_raw.astype(jnp.float32) - base_v.astype(jnp.float32))
    ).astype(jnp.bfloat16)
    block_pos = seq_rank * per_dev + jnp.arange(per_dev)
    window_list = jnp.stack(
        [block_pos - 1, block_pos, block_pos + 1, jnp.full((per_dev,), global_id)], axis=1
    )
    slot_list = jnp.concatenate(
        [
            jnp.broadcast_to(window_list[:, None], (per_dev, head_count, 4)),
            jnp.transpose(my_lists, (1, 0, 2)),
        ],
        axis=2,
    )
    live_mask = live_slots(slot_list, block_total)
    key_live = jnp.repeat(live_mask, BLOCK, axis=2)[:, :, None, :]
    q_heads = q_mix.reshape(per_dev, BLOCK, head_count, HEAD_DIM)
    k_heads = k_mix.reshape(per_dev, head_count, 6 * BLOCK, HEAD_DIM)
    v_heads = v_mix.reshape(per_dev, head_count, 6 * BLOCK, HEAD_DIM)
    out_heads = cotangent.reshape(per_dev, BLOCK, head_count, HEAD_DIM)
    scores = (
        jnp.einsum("iqhd,ihkd->ihqk", q_heads, k_heads, preferred_element_type=jnp.float32)
        * inv_root
    )
    scores = jnp.where(key_live, scores, -1e30)
    row_peak = jnp.max(scores, axis=-1, keepdims=True)
    exponent = jnp.where(key_live, jnp.exp(scores - row_peak), 0.0)
    weights_soft = exponent / jnp.sum(exponent, axis=-1, keepdims=True)
    probs_low = weights_soft.astype(jnp.bfloat16)
    attended = jnp.einsum("ihqk,ihkd->iqhd", probs_low, v_heads, preferred_element_type=jnp.float32)
    row_term = jnp.sum(out_heads.astype(jnp.float32) * attended, axis=-1)
    dprobs = jnp.einsum("iqhd,ihkd->ihqk", out_heads, v_heads, preferred_element_type=jnp.float32)
    dscore_low = (weights_soft * (dprobs - jnp.swapaxes(row_term, 1, 2)[..., None])).astype(
        jnp.bfloat16
    )
    grad_q = (
        jnp.einsum("ihqk,ihkd->iqhd", dscore_low, k_heads, preferred_element_type=jnp.float32)
        * inv_root
    )
    grad_k = (
        jnp.einsum("ihqk,iqhd->ihkd", dscore_low, q_heads, preferred_element_type=jnp.float32)
        * inv_root
    )
    grad_v = jnp.einsum("ihqk,iqhd->ihkd", probs_low, out_heads, preferred_element_type=jnp.float32)
    query_term = (q_raw.astype(jnp.float32) - base_q) * grad_q.reshape(per_dev, BLOCK, feat_dev)
    live_float = live_mask[:, :, :, None, None].astype(jnp.float32)
    key_term = (
        (key_raw.astype(jnp.float32) - base_k.astype(jnp.float32))
        * grad_k.reshape(per_dev, head_count, 6, BLOCK, HEAD_DIM)
        + (value_raw.astype(jnp.float32) - base_v.astype(jnp.float32))
        * grad_v.reshape(per_dev, head_count, 6, BLOCK, HEAD_DIM)
    ) * live_float
    near_term = jnp.transpose(key_term[:, :, 0:4], (0, 2, 3, 1, 4)).reshape(
        per_dev, 4, BLOCK, feat_dev
    )
    wide_total = jnp.zeros((per_dev + 2, BLOCK, feat_dev), jnp.float32)
    wide_total = wide_total.at[1 : per_dev + 1].add(near_term[:, 1])
    wide_total = wide_total.at[0:per_dev].add(near_term[:, 0])
    wide_total = wide_total.at[2 : per_dev + 2].add(near_term[:, 2])
    local_total = wide_total[1 : per_dev + 1] + query_term
    lower_rim = wide_total[0]
    upper_rim = wide_total[per_dev + 1]
    from_above = shifted(lower_rim.astype(jnp.bfloat16), "seq", -1).astype(lower_rim.dtype)
    from_below = shifted(upper_rim.astype(jnp.bfloat16), "seq", 1).astype(upper_rim.dtype)
    local_total = local_total.at[0].add(from_below)
    local_total = local_total.at[per_dev - 1].add(from_above)
    glob_term = jnp.sum(near_term[:, 3], axis=0)
    is_owner = seq_rank == owner_glob
    place_mask = jnp.arange(per_dev) == local_glob
    glob_total = lax.psum(glob_term, "seq")
    place_weight = (place_mask & is_owner).astype(jnp.float32)
    local_total = local_total + place_weight[:, None, None] * glob_total[None]
    random_term = jnp.transpose(key_term[:, :, 4:], (1, 0, 2, 3, 4)).reshape(
        requests, BLOCK, HEAD_DIM
    )
    reduced = lax.psum_scatter(
        random_term.astype(jnp.bfloat16), "base", scatter_dimension=1, tiled=True
    ).astype(jnp.float32)
    returning = (
        jnp.zeros((seq_count * capacity,) + reduced.shape[1:], jnp.float32).at[my_slot].set(reduced)
    )
    arrived = lax.all_to_all(
        returning.astype(jnp.bfloat16), "seq", split_axis=0, concat_axis=0, tiled=True
    ).astype(returning.dtype)
    arrived = jnp.where(has_slot[:, None, None], arrived, 0.0)
    back_part = (
        jnp.zeros((per_dev * head_count,) + reduced.shape[1:], jnp.float32)
        .at[slot_pick]
        .add(arrived)
    )
    back_part = jnp.transpose(
        back_part.reshape((per_dev, head_count) + reduced.shape[1:]), (0, 2, 1, 3)
    )
    empty_full = jnp.zeros((per_dev, BLOCK, head_count, HEAD_DIM), jnp.float32)
    back_full = lax.dynamic_update_slice_in_dim(
        empty_full, back_part, base_rank * part_rows, axis=1
    )
    local_total = local_total + back_full.reshape(per_dev, BLOCK, feat_dev)
    summed = lax.psum_scatter(
        local_total.reshape(tok_dev, feat_dev).astype(jnp.bfloat16),
        "base",
        scatter_dimension=1,
        tiled=True,
    ).astype(jnp.float32)
    return (summed / base_count).astype(jnp.bfloat16)


def solution(mesh):
    placed = (
        P("seq", "head"),
        P("seq", "head"),
        P("seq", "head"),
        P("seq", "head"),
        P(None, None, "head"),
        P("base", None),
        P("base"),
        P(),
        P("head", None, None),
    )
    return jax.shard_map(
        per_device,
        mesh=mesh,
        in_specs=placed,
        out_specs=P("seq", ("head", "base")),
        check_vma=False,
    )
```

profile of v0, /device:TPU:8, one launch (start us, length us, event | category | flops | bytes accessed | tf_op | source)
XLA Modules:
  0.0 629.9 jit_solution(3468655859286696939)
XLA Ops:
  15.8 18.7 %all-to-all-start = ((bf16[2,64,16,128]{3,2,0,1:T(8,128)(2,1)}), bf16[2,64,16,128]{3,2,0,1:T(8,128)(2,1)S(1)}, u32[]{:S(2)}, u32[]{:S(2)}) async-start(bf16[2,64,16,128]{3,2,0,1:T(8,128)(2,1)} %select_bitcast_fusion), calls=%async_computation | async-start | bytes 1048576 | tf_op jit(solution)/shard_map/all_to_all | solution.py:131
  35.5 3.4 collective-permute-start
  38.8 3.2 collective-permute-start.1
  45.3 11.8 %gather_fusion.3 = s32[2048]{0:T(1024)S(1)} fusion(s32[8192]{0:T(1024)S(1)} %bitcast.217, s32[2048]{0:T(1024)S(1)} %broadcast_clamp_fusion), kind=kCustom, calls=%fused_computation.3 | custom fusion | bytes 24576 | tf_op jit(solution)/shard_map/gather | solution.py:139
  58.6 9.8 %all-to-all-done = bf16[2,64,16,128]{3,2,0,1:T(8,128)(2,1)S(1)} async-done(((bf16[2,64,16,128]{3,2,0,1:T(8,128)(2,1)}), bf16[2,64,16,128]{3,2,0,1:T(8,128)(2,1)S(1)}, u32[]{:S(2)}, u32[]{:S(2)}) %all-to-all-start) | async-done | bytes 524320 | tf_op jit(solution)/shard_map/all_to_all | solution.py:131
  74.7 59.0 %gather_fusion.4 = bf16[6144,128]{1,0:T(8,128)(2,1)} fusion(bf16[64,8,128]{2,1,0:T(8,128)(2,1)S(1)} %bitcast.219, s32[6144]{0:T(1024)S(1)} %reshape.829), kind=kCustom, calls=%fused_computation.4 | custom fusion | bytes 3194880 | tf_op jit(solution)/shard_map/gather | solution.py:156
  133.7 59.0 %gather_fusion.6 = bf16[6144,128]{1,0:T(8,128)(2,1)} fusion(bf16[64,8,128]{2,1,0:T(8,128)(2,1)S(1)} %bitcast.218, s32[6144]{0:T(1024)S(1)} %reshape.829), kind=kCustom, calls=%fused_computation.6 | custom fusion | bytes 3194880 | tf_op jit(solution)/shard_map/gather | solution.py:157
  201.4 80.3 %all-reduce.4.cloned.1.call-done = bf16[2,64,8,128]{3,2,1,0:T(8,128)(2,1)} async-done(((bf16[2,64,8,128]{3,2,1,0:T(8,128)(2,1)}), bf16[2,64,8,128]{3,2,1,0:T(8,128)(2,1)}) %all-reduce.4.cloned.1.call-update) | async-done | bytes 262160 | tf_op jit(solution)/shard_map/psum | solution.py:32
  282.7 2.9 maximum_bitcast_fusion
  288.8 2.3 copy.105
  296.4 6.1 fusion.29
  302.5 3.5 add_convert_fusion
  306.0 4.4 fusion.13
  310.5 2.9 fusion.10
  316.0 11.3 %fusion.3 = f32[2,8,6,64,128]{4,1,3,0,2:T(8,128)S(1)} fusion(f32[2,8,6,64,128]{4,3,2,1,0:T(8,128)S(1)} %bitcast.240, f32[2,8,6,64,128]{4,3,2,1,0:T(8,128)S(1)} %bitcast.221, f32[2,8,6,64,128]{4,3,2,1,0:T(8,128)S(1)} %bitcast.226, f32[2,8,6,64,128]{4,3,2,1,0:T(8,128)S(1)} %bitcast.223, f32[2,8,6]{1,0,2:T(2,128)S(1)} %copy.112, ...), kind=kLoop, calls=%fused_computation.15 | loop fusion | flops 7864320 | bytes 18874752 | tf_op jit(solution)/shard_map/mul | solution.py:213
  335.3 20.9 %reduce-scatter.3.cloned.1.call-done = bf16[32,16,128]{2,1,0:T(8,128)(2,1)} async-done(((bf16[32,64,128]{2,1,0:T(8,128)(2,1)}), bf16[32,16,128]{2,1,0:T(8,128)(2,1)}) %reduce-scatter.3.cloned.1.call-update) | async-done | bytes 131088 | tf_op jit(solution)/shard_map/reduce_scatter | solution.py:242
  359.4 15.8 %all-to-all-start.1 = ((bf16[64,16,128]{2,1,0:T(8,128)(2,1)}), bf16[64,16,128]{2,1,0:T(8,128)(2,1)S(1)}, u32[]{:S(2)}, u32[]{:S(2)}) async-start(bf16[64,16,128]{2,1,0:T(8,128)(2,1)} %convert_element_type.182), calls=%async_computation.2 | async-start | bytes 524288 | tf_op jit(solution)/shard_map/all_to_all | solution.py:248
  375.3 3.4 collective-permute-start.2
  378.7 2.5 collective-permute-start.3
  382.9 3.2 collective-permute-done.3
  386.1 10.4 %all-to-all-done.1 = bf16[64,16,128]{2,1,0:T(8,128)(2,1)S(1)} async-done(((bf16[64,16,128]{2,1,0:T(8,128)(2,1)}), bf16[64,16,128]{2,1,0:T(8,128)(2,1)S(1)}, u32[]{:S(2)}, u32[]{:S(2)}) %all-to-all-start.1) | async-done | bytes 262176 | tf_op jit(solution)/shard_map/all_to_all | solution.py:248
  396.7 3.0 scatter_fusion.1
  399.9 195.2 %all-reduce.6.cloned.1.call-done = f32[64,1024]{1,0:T(8,128)} async-done(((f32[64,1024]{1,0:T(8,128)}), f32[64,1024]{1,0:T(8,128)}) %all-reduce.6.cloned.1.call-update) | async-done | bytes 262160 | tf_op jit(solution)/shard_map/psum | solution.py:236
  596.9 24.0 %reduce-scatter.5.cloned.1.call-done = bf16[128,256]{1,0:T(8,128)(2,1)} async-done(((bf16[128,1024]{1,0:T(8,128)(2,1)}), bf16[128,256]{1,0:T(8,128)(2,1)}) %reduce-scatter.5.cloned.1.call-update) | async-done | bytes 65552 | tf_op jit(solution)/shard_map/reduce_scatter | solution.py:265
  (187 shorter events, 55.8 us)
Async XLA Ops:
  7.4 35.1 %copy-start = (s32[1,8192]{1,0:T(1,128)S(1)}, s32[1,8192]{1,0:T(1,128)}, u32[]{:S(2)}) copy-start(s32[1,8192]{1,0:T(1,128)} %param.24) | copy-start | bytes 98308
  7.4 6.7 %copy-start.12 = (bf16[128,1024]{1,0:T(8,128)(2,1)S(1)}, bf16[128,1024]{1,0:T(8,128)(2,1)}, u32[]{:S(2)}) copy-start(bf16[128,1024]{1,0:T(8,128)(2,1)} %param.20) | copy-start | bytes 786436
  7.4 6.6 %copy-start.13 = (bf16[128,1024]{1,0:T(8,128)(2,1)S(1)}, bf16[128,1024]{1,0:T(8,128)(2,1)}, u32[]{:S(2)}) copy-start(bf16[128,1024]{1,0:T(8,128)(2,1)} %param.21) | copy-start | bytes 786436
  7.4 274.3 %all-reduce.4.cloned.1.call-start = ((), (), s32[]{:S(2)}) async-start(), calls=%async_computation.4 | async-start | bytes 524288 | tf_op jit(solution)/shard_map/psum | solution.py:32
  15.8 52.6 %all-to-all-start = ((bf16[2,64,16,128]{3,2,0,1:T(8,128)(2,1)}), bf16[2,64,16,128]{3,2,0,1:T(8,128)(2,1)S(1)}, u32[]{:S(2)}, u32[]{:S(2)}) async-start(bf16[2,64,16,128]{3,2,0,1:T(8,128)(2,1)} %select_bitcast_fusion), calls=%async_computation | async-start | bytes 1048576 | tf_op jit(solution)/shard_map/all_to_all | solution.py:131
  34.6 251.1 %all-gather.2.cloned.1.call-start = ((), (), s32[]{:S(2)}) async-start(), calls=%async_computation.5 | async-start | bytes 1310720 | tf_op jit(solution)/shard_map/all_gather | solution.py:133
  35.5 161.9 %collective-permute-start = (bf16[2,64,1024]{2,1,0:T(8,128)(2,1)}, bf16[2,64,1024]{2,1,0:T(8,128)(2,1)}, u32[]{:S(2)}, u32[]{:S(2)}) collective-permute-start(bf16[2,64,1024]{2,1,0:T(8,128)(2,1)} %get-tuple-element.76), channel_id=1, source_target_pairs={{0,8},{8,16},{16,24},{24,32},{32,40},{40,48},{48,56},{56,64},{64,7... | collective-permute-start | bytes 786440 | tf_op jit(solution)/shard_map/ppermute | solution.py:21
  38.8 158.5 %collective-permute-start.1 = (bf16[2,64,1024]{2,1,0:T(8,128)(2,1)}, bf16[2,64,1024]{2,1,0:T(8,128)(2,1)}, u32[]{:S(2)}, u32[]{:S(2)}) collective-permute-start(bf16[2,64,1024]{2,1,0:T(8,128)(2,1)} %get-tuple-element.77), channel_id=1, source_target_pairs={{8,0},{16,8},{24,16},{32,24},{40,32},{48,40},{56,48},{64,56},{72,6... | collective-permute-start | bytes 786440 | tf_op jit(solution)/shard_map/ppermute | solution.py:23
  45.3 11.9 %copy-start.23 = (bf16[3,64,1024]{2,1,0:T(8,128)(2,1)S(1)}, bf16[3,64,1024]{2,1,0:T(8,128)(2,1)}, u32[]{:S(2)}) copy-start(bf16[3,64,1024]{2,1,0:T(8,128)(2,1)} %param.23) | copy-start | bytes 1179652
  57.2 12.9 %copy-start.22 = (bf16[128,1024]{1,0:T(8,128)(2,1)S(1)}, bf16[128,1024]{1,0:T(8,128)(2,1)}, u32[]{:S(2)}) copy-start(bf16[128,1024]{1,0:T(8,128)(2,1)} %param.19) | copy-start | bytes 786436
  58.5 13.6 %copy-start.24 = (bf16[128,1024]{1,0:T(8,128)(2,1)S(1)}, bf16[128,1024]{1,0:T(8,128)(2,1)}, u32[]{:S(2)}) copy-start(bf16[128,1024]{1,0:T(8,128)(2,1)} %param.22) | copy-start | bytes 786436
  69.9 286.3 %reduce-scatter.3.cloned.1.call-start = ((), (), s32[]{:S(2)}) async-start(), calls=%async_computation.7 | async-start | bytes 655360 | tf_op jit(solution)/shard_map/reduce_scatter | solution.py:242
  194.6 2.8 copy-start.14
  310.4 3.8 copy-start.5
  310.5 3.8 copy-start.16
  313.4 2.5 copy-start.9
  331.5 263.6 %all-reduce.6.cloned.1.call-start = ((), (), s32[]{:S(2)}) async-start(), calls=%async_computation.6 | async-start | bytes 524288 | tf_op jit(solution)/shard_map/psum | solution.py:236
  333.5 47.7 %copy-start.7 = (bf16[2,8,384,128]{3,2,1,0:T(8,128)(2,1)S(1)}, bf16[2,8,384,128]{3,2,1,0:T(8,128)(2,1)}, u32[]{:S(2)}) copy-start(bf16[2,8,384,128]{3,2,1,0:T(8,128)(2,1)} %copy-done.6) | copy-start | bytes 4718596
  359.4 23.3 %copy-start.21 = (f32[128,1024]{1,0:T(8,128)S(1)}, f32[128,1024]{1,0:T(8,128)}, u32[]{:S(2)}) copy-start(f32[128,1024]{1,0:T(8,128)} %convert_subtract_fusion) | copy-start | bytes 1572868
  359.4 37.2 %all-to-all-start.1 = ((bf16[64,16,128]{2,1,0:T(8,128)(2,1)}), bf16[64,16,128]{2,1,0:T(8,128)(2,1)S(1)}, u32[]{:S(2)}, u32[]{:S(2)}) async-start(bf16[64,16,128]{2,1,0:T(8,128)(2,1)} %convert_element_type.182), calls=%async_computation.2 | async-start | bytes 524288 | tf_op jit(solution)/shard_map/all_to_all | solution.py:248
  375.2 245.7 %reduce-scatter.5.cloned.1.call-start = ((), (), s32[]{:S(2)}) async-start(), calls=%async_computation.8 | async-start | bytes 327680 | tf_op jit(solution)/shard_map/reduce_scatter | solution.py:265
  375.3 7.5 %collective-permute-start.2 = (bf16[64,1024]{1,0:T(8,128)(2,1)}, bf16[64,1024]{1,0:T(8,128)(2,1)S(1)}, u32[]{:S(2)}, u32[]{:S(2)}) collective-permute-start(bf16[64,1024]{1,0:T(8,128)(2,1)} %fusion.33), channel_id=1, source_target_pairs={{0,8},{8,16},{16,24},{24,32},{32,40},{40,48},{48,56},{56,64},{64,7... | collective-permute-start | bytes 393224 | tf_op jit(solution)/shard_map/ppermute | solution.py:38
  378.7 7.4 %collective-permute-start.3 = (bf16[64,1024]{1,0:T(8,128)(2,1)S(1)}, bf16[64,1024]{1,0:T(8,128)(2,1)S(1)}, u32[]{:S(2)}, u32[]{:S(2)}) collective-permute-start(bf16[64,1024]{1,0:T(8,128)(2,1)S(1)} %fusion.34), channel_id=1, source_target_pairs={{8,0},{16,8},{24,16},{32,24},{40,32},{48,40},{56,48},{64,56},{72,6... | collective-permute-start | bytes 393224 | tf_op jit(solution)/shard_map/ppermute | solution.py:38
  396.7 225.6 %copy-start.1 = (s32[1,8192]{1,0:T(1,128)S(1)}, s32[1,8192]{1,0:T(1,128)}, u32[]{:S(2)}) copy-start(s32[1,8192]{1,0:T(1,128)} %param.24) | copy-start | bytes 98308
  (12 other events, 19.7 us)
Sparse Core Ops, SparseCore 0:
  11.6 270.0 all-reduce.3
  336.2 258.8 all-reduce.5
Sparse Core Ops, SparseCore 1:
  70.0 25.2 all-gather.1
  331.6 24.5 reduce-scatter.2
  597.0 23.8 reduce-scatter.4
where the time goes:
time: 630 us
  waiting for transfers between devices  344 us (55%)
  local copies, waits for them, and re-layouts  162 us (26%)
  starting transfers between devices  47.3 us (8%)
  other arithmetic  43.4 us (7%)
  between operations  17.2 us (3%)
  matrix products  16.5 us (3%)
    psum x1, waiting for transfers between devices, per_device(): glob_total = lax.psum(glob_term, 'seq')  195 us
    psum x1, waiting for transfers between devices, spread(): return lax.psum(jnp.where(mine, array, jnp.zeros_like(array)), axis)  80.3 us
    gather x1, local copies, waits for them, and re-layouts, per_device(): base_v = ref_heads[2][slot_ids, pick_head]  59 us
    gather x1, local copies, waits for them, and re-layouts, per_device(): base_k = ref_heads[1][slot_ids, pick_head]  59 us
    reduce_scatter x1, waiting for transfers between devices, per_device(): lax.psum_scatter(local_total.reshape(tok_dev, feat_dev).astype(jnp.bfloat...  24 us
    reduce_scatter x1, waiting for transfers between devices, per_device(): lax.psum_scatter(random_term.astype(jnp.bfloat16), 'base', scatter_dimens...  20.9 us
    all_to_all x1, starting transfers between devices, per_device(): lax.all_to_all(outgoing, 'seq', split_axis=1, concat_axis=1, tiled=True)  18.7 us
    all_to_all x1, starting transfers between devices, per_device(): lax.all_to_all(returning.astype(jnp.bfloat16), 'seq', split_axis=0, conca...  15.8 us
  transfers between devices with their start and end apart: 11, of which 7 were waited for; matrix products, arithmetic and copies ran while one was open for 27% of the time, Pallas kernels for 0%

commit v1 on v0

v1 whole, which is shorter than its diff:
```python
import functools
import math

import jax
import jax.numpy as jnp
from jax import lax
from jax.experimental import pallas as pl
from jax.experimental.pallas import tpu as pltpu
from jax.sharding import PartitionSpec as P

HEAD_DIM = 128
BLOCK = 64
RAND = 2
BF16 = jnp.bfloat16
F32 = jnp.float32


def matmul(left, right, dims):
    return lax.dot_general(left, right, (dims, ((), ())), preferred_element_type=F32)


def attention_kernel(
    samples,
    heads,
    weight_ref,
    live_ref,
    slot_ids_ref,
    query_ids_ref,
    ref_kv_ref,
    ref_q_ref,
    query_ref,
    key_ref,
    value_ref,
    cot_ref,
    below_ref,
    above_ref,
    glob_ref,
    rand_ref,
    local_ref,
    low_rim_ref,
    high_rim_ref,
    glob_term_ref,
    rand_term_ref,
    raw_ref,
    term_ref,
    query_term_ref,
):
    inv_root = 1.0 / math.sqrt(HEAD_DIM)
    bank = ref_q_ref.shape[0]
    near = 6 * BLOCK
    parts, _, _, part_rows, _ = rand_ref.shape
    rank = lax.broadcasted_iota(jnp.int32, (bank, 10 * BLOCK), 0)
    rank_q = lax.broadcasted_iota(jnp.int32, (bank, 2 * BLOCK), 0)
    for head in range(heads):
        cols = slice(head * HEAD_DIM, (head + 1) * HEAD_DIM)
        for kv in range(2):
            own = (key_ref, value_ref)[kv]
            to = slice(kv * HEAD_DIM, (kv + 1) * HEAD_DIM)
            raw_ref[0:64, to] = below_ref[kv, :, cols]
            raw_ref[64:192, to] = own[:, cols]
            raw_ref[192:256, to] = above_ref[kv, :, cols]
            raw_ref[256:320, to] = glob_ref[head, kv]
            raw_ref[320:384, to] = jnp.zeros((BLOCK, HEAD_DIM), BF16)
            for slot in range(2 * RAND):
                for part in range(parts):
                    start = near + slot * BLOCK + part * part_rows
                    raw_ref[start : start + part_rows, to] = rand_ref[
                        part, head * 2 * RAND + slot, kv
                    ]
        live = jnp.concatenate(
            [
                jnp.broadcast_to(live_ref[head, 0:1], (BLOCK, 8 * BLOCK)),
                jnp.broadcast_to(live_ref[head, 1:2], (BLOCK, 8 * BLOCK)),
            ],
            axis=0,
        )
        cot = cot_ref[:, cols]
        for sample in range(samples):
            weight = weight_ref[sample]
            hot = (rank == slot_ids_ref[sample, head]).astype(F32).astype(BF16)
            base = matmul(hot, ref_kv_ref[head], ((0,), (0,)))
            diff = raw_ref[...].astype(F32) - base
            mix = (base + weight * diff).astype(BF16)
            hot_q = (rank_q == query_ids_ref[sample]).astype(F32).astype(BF16)
            base_q = matmul(hot_q, ref_q_ref[:, cols], ((0,), (0,)))
            diff_q = query_ref[:, cols].astype(F32) - base_q
            q_mix = (base_q + weight * diff_q).astype(BF16)
            k_mix = mix[:, 0:HEAD_DIM]
            v_mix = mix[:, HEAD_DIM:]

            def over_keys(rows, keys):
                return jnp.concatenate(
                    [
                        matmul(rows, keys[0:near], ((1,), (1,))),
                        jnp.concatenate(
                            [
                                matmul(rows[0:64], keys[near : near + 128], ((1,), (1,))),
                                matmul(rows[64:128], keys[near + 128 : near + 256], ((1,), (1,))),
                            ],
                            axis=0,
                        ),
                    ],
                    axis=1,
                )

            def to_rows(weights, keys):
                return matmul(weights[:, 0:near], keys[0:near], ((1,), (0,))) + jnp.concatenate(
                    [
                        matmul(weights[0:64, near:], keys[near : near + 128], ((1,), (0,))),
                        matmul(weights[64:128, near:], keys[near + 128 : near + 256], ((1,), (0,))),
                    ],
                    axis=0,
                )

            def to_keys(weights, rows):
                return jnp.concatenate(
                    [
                        matmul(weights[:, 0:near], rows, ((0,), (0,))),
                        matmul(weights[0:64, near:], rows[0:64], ((0,), (0,))),
                        matmul(weights[64:128, near:], rows[64:128], ((0,), (0,))),
                    ],
                    axis=0,
                )

            scores = jnp.where(live > 0.5, over_keys(q_mix, k_mix) * inv_root, -1e30)
            peak = jnp.max(scores, axis=1, keepdims=True)
            exponent = jnp.where(live > 0.5, jnp.exp(scores - peak), 0.0)
            probs = exponent / jnp.sum(exponent, axis=1, keepdims=True)
            probs_low = probs.astype(BF16)
            attended = to_rows(probs_low, v_mix)
            row_term = jnp.sum(cot.astype(F32) * attended, axis=1, keepdims=True)
            dscore = (probs * (over_keys(cot, v_mix) - row_term)).astype(BF16)
            query_term = diff_q * (to_rows(dscore, k_mix) * inv_root)
            term = diff[:, 0:HEAD_DIM] * (to_keys(dscore, q_mix) * inv_root) + diff[
                :, HEAD_DIM:
            ] * to_keys(probs_low, cot)
            if sample == 0:
                term_ref[...] = term
                query_term_ref[...] = query_term
            else:
                term_ref[...] += term
                query_term_ref[...] += query_term
        low_rim_ref[:, cols] = term_ref[0:64].astype(BF16)
        local_ref[:, cols] = term_ref[64:192] + query_term_ref[...]
        high_rim_ref[:, cols] = term_ref[192:256].astype(BF16)
        glob_term_ref[:, cols] = term_ref[256:320]
        for slot in range(2 * RAND):
            for part in range(parts):
                start = near + slot * BLOCK + part * part_rows
                rand_term_ref[part, head * 2 * RAND + slot] = term_ref[
                    start : start + part_rows
                ].astype(BF16)


def attention(
    weights, live, slot_ids, query_ids, ref_kv, ref_q, query, key, value, cot, below, above, glob, rand
):
    samples = weights.shape[0]
    heads = ref_kv.shape[0]
    parts, slots, _, part_rows, _ = rand.shape
    feat = query.shape[1]
    vmem = pl.BlockSpec(memory_space=pltpu.VMEM)
    return pl.pallas_call(
        functools.partial(attention_kernel, samples, heads),
        out_shape=[
            jax.ShapeDtypeStruct((2 * BLOCK, feat), F32),
            jax.ShapeDtypeStruct((BLOCK, feat), BF16),
            jax.ShapeDtypeStruct((BLOCK, feat), BF16),
            jax.ShapeDtypeStruct((BLOCK, feat), F32),
            jax.ShapeDtypeStruct((parts, slots, part_rows, HEAD_DIM), BF16),
        ],
        in_specs=[pl.BlockSpec(memory_space=pltpu.SMEM)] + [vmem] * 13,
        out_specs=[vmem] * 5,
        scratch_shapes=[
            pltpu.VMEM((10 * BLOCK, 2 * HEAD_DIM), BF16),
            pltpu.VMEM((10 * BLOCK, HEAD_DIM), F32),
            pltpu.VMEM((2 * BLOCK, HEAD_DIM), F32),
        ],
        compiler_params=pltpu.CompilerParams(vmem_limit_bytes=32 * 1024 * 1024),
        cost_estimate=pl.CostEstimate(
            flops=900_000_000, bytes_accessed=2_000_000, transcendentals=600_000
        ),
        name="attention",
    )(weights, live, slot_ids, query_ids, ref_kv, ref_q, query, key, value, cot, below, above, glob, rand)


def live_slots(slot_list, block_total):
    inside = (slot_list >= 0) & (slot_list < block_total)
    slot_count = slot_list.shape[-1]
    earlier = slot_list[..., :, None] == slot_list[..., None, :]
    lower_mask = jnp.arange(slot_count)[:, None] > jnp.arange(slot_count)[None, :]
    repeated = jnp.any(earlier & lower_mask, axis=-1)
    return inside & jnp.logical_not(repeated)


def exchange(array, axis):
    return lax.all_to_all(array, axis, 0, 0, tiled=True)


def swapped(array, axis, bit):
    return lax.ppermute(array, axis, [(i, i ^ bit) for i in range(lax.axis_size(axis))])


def take(array, index):
    return array.at[index].get(mode="promise_in_bounds")


def per_device(
    queries,
    key_rows,
    values,
    cotangent,
    reference_set,
    sample_ids,
    mix_weight,
    global_block,
    random_blocks,
):
    seq_count = lax.axis_size("seq")
    seq_rank = lax.axis_index("seq")
    base_count = lax.axis_size("base")
    base_rank = lax.axis_index("base")
    tok_dev, feat_dev = queries.shape
    per_dev = tok_dev // BLOCK
    head_count = feat_dev // HEAD_DIM
    heads = head_count // base_count
    feat = heads * HEAD_DIM
    block_total = per_dev * seq_count
    requests = head_count * per_dev * RAND
    part_rows = BLOCK // base_count
    bank = reference_set.shape[1]
    bits = [1 << i for i in range(seq_count.bit_length() - 1)]
    global_id = global_block[0]

    table = random_blocks.reshape(head_count, seq_count, per_dev, RAND)
    unit = (table % per_dev) * head_count + jnp.arange(head_count)[:, None, None, None]
    wanted = table // per_dev == seq_rank
    pick = jnp.sum(jnp.where(wanted, unit + 1, 0), axis=(0, 2, 3))
    my_table = lax.dynamic_index_in_dim(table, seq_rank, 1, keepdims=False)
    my_owner = (my_table // per_dev).reshape(requests)

    start = base_rank * part_rows

    def row_part(rows):
        cells = rows.reshape(per_dev, BLOCK, head_count, HEAD_DIM)
        cells = lax.dynamic_slice_in_dim(cells, start, part_rows, axis=1)
        return jnp.transpose(cells, (0, 2, 1, 3)).reshape(
            per_dev * head_count, part_rows, HEAD_DIM
        )

    own_units = jnp.stack([row_part(key_rows), row_part(values)], axis=1)
    outgoing = take(own_units, jnp.maximum(pick - 1, 0))
    incoming = exchange(outgoing, "seq")
    fetched = take(incoming, my_owner)
    rand = exchange(fetched, "base").reshape(
        base_count, heads * per_dev * RAND, 2, part_rows, HEAD_DIM
    )

    tok_ids = sample_ids.astype(F32).reshape(-1, HEAD_DIM)
    note = jnp.concatenate(
        [tok_ids, jnp.broadcast_to(mix_weight[:, None], (8, HEAD_DIM))], axis=0
    )
    others = [swapped(note, "base", bit) for bit in (1, 2, 3)]
    notes = jnp.stack([note] + others)
    weights = notes[:, -1, 0]
    ids = notes[:, 0 : tok_ids.shape[0]].astype(jnp.int32).reshape(base_count, block_total, BLOCK)

    def mine(rows):
        return lax.dynamic_slice_in_dim(rows, base_rank * feat, feat, axis=1)

    query, key, value, cot = (mine(rows) for rows in (queries, key_rows, values, cotangent))
    refs = lax.dynamic_slice_in_dim(reference_set, base_rank * feat, feat, axis=2)
    ref_q = refs[0]
    ref_kv = jnp.transpose(refs[1:].reshape(2, bank, heads, HEAD_DIM), (2, 1, 0, 3)).reshape(
        heads, bank, 2 * HEAD_DIM
    )

    pair = jnp.stack([key, value])
    up = [(i, (i + 1) % seq_count) for i in range(seq_count)]
    down = [((i + 1) % seq_count, i) for i in range(seq_count)]
    below = lax.ppermute(pair[:, tok_dev - BLOCK :], "seq", up)
    above = lax.ppermute(pair[:, 0:BLOCK], "seq", down)

    owner_glob = global_id // per_dev
    glob_own = lax.dynamic_slice_in_dim(pair, (global_id % per_dev) * BLOCK, BLOCK, axis=1)
    glob_rows = jnp.transpose(glob_own.reshape(2, BLOCK, heads, HEAD_DIM), (2, 0, 1, 3)).reshape(
        heads * 2 * BLOCK, HEAD_DIM
    )
    distance = owner_glob ^ seq_rank
    for bit in bits:
        came = swapped(glob_rows, "seq", bit)
        glob_rows = jnp.where(distance & -bit == bit, came, glob_rows)
    glob = glob_rows.reshape(heads, 2, BLOCK, HEAD_DIM)

    my_heads = lax.dynamic_slice_in_dim(my_table, base_rank * heads, heads, axis=0)
    block_pos = seq_rank * per_dev + jnp.arange(per_dev)
    window = jnp.stack(
        [block_pos - 1, block_pos, block_pos + 1, jnp.full((per_dev,), global_id)], axis=1
    )
    slot_list = jnp.concatenate(
        [jnp.broadcast_to(window[None], (heads, per_dev, 4)), my_heads], axis=2
    )
    alive = live_slots(slot_list, block_total).astype(F32)
    none = jnp.zeros((heads, 1), F32)
    first = jnp.concatenate([alive[:, 0, 0:3], none, alive[:, 0, 3:4], none, alive[:, 0, 4:]], 1)
    second = jnp.concatenate([none, alive[:, 1, 0:4], none, alive[:, 1, 4:]], 1)
    live = jnp.repeat(jnp.stack([first, second], axis=1), BLOCK, axis=2)
    wide = jnp.clip(seq_rank * per_dev - 1 + jnp.arange(per_dev + 2), 0, block_total - 1)
    near_blocks = jnp.concatenate([wide, global_block, global_block])
    blocks = jnp.concatenate(
        [
            jnp.broadcast_to(near_blocks[None], (heads, per_dev + 4)),
            my_heads.reshape(heads, per_dev * RAND),
        ],
        axis=1,
    )
    slot_ids = ids.at[:, blocks.reshape(-1)].get(mode="promise_in_bounds").reshape(
        base_count, heads, 1, blocks.shape[1] * BLOCK
    )
    query_ids = lax.dynamic_slice_in_dim(ids, seq_rank * per_dev, per_dev, axis=1).reshape(
        base_count, 1, tok_dev
    )

    local, low_rim, high_rim, glob_term, rand_term = attention(
        weights, live, slot_ids, query_ids, ref_kv, ref_q, query, key, value, cot, below, above, glob, rand
    )

    from_above = lax.ppermute(low_rim, "seq", down)
    from_below = lax.ppermute(high_rim, "seq", up)

    for bit in bits:
        glob_term = glob_term + swapped(glob_term.astype(BF16), "seq", bit).astype(F32)

    terms = exchange(rand_term.reshape(-1, part_rows, HEAD_DIM), "base")
    order = jnp.arange(1, requests + 1)
    sent = jnp.sum(
        jnp.where(my_owner[None, :] == jnp.arange(seq_count)[:, None], order[None, :], 0), axis=1
    )
    arrived = exchange(take(terms, jnp.maximum(sent - 1, 0)), "seq")
    units = per_dev * head_count
    place = (pick[None, :] == jnp.arange(1, units + 1)[:, None]).astype(BF16)
    back = matmul(place, arrived, ((1,), (0,)))
    back = jnp.transpose(
        back.astype(BF16).reshape(per_dev, base_count, heads, part_rows, HEAD_DIM), (1, 0, 2, 3, 4)
    )
    back = exchange(back.reshape(-1, part_rows, HEAD_DIM), "base").reshape(
        base_count, per_dev, heads, part_rows, HEAD_DIM
    )
    back = jnp.transpose(back, (1, 0, 3, 2, 4)).reshape(tok_dev, feat).astype(F32)
    glob_rows_total = glob_term
    is_place = (jnp.arange(per_dev) + seq_rank * per_dev == global_id).astype(F32)
    glob_add = (is_place[:, None, None] * glob_rows_total[None]).reshape(tok_dev, feat)
    edges = jnp.concatenate([from_below, from_above], axis=0).astype(F32)
    total = local + edges + glob_add + back
    return (total / base_count).astype(BF16)


def solution(mesh):
    placed = (
        P("seq", "head"),
        P("seq", "head"),
        P("seq", "head"),
        P("seq", "head"),
        P(None, None, "head"),
        P("base", None),
        P("base"),
        P(),
        P("head", None, None),
    )
    return jax.shard_map(
        per_device,
        mesh=mesh,
        in_specs=placed,
        out_specs=P("seq", ("head", "base")),
        check_vma=False,
    )
```

time: 630 us -> 192 us (0.30)
  waiting for transfers between devices: 344 us -> 45.4 us
  local copies, waits for them, and re-layouts: 162 us -> 10.5 us
  starting transfers between devices: 47.3 us -> 120 us
  other arithmetic: 43.4 us -> 2.89 us
  matrix products: 16.5 us -> 0.21 us
  between operations: 17.2 us -> 2.15 us
  Pallas kernels: 0 us -> 9.44 us
    psum x2 -> x0, waiting for transfers between devices: 275 us -> none  [the longest x1 195 us: per_device(): glob_total = lax.psum(glob_term, 'seq')]
    gather x8 -> x5, local copies, waits for them, and re-layouts: 134 us -> 4.71 us  [the longest x3 4.11 us: take(): return array.at[index].get(mode='promise_in_bounds')]
    ppermute x4 -> x19, starting transfers between devices: 12.4 us -> 86.8 us  [the longest x15 76.2 us: swapped(): lax.ppermute(array, axis, [(i, i ^ bit) for i in range(lax.axis_size(axis...]
    reduce_scatter x2 -> x0, waiting for transfers between devices: 44.9 us -> none  [the longest x1 24 us: per_device(): lax.psum_scatter(local_total.reshape(tok_dev, feat_dev).astype(jnp.bfloat...]
    ppermute x4 -> x19, waiting for transfers between devices: 3.17 us -> 32.7 us  [the longest x15 32.7 us: swapped(): lax.ppermute(array, axis, [(i, i ^ bit) for i in range(lax.axis_size(axis...]
    dot_general x6 -> x1, matrix products: 16.5 us -> 0.21 us  [matmul(): lax.dot_general(left, right, (dims, ((), ())), preferred_element_type=F32)]
    convert_element_type x12, other arithmetic: 13.8 us -> 1.69 us  [the longest x1 0.78 us: per_device(): tok_ids = sample_ids.astype(F32).reshape(-1, HEAD_DIM)]
    mul x2 -> x0, other arithmetic: 11.3 us -> none  [the longest x1 11.3 us: per_device(): ((key_raw.astype(jnp.float32) - base_k.astype(jnp.float32)) * grad_k.resh...]
  transfers between devices with their start and end apart: 11 -> 24, of which waited for: 7 -> 10; matrix products, arithmetic and copies ran while one was open for 27% -> 6% of each run, Pallas kernels for 0% -> 0%
where the time goes in v1:
time: 192 us; the launch traced here: 190 us
  starting transfers between devices  120 us (62%)
  waiting for transfers between devices  45.4 us (24%)
  local copies, waits for them, and re-layouts  10.5 us (5%)
  Pallas kernels  9.44 us (5%)
  other arithmetic  2.89 us (2%)
  between operations  2.15 us (1%)
    ppermute x15, starting transfers between devices, swapped(): lax.ppermute(array, axis, [(i, i ^ bit) for i in range(lax.axis_size(axis...  76.2 us
    all_to_all x5, starting transfers between devices, exchange(): return lax.all_to_all(array, axis, 0, 0, tiled=True)  32.9 us
    ppermute x15, waiting for transfers between devices, swapped(): lax.ppermute(array, axis, [(i, i ^ bit) for i in range(lax.axis_size(axis...  32.7 us
    all_to_all x5, waiting for transfers between devices, exchange(): return lax.all_to_all(array, axis, 0, 0, tiled=True)  12.7 us
    pallas_call x1, Pallas kernels, attention(): pl.pallas_call(functools.partial(attention_kernel, samples, heads), out_s...  9.44 us
    ppermute x1, starting transfers between devices, per_device(): from_below = lax.ppermute(high_rim, 'seq', up)  4.14 us
    gather x3, local copies, waits for them, and re-layouts, take(): return array.at[index].get(mode='promise_in_bounds')  4.11 us
  transfers between devices with their start and end apart: 24, of which 10 were waited for; matrix products, arithmetic and copies ran while one was open for 6% of the time, Pallas kernels for 0%

profile of v1, /device:TPU:8, one launch (start us, length us, event | category | flops | bytes accessed | tf_op | source)
XLA Modules:
  0.0 190.2 jit_solution(2768831666489676011)
XLA Ops:
  1.5 4.9 %collective-permute-start.1 = (f32[72,128]{1,0:T(8,128)S(1)}, f32[72,128]{1,0:T(8,128)S(1)}, u32[]{:S(2)}, u32[]{:S(2)}) collective-permute-start(f32[72,128]{1,0:T(8,128)S(1)} %get-tuple-element.21), channel_id=1, source_target_pairs={{0,2},{1,3},{2,0},{3,1},{4,6},{5,7},{6,4},{7,5},{8,10},{9,11},{10,... | collective-permute-start | bytes 110600 | tf_op jit(solution)/shard_map/ppermute | solution.py:201
  13.1 7.8 %collective-permute-start.5 = (bf16[256,128]{1,0:T(8,128)(2,1)S(1)}, bf16[256,128]{1,0:T(8,128)(2,1)S(1)}, u32[]{:S(2)}, u32[]{:S(2)}) collective-permute-start(bf16[256,128]{1,0:T(8,128)(2,1)S(1)} %bitcast.94), channel_id=1, source_target_pairs={{0,8},{8,0},{16,24},{24,16},{32,40},{40,32},{48,56},{56,48},{64,72... | collective-permute-start | bytes 196616 | tf_op jit(solution)/shard_map/ppermute | solution.py:201
  25.8 15.0 %all-to-all-start = ((bf16[64,2,16,128]{3,2,1,0:T(8,128)(2,1)}), bf16[64,2,16,128]{3,2,1,0:T(8,128)(2,1)S(1)}, u32[]{:S(2)}, u32[]{:S(2)}) async-start(bf16[64,2,16,128]{3,2,1,0:T(8,128)(2,1)} %gather_fusion.1), calls=%async_computation | async-start | bytes 1048576 | tf_op jit(solution)/shard_map/all_to_all | solution.py:197
  44.1 4.0 %collective-permute-start.6 = (bf16[256,128]{1,0:T(8,128)(2,1)S(1)}, bf16[256,128]{1,0:T(8,128)(2,1)S(1)}, u32[]{:S(2)}, u32[]{:S(2)}) collective-permute-start(bf16[256,128]{1,0:T(8,128)(2,1)S(1)} %broadcast_select_fusion), channel_id=1, source_target_pairs={{0,16},{8,24},{16,0},{24,8},{32,48},{40,56},{48,32},{56,40},{64,80... | collective-permute-start | bytes 196616 | tf_op jit(solution)/shard_map/ppermute | solution.py:201
  48.2 3.9 %collective-permute-done.6 = bf16[256,128]{1,0:T(8,128)(2,1)S(1)} collective-permute-done((bf16[256,128]{1,0:T(8,128)(2,1)S(1)}, bf16[256,128]{1,0:T(8,128)(2,1)S(1)}, u32[]{:S(2)}, u32[]{:S(2)}) %collective-permute-start.6) | collective-permute-done | bytes 65568 | tf_op jit(solution)/shard_map/ppermute | solution.py:201
  55.3 9.0 %collective-permute-done.7 = bf16[256,128]{1,0:T(8,128)(2,1)S(1)} collective-permute-done((bf16[256,128]{1,0:T(8,128)(2,1)S(1)}, bf16[256,128]{1,0:T(8,128)(2,1)S(1)}, u32[]{:S(2)}, u32[]{:S(2)}) %collective-permute-start.7) | collective-permute-done | bytes 65568 | tf_op jit(solution)/shard_map/ppermute | solution.py:201
  64.3 3.3 %collective-permute-start.8 = (bf16[256,128]{1,0:T(8,128)(2,1)S(1)}, bf16[256,128]{1,0:T(8,128)(2,1)S(1)}, u32[]{:S(2)}, u32[]{:S(2)}) collective-permute-start(bf16[256,128]{1,0:T(8,128)(2,1)S(1)} %broadcast_select_fusion.2), channel_id=1, source_target_pairs={{0,64},{8,72},{16,80},{24,88},{32,96},{40,104},{48,112},{56,120},{... | collective-permute-start | bytes 196616 | tf_op jit(solution)/shard_map/ppermute | solution.py:201
  67.6 4.1 %collective-permute-done.8 = bf16[256,128]{1,0:T(8,128)(2,1)S(1)} collective-permute-done((bf16[256,128]{1,0:T(8,128)(2,1)S(1)}, bf16[256,128]{1,0:T(8,128)(2,1)S(1)}, u32[]{:S(2)}, u32[]{:S(2)}) %collective-permute-start.8) | collective-permute-done | bytes 65568 | tf_op jit(solution)/shard_map/ppermute | solution.py:201
  74.4 6.7 %collective-permute-start.9 = (bf16[256,128]{1,0:T(8,128)(2,1)S(1)}, bf16[256,128]{1,0:T(8,128)(2,1)S(1)}, u32[]{:S(2)}, u32[]{:S(2)}) collective-permute-start(bf16[256,128]{1,0:T(8,128)(2,1)S(1)} %broadcast_select_fusion.3), channel_id=1, source_target_pairs={{0,128},{8,136},{16,144},{24,152},{32,160},{40,168},{48,176},{56,1... | collective-permute-start | bytes 196616 | tf_op jit(solution)/shard_map/ppermute | solution.py:201
  81.4 5.3 %collective-permute-done.9 = bf16[256,128]{1,0:T(8,128)(2,1)S(1)} collective-permute-done((bf16[256,128]{1,0:T(8,128)(2,1)S(1)}, bf16[256,128]{1,0:T(8,128)(2,1)S(1)}, u32[]{:S(2)}, u32[]{:S(2)}) %collective-permute-start.9) | collective-permute-done | bytes 65568 | tf_op jit(solution)/shard_map/ppermute | solution.py:201
  86.7 11.4 %collective-permute-start.10 = (bf16[256,128]{1,0:T(8,128)(2,1)S(1)}, bf16[256,128]{1,0:T(8,128)(2,1)S(1)}, u32[]{:S(2)}, u32[]{:S(2)}) collective-permute-start(bf16[256,128]{1,0:T(8,128)(2,1)S(1)} %broadcast_select_fusion.4), channel_id=1, source_target_pairs={{0,256},{8,264},{16,272},{24,280},{32,288},{40,296},{48,304},{56,3... | collective-permute-start | bytes 196616 | tf_op jit(solution)/shard_map/ppermute | solution.py:201
  100.3 3.9 %all-to-all-start.1 = ((bf16[32,2,16,128]{3,2,1,0:T(8,128)(2,1)}), bf16[32,2,16,128]{3,2,1,0:T(8,128)(2,1)S(1)}, u32[]{:S(2)}, u32[]{:S(2)}) async-start(bf16[32,2,16,128]{3,2,1,0:T(8,128)(2,1)} %gather_fusion.2), calls=%async_computation.1 | async-start | bytes 524288 | tf_op jit(solution)/shard_map/all_to_all | solution.py:197
  104.3 6.6 %all-to-all-done.1 = bf16[32,2,16,128]{3,2,1,0:T(8,128)(2,1)S(1)} async-done(((bf16[32,2,16,128]{3,2,1,0:T(8,128)(2,1)}), bf16[32,2,16,128]{3,2,1,0:T(8,128)(2,1)S(1)}, u32[]{:S(2)}, u32[]{:S(2)}) %all-to-all-start.1) | async-done | bytes 262176 | tf_op jit(solution)/shard_map/all_to_all | solution.py:197
  110.9 9.4 %attention.1 = (f32[128,256]{1,0:T(8,128)S(1)}, bf16[64,256]{1,0:T(8,128)(2,1)S(1)}, bf16[64,256]{1,0:T(8,128)(2,1)S(1)}, f32[64,256]{1,0:T(8,128)S(1)}, bf16[4,8,16,128]{3,2,1,0:T(8,128)(2,1)}) custom-call(f32[4]{0:T(128)S(1)} %maximum_reduce_fusion.weight_ref, f32[2,2,512]{2,1,0:T(2,128)S(1)} %reshape.284.live_ref, ...), custom_call_target="tpu_custom_call" | custom-call | flops 900000000 | bytes 2000000 | tf_op jit(solution)/shard_map/attention/pallas_call | solution.py:163
  122.9 3.3 %all-to-all-start.2 = ((bf16[32,16,128]{2,1,0:T(8,128)(2,1)}), bf16[32,16,128]{2,1,0:T(8,128)(2,1)S(1)}, u32[]{:S(2)}, u32[]{:S(2)}) async-start(bf16[32,16,128]{2,1,0:T(8,128)(2,1)} %bitcast.33), calls=%async_computation.2 | async-start | bytes 262144 | tf_op jit(solution)/shard_map/all_to_all | solution.py:197
  126.3 4.3 %collective-permute-start.14 = (bf16[64,256]{1,0:T(8,128)(2,1)S(1)}, bf16[64,256]{1,0:T(8,128)(2,1)S(1)}, u32[]{:S(2)}, u32[]{:S(2)}) collective-permute-start(bf16[64,256]{1,0:T(8,128)(2,1)S(1)} %fusion.8), channel_id=1, source_target_pairs={{0,16},{8,24},{16,0},{24,8},{32,48},{40,56},{48,32},{56,40},{64,80... | collective-permute-start | bytes 98312 | tf_op jit(solution)/shard_map/ppermute | solution.py:201
  133.5 7.2 %all-to-all-start.3 = ((bf16[64,16,128]{2,1,0:T(8,128)(2,1)}), bf16[64,16,128]{2,1,0:T(8,128)(2,1)S(1)}, u32[]{:S(2)}, u32[]{:S(2)}) async-start(bf16[64,16,128]{2,1,0:T(8,128)(2,1)} %gather_fusion.3), calls=%async_computation.3 | async-start | bytes 524288 | tf_op jit(solution)/shard_map/all_to_all | solution.py:197
  140.8 3.4 %collective-permute-start.15 = (bf16[64,256]{1,0:T(8,128)(2,1)S(1)}, bf16[64,256]{1,0:T(8,128)(2,1)S(1)}, u32[]{:S(2)}, u32[]{:S(2)}) collective-permute-start(bf16[64,256]{1,0:T(8,128)(2,1)S(1)} %fusion.22), channel_id=1, source_target_pairs={{0,32},{8,40},{16,48},{24,56},{32,0},{40,8},{48,16},{56,24},{64,96... | collective-permute-start | bytes 98312 | tf_op jit(solution)/shard_map/ppermute | solution.py:201
  144.2 6.2 %collective-permute-done.15 = bf16[64,256]{1,0:T(8,128)(2,1)S(1)} collective-permute-done((bf16[64,256]{1,0:T(8,128)(2,1)S(1)}, bf16[64,256]{1,0:T(8,128)(2,1)S(1)}, u32[]{:S(2)}, u32[]{:S(2)}) %collective-permute-start.15) | collective-permute-done | bytes 32800 | tf_op jit(solution)/shard_map/ppermute | solution.py:201
  150.4 3.7 %collective-permute-start.16 = (bf16[64,256]{1,0:T(8,128)(2,1)S(1)}, bf16[64,256]{1,0:T(8,128)(2,1)S(1)}, u32[]{:S(2)}, u32[]{:S(2)}) collective-permute-start(bf16[64,256]{1,0:T(8,128)(2,1)S(1)} %fusion.9), channel_id=1, source_target_pairs={{0,64},{8,72},{16,80},{24,88},{32,96},{40,104},{48,112},{56,120},{... | collective-permute-start | bytes 98312 | tf_op jit(solution)/shard_map/ppermute | solution.py:201
  157.2 7.0 %collective-permute-start.17 = (bf16[64,256]{1,0:T(8,128)(2,1)S(1)}, bf16[64,256]{1,0:T(8,128)(2,1)S(1)}, u32[]{:S(2)}, u32[]{:S(2)}) collective-permute-start(bf16[64,256]{1,0:T(8,128)(2,1)S(1)} %get-tuple-element.15), channel_id=1, source_target_pairs={{0,128},{8,136},{16,144},{24,152},{32,160},{40,168},{48,176},{56,1... | collective-permute-start | bytes 98312 | tf_op jit(solution)/shard_map/ppermute | solution.py:201
  164.3 4.1 %collective-permute-start.11 = (bf16[64,256]{1,0:T(8,128)(2,1)S(1)}, bf16[64,256]{1,0:T(8,128)(2,1)S(1)}, u32[]{:S(2)}, u32[]{:S(2)}) collective-permute-start(bf16[64,256]{1,0:T(8,128)(2,1)S(1)} %get-tuple-element.11), channel_id=1, source_target_pairs={{0,8},{8,16},{16,24},{24,32},{32,40},{40,48},{48,56},{56,64},{64,7... | collective-permute-start | bytes 98312 | tf_op jit(solution)/shard_map/ppermute | solution.py:329
  170.4 9.2 %collective-permute-start.18 = (bf16[64,256]{1,0:T(8,128)(2,1)S(1)}, bf16[64,256]{1,0:T(8,128)(2,1)S(1)}, u32[]{:S(2)}, u32[]{:S(2)}) collective-permute-start(bf16[64,256]{1,0:T(8,128)(2,1)S(1)} %fusion.10), channel_id=1, source_target_pairs={{0,256},{8,264},{16,272},{24,280},{32,288},{40,296},{48,304},{56,3... | collective-permute-start | bytes 98312 | tf_op jit(solution)/shard_map/ppermute | solution.py:201
  185.0 4.4 %all-to-all-done.4 = bf16[16,16,128]{2,1,0:T(8,128)(2,1)S(1)} async-done(((bf16[16,16,128]{2,1,0:T(8,128)(2,1)}), bf16[16,16,128]{2,1,0:T(8,128)(2,1)S(1)}, u32[]{:S(2)}, u32[]{:S(2)}) %all-to-all-start.4) | async-done | bytes 65568 | tf_op jit(solution)/shard_map/all_to_all | solution.py:197
  (131 shorter events, 39.8 us)
Async XLA Ops:
  1.5 72.8 %collective-permute-start.1 = (f32[72,128]{1,0:T(8,128)S(1)}, f32[72,128]{1,0:T(8,128)S(1)}, u32[]{:S(2)}, u32[]{:S(2)}) collective-permute-start(f32[72,128]{1,0:T(8,128)S(1)} %get-tuple-element.21), channel_id=1, source_target_pairs={{0,2},{1,3},{2,0},{3,1},{4,6},{5,7},{6,4},{7,5},{8,10},{9,11},{10,... | collective-permute-start | bytes 110600 | tf_op jit(solution)/shard_map/ppermute | solution.py:201
  6.4 74.6 %collective-permute-start = (f32[72,128]{1,0:T(8,128)S(1)}, f32[72,128]{1,0:T(8,128)S(1)}, u32[]{:S(2)}, u32[]{:S(2)}) collective-permute-start(f32[72,128]{1,0:T(8,128)S(1)} %get-tuple-element.21), channel_id=1, source_target_pairs={{0,1},{1,0},{2,3},{3,2},{4,5},{5,4},{6,7},{7,6},{8,9},{9,8},{10,11... | collective-permute-start | bytes 110600 | tf_op jit(solution)/shard_map/ppermute | solution.py:201
  9.0 72.1 %collective-permute-start.2 = (f32[72,128]{1,0:T(8,128)S(1)}, f32[72,128]{1,0:T(8,128)S(1)}, u32[]{:S(2)}, u32[]{:S(2)}) collective-permute-start(f32[72,128]{1,0:T(8,128)S(1)} %get-tuple-element.21), channel_id=1, source_target_pairs={{0,3},{1,2},{2,1},{3,0},{4,7},{5,6},{6,5},{7,4},{8,11},{9,10},{10,... | collective-permute-start | bytes 110600 | tf_op jit(solution)/shard_map/ppermute | solution.py:201
  13.1 31.0 %collective-permute-start.5 = (bf16[256,128]{1,0:T(8,128)(2,1)S(1)}, bf16[256,128]{1,0:T(8,128)(2,1)S(1)}, u32[]{:S(2)}, u32[]{:S(2)}) collective-permute-start(bf16[256,128]{1,0:T(8,128)(2,1)S(1)} %bitcast.94), channel_id=1, source_target_pairs={{0,8},{8,0},{16,24},{24,16},{32,40},{40,32},{48,56},{56,48},{64,72... | collective-permute-start | bytes 196616 | tf_op jit(solution)/shard_map/ppermute | solution.py:201
  20.9 83.4 %collective-permute-start.3 = (bf16[2,64,256]{2,1,0:T(8,128)(2,1)S(1)}, bf16[2,64,256]{2,1,0:T(8,128)(2,1)S(1)}, u32[]{:S(2)}, u32[]{:S(2)}) collective-permute-start(bf16[2,64,256]{2,1,0:T(8,128)(2,1)S(1)} %get-tuple-element.18), channel_id=1, source_target_pairs={{0,8},{8,16},{16,24},{24,32},{32,40},{40,48},{48,56},{56,64},{64,7... | collective-permute-start | bytes 196616 | tf_op jit(solution)/shard_map/ppermute | solution.py:281
  25.8 73.3 %all-to-all-start = ((bf16[64,2,16,128]{3,2,1,0:T(8,128)(2,1)}), bf16[64,2,16,128]{3,2,1,0:T(8,128)(2,1)S(1)}, u32[]{:S(2)}, u32[]{:S(2)}) async-start(bf16[64,2,16,128]{3,2,1,0:T(8,128)(2,1)} %gather_fusion.1), calls=%async_computation | async-start | bytes 1048576 | tf_op jit(solution)/shard_map/all_to_all | solution.py:197
  44.1 7.9 %collective-permute-start.6 = (bf16[256,128]{1,0:T(8,128)(2,1)S(1)}, bf16[256,128]{1,0:T(8,128)(2,1)S(1)}, u32[]{:S(2)}, u32[]{:S(2)}) collective-permute-start(bf16[256,128]{1,0:T(8,128)(2,1)S(1)} %broadcast_select_fusion), channel_id=1, source_target_pairs={{0,16},{8,24},{16,0},{24,8},{32,48},{40,56},{48,32},{56,40},{64,80... | collective-permute-start | bytes 196616 | tf_op jit(solution)/shard_map/ppermute | solution.py:201
  52.0 12.2 %collective-permute-start.7 = (bf16[256,128]{1,0:T(8,128)(2,1)S(1)}, bf16[256,128]{1,0:T(8,128)(2,1)S(1)}, u32[]{:S(2)}, u32[]{:S(2)}) collective-permute-start(bf16[256,128]{1,0:T(8,128)(2,1)S(1)} %broadcast_select_fusion.1), channel_id=1, source_target_pairs={{0,32},{8,40},{16,48},{24,56},{32,0},{40,8},{48,16},{56,24},{64,96... | collective-permute-start | bytes 196616 | tf_op jit(solution)/shard_map/ppermute | solution.py:201
  64.3 7.4 %collective-permute-start.8 = (bf16[256,128]{1,0:T(8,128)(2,1)S(1)}, bf16[256,128]{1,0:T(8,128)(2,1)S(1)}, u32[]{:S(2)}, u32[]{:S(2)}) collective-permute-start(bf16[256,128]{1,0:T(8,128)(2,1)S(1)} %broadcast_select_fusion.2), channel_id=1, source_target_pairs={{0,64},{8,72},{16,80},{24,88},{32,96},{40,104},{48,112},{56,120},{... | collective-permute-start | bytes 196616 | tf_op jit(solution)/shard_map/ppermute | solution.py:201
  71.7 32.6 %collective-permute-start.4 = (bf16[2,64,256]{2,1,0:T(8,128)(2,1)S(1)}, bf16[2,64,256]{2,1,0:T(8,128)(2,1)S(1)}, u32[]{:S(2)}, u32[]{:S(2)}) collective-permute-start(bf16[2,64,256]{2,1,0:T(8,128)(2,1)S(1)} %get-tuple-element.19), channel_id=1, source_target_pairs={{8,0},{16,8},{24,16},{32,24},{40,32},{48,40},{56,48},{64,56},{72,6... | collective-permute-start | bytes 196616 | tf_op jit(solution)/shard_map/ppermute | solution.py:282
  74.4 12.3 %collective-permute-start.9 = (bf16[256,128]{1,0:T(8,128)(2,1)S(1)}, bf16[256,128]{1,0:T(8,128)(2,1)S(1)}, u32[]{:S(2)}, u32[]{:S(2)}) collective-permute-start(bf16[256,128]{1,0:T(8,128)(2,1)S(1)} %broadcast_select_fusion.3), channel_id=1, source_target_pairs={{0,128},{8,136},{16,144},{24,152},{32,160},{40,168},{48,176},{56,1... | collective-permute-start | bytes 196616 | tf_op jit(solution)/shard_map/ppermute | solution.py:201
  86.7 17.6 %collective-permute-start.10 = (bf16[256,128]{1,0:T(8,128)(2,1)S(1)}, bf16[256,128]{1,0:T(8,128)(2,1)S(1)}, u32[]{:S(2)}, u32[]{:S(2)}) collective-permute-start(bf16[256,128]{1,0:T(8,128)(2,1)S(1)} %broadcast_select_fusion.4), channel_id=1, source_target_pairs={{0,256},{8,264},{16,272},{24,280},{32,288},{40,296},{48,304},{56,3... | collective-permute-start | bytes 196616 | tf_op jit(solution)/shard_map/ppermute | solution.py:201
  100.3 10.6 %all-to-all-start.1 = ((bf16[32,2,16,128]{3,2,1,0:T(8,128)(2,1)}), bf16[32,2,16,128]{3,2,1,0:T(8,128)(2,1)S(1)}, u32[]{:S(2)}, u32[]{:S(2)}) async-start(bf16[32,2,16,128]{3,2,1,0:T(8,128)(2,1)} %gather_fusion.2), calls=%async_computation.1 | async-start | bytes 524288 | tf_op jit(solution)/shard_map/all_to_all | solution.py:197
  120.4 5.9 %collective-permute-start.13 = (bf16[64,256]{1,0:T(8,128)(2,1)S(1)}, bf16[64,256]{1,0:T(8,128)(2,1)S(1)}, u32[]{:S(2)}, u32[]{:S(2)}) collective-permute-start(bf16[64,256]{1,0:T(8,128)(2,1)S(1)} %convert_element_type.79), channel_id=1, source_target_pairs={{0,8},{8,0},{16,24},{24,16},{32,40},{40,32},{48,56},{56,48},{64,72... | collective-permute-start | bytes 98312 | tf_op jit(solution)/shard_map/ppermute | solution.py:201
  122.9 9.3 %all-to-all-start.2 = ((bf16[32,16,128]{2,1,0:T(8,128)(2,1)}), bf16[32,16,128]{2,1,0:T(8,128)(2,1)S(1)}, u32[]{:S(2)}, u32[]{:S(2)}) async-start(bf16[32,16,128]{2,1,0:T(8,128)(2,1)} %bitcast.33), calls=%async_computation.2 | async-start | bytes 262144 | tf_op jit(solution)/shard_map/all_to_all | solution.py:197
  126.3 14.5 %collective-permute-start.14 = (bf16[64,256]{1,0:T(8,128)(2,1)S(1)}, bf16[64,256]{1,0:T(8,128)(2,1)S(1)}, u32[]{:S(2)}, u32[]{:S(2)}) collective-permute-start(bf16[64,256]{1,0:T(8,128)(2,1)S(1)} %fusion.8), channel_id=1, source_target_pairs={{0,16},{8,24},{16,0},{24,8},{32,48},{40,56},{48,32},{56,40},{64,80... | collective-permute-start | bytes 98312 | tf_op jit(solution)/shard_map/ppermute | solution.py:201
  133.5 46.1 %all-to-all-start.3 = ((bf16[64,16,128]{2,1,0:T(8,128)(2,1)}), bf16[64,16,128]{2,1,0:T(8,128)(2,1)S(1)}, u32[]{:S(2)}, u32[]{:S(2)}) async-start(bf16[64,16,128]{2,1,0:T(8,128)(2,1)} %gather_fusion.3), calls=%async_computation.3 | async-start | bytes 524288 | tf_op jit(solution)/shard_map/all_to_all | solution.py:197
  140.8 9.6 %collective-permute-start.15 = (bf16[64,256]{1,0:T(8,128)(2,1)S(1)}, bf16[64,256]{1,0:T(8,128)(2,1)S(1)}, u32[]{:S(2)}, u32[]{:S(2)}) collective-permute-start(bf16[64,256]{1,0:T(8,128)(2,1)S(1)} %fusion.22), channel_id=1, source_target_pairs={{0,32},{8,40},{16,48},{24,56},{32,0},{40,8},{48,16},{56,24},{64,96... | collective-permute-start | bytes 98312 | tf_op jit(solution)/shard_map/ppermute | solution.py:201
  150.4 6.7 %collective-permute-start.16 = (bf16[64,256]{1,0:T(8,128)(2,1)S(1)}, bf16[64,256]{1,0:T(8,128)(2,1)S(1)}, u32[]{:S(2)}, u32[]{:S(2)}) collective-permute-start(bf16[64,256]{1,0:T(8,128)(2,1)S(1)} %fusion.9), channel_id=1, source_target_pairs={{0,64},{8,72},{16,80},{24,88},{32,96},{40,104},{48,112},{56,120},{... | collective-permute-start | bytes 98312 | tf_op jit(solution)/shard_map/ppermute | solution.py:201
  157.2 13.2 %collective-permute-start.17 = (bf16[64,256]{1,0:T(8,128)(2,1)S(1)}, bf16[64,256]{1,0:T(8,128)(2,1)S(1)}, u32[]{:S(2)}, u32[]{:S(2)}) collective-permute-start(bf16[64,256]{1,0:T(8,128)(2,1)S(1)} %get-tuple-element.15), channel_id=1, source_target_pairs={{0,128},{8,136},{16,144},{24,152},{32,160},{40,168},{48,176},{56,1... | collective-permute-start | bytes 98312 | tf_op jit(solution)/shard_map/ppermute | solution.py:201
  164.3 25.2 %collective-permute-start.11 = (bf16[64,256]{1,0:T(8,128)(2,1)S(1)}, bf16[64,256]{1,0:T(8,128)(2,1)S(1)}, u32[]{:S(2)}, u32[]{:S(2)}) collective-permute-start(bf16[64,256]{1,0:T(8,128)(2,1)S(1)} %get-tuple-element.11), channel_id=1, source_target_pairs={{0,8},{8,16},{16,24},{24,32},{32,40},{40,48},{48,56},{56,64},{64,7... | collective-permute-start | bytes 98312 | tf_op jit(solution)/shard_map/ppermute | solution.py:329
  168.5 21.0 %collective-permute-start.12 = (bf16[64,256]{1,0:T(8,128)(2,1)S(1)}, bf16[64,256]{1,0:T(8,128)(2,1)S(1)}, u32[]{:S(2)}, u32[]{:S(2)}) collective-permute-start(bf16[64,256]{1,0:T(8,128)(2,1)S(1)} %get-tuple-element.12), channel_id=1, source_target_pairs={{8,0},{16,8},{24,16},{32,24},{40,32},{48,40},{56,48},{64,56},{72,6... | collective-permute-start | bytes 98312 | tf_op jit(solution)/shard_map/ppermute | solution.py:328
  170.4 14.5 %collective-permute-start.18 = (bf16[64,256]{1,0:T(8,128)(2,1)S(1)}, bf16[64,256]{1,0:T(8,128)(2,1)S(1)}, u32[]{:S(2)}, u32[]{:S(2)}) collective-permute-start(bf16[64,256]{1,0:T(8,128)(2,1)S(1)} %fusion.10), channel_id=1, source_target_pairs={{0,256},{8,264},{16,272},{24,280},{32,288},{40,296},{48,304},{56,3... | collective-permute-start | bytes 98312 | tf_op jit(solution)/shard_map/ppermute | solution.py:201
  180.5 8.9 %all-to-all-start.4 = ((bf16[16,16,128]{2,1,0:T(8,128)(2,1)}), bf16[16,16,128]{2,1,0:T(8,128)(2,1)S(1)}, u32[]{:S(2)}, u32[]{:S(2)}) async-start(bf16[16,16,128]{2,1,0:T(8,128)(2,1)} %bitcast.36), calls=%async_computation.4 | async-start | bytes 131072 | tf_op jit(solution)/shard_map/all_to_all | solution.py:197
  (4 other events, 63.3 us)

commit v2 on v1

v2 whole, which is shorter than its diff:
```python
import functools
import math

import jax
import jax.numpy as jnp
from jax import lax
from jax.experimental import pallas as pl
from jax.experimental.pallas import tpu as pltpu
from jax.sharding import PartitionSpec as P

HEAD_DIM = 128
BLOCK = 64
RAND = 2
SEQ_MINOR = 4
PIECE = 8
NOTE_ROWS = 16
NEAR = 6 * BLOCK
BF16 = jnp.bfloat16
F32 = jnp.float32
VMEM = pl.BlockSpec(memory_space=pltpu.VMEM)
SMEM = pl.BlockSpec(memory_space=pltpu.SMEM)


def matmul(left, right, dims):
    return lax.dot_general(left, right, (dims, ((), ())), preferred_element_type=F32)


def columns(first):
    return pl.ds(pl.multiple_of(first, HEAD_DIM), HEAD_DIM)


def prepare_kernel(
    part_rows, heads, glob_ref, pick_ref, key_ref, value_ref, outgoing_ref, low_ref, high_ref
):
    base_rank = lax.axis_index("base")
    head_count = key_ref.shape[1] // HEAD_DIM
    glob_start = pl.multiple_of((glob_ref[0] % 2) * BLOCK, BLOCK)
    for slot in range(pick_ref.shape[0]):
        unit = jnp.maximum(pick_ref[slot] - 1, 0)
        rows = pl.ds(
            pl.multiple_of((unit // head_count) * BLOCK + base_rank * part_rows, part_rows),
            part_rows,
        )
        cols = columns((unit % head_count) * HEAD_DIM)
        outgoing_ref[slot, 0:part_rows] = key_ref[rows, cols]
        outgoing_ref[slot, part_rows : 2 * part_rows] = value_ref[rows, cols]
    pieces = heads * 2 * BLOCK // PIECE
    for head in range(heads):
        cols = columns((base_rank * heads + head) * HEAD_DIM)
        for kv in range(2):
            own = (key_ref, value_ref)[kv]
            unit = slice((head * 2 + kv) * BLOCK, (head * 2 + kv + 1) * BLOCK)
            low_ref[unit] = own[0:BLOCK, cols]
            high_ref[unit] = own[BLOCK:, cols]
            rows = own[pl.ds(glob_start, BLOCK), cols].astype(F32)
            for i in range(BLOCK // PIECE):
                piece = rows[i * PIECE : (i + 1) * PIECE].astype(BF16)
                first = (head * 2 + kv) * (BLOCK // PIECE) + i
                for slot in range(first, pick_ref.shape[0], pieces):
                    outgoing_ref[slot, 2 * part_rows :] = piece


def prepare(glob_block, pick, key_rows, value_rows, part_rows, heads):
    edge = jax.ShapeDtypeStruct((heads * 2 * BLOCK, HEAD_DIM), BF16)
    return pl.pallas_call(
        functools.partial(prepare_kernel, part_rows, heads),
        out_shape=[
            jax.ShapeDtypeStruct((pick.shape[0], 2 * part_rows + PIECE, HEAD_DIM), BF16),
            edge,
            edge,
        ],
        in_specs=[SMEM, SMEM, VMEM, VMEM],
        out_specs=[VMEM] * 3,
        cost_estimate=pl.CostEstimate(flops=0, bytes_accessed=1_400_000, transcendentals=0),
        name="prepare",
    )(glob_block, pick, key_rows, value_rows)


def gather_kernel(
    part_rows, block_total, place_ref, table_ref, weight_ref, ids_ref, incoming_ref, *out_refs
):
    requests = table_ref.shape[0] // len(out_refs)
    lane = lax.broadcasted_iota(jnp.int32, (1, HEAD_DIM), 1)

    def block_row(block, half):
        row = ids_ref[pl.ds(block // 2, 1), :]
        return jnp.where(block % 2 == half, row, pltpu.roll(row, BLOCK, 1))

    def pair_row(left, right):
        return jnp.where(lane < BLOCK, block_row(left, 0), block_row(right, 1))

    first = place_ref[0] * 2
    glob = place_ref[2]
    below = jnp.maximum(first - 1, 0)
    above = jnp.minimum(first + 2, block_total - 1)
    shared = [pair_row(below, first), pair_row(first + 1, above), pair_row(glob, glob)]
    own = [pair_row(first, first + 1)]
    weight = jnp.full((1, HEAD_DIM), weight_ref[0], F32)
    high = weight.astype(BF16).astype(F32)
    rest = weight - high
    middle = rest.astype(BF16).astype(F32)
    pieces = jnp.where(lane == 0, high, jnp.where(lane == 1, middle, rest - middle))
    blank = jnp.zeros((NOTE_ROWS - 5 - requests // 2, HEAD_DIM), F32)
    for step, out_ref in enumerate(out_refs):
        base = place_ref[1] ^ step
        for request in range(requests):
            owner = table_ref[base * requests + request] // 2
            out_ref[request * 2 * part_rows : (request + 1) * 2 * part_rows] = incoming_ref[
                owner, 0 : 2 * part_rows
            ]
        drawn = [
            pair_row(table_ref[base * requests + 2 * i], table_ref[base * requests + 2 * i + 1])
            for i in range(requests // 2)
        ]
        notes = jnp.concatenate(
            [row.astype(F32) for row in shared + own + drawn] + [pieces, blank], axis=0
        )
        out_ref[requests * 2 * part_rows :] = notes.astype(BF16)


def gather(place, table, weight, ids, incoming, bases, part_rows, block_total):
    rows = table.shape[0] // bases * 2 * part_rows + NOTE_ROWS
    return pl.pallas_call(
        functools.partial(gather_kernel, part_rows, block_total),
        out_shape=[jax.ShapeDtypeStruct((rows, HEAD_DIM), BF16)] * bases,
        in_specs=[SMEM, SMEM, SMEM, VMEM, VMEM],
        out_specs=[VMEM] * bases,
        cost_estimate=pl.CostEstimate(flops=0, bytes_accessed=1_000_000, transcendentals=0),
        name="gather",
    )(place, table, weight, ids, incoming)


def attention_kernel(
    samples,
    heads,
    part_rows,
    block_total,
    place_ref,
    table_ref,
    refs_ref,
    query_ref,
    key_ref,
    value_ref,
    cot_ref,
    glob_ref,
    below_ref,
    above_ref,
    *refs,
):
    rand_refs = refs[0:samples]
    (
        local_ref,
        glob_term_ref,
        low_rim_ref,
        high_rim_ref,
        rand_term_ref,
        raw_ref,
        term_ref,
        query_term_ref,
    ) = refs[samples:]
    inv_root = 1.0 / math.sqrt(HEAD_DIM)
    bank = refs_ref.shape[1]
    parts = samples
    slots = 2 * RAND
    seq_rank, base_rank, glob_block = place_ref[0], place_ref[1], place_ref[2]
    rank = lax.broadcasted_iota(jnp.int32, (bank, HEAD_DIM), 0).astype(F32)
    lane = lax.broadcasted_iota(jnp.int32, (BLOCK, HEAD_DIM), 1)
    note_start = rand_refs[0].shape[0] - NOTE_ROWS
    own_notes = 3
    drawn_notes = 4
    weight_note = drawn_notes + heads * RAND
    for head in range(heads):
        first_col = (base_rank * heads + head) * HEAD_DIM
        cols = columns(first_col)
        here = slice(head * HEAD_DIM, (head + 1) * HEAD_DIM)
        for kv in range(2):
            own = (key_ref, value_ref)[kv]
            to = slice(kv * HEAD_DIM, (kv + 1) * HEAD_DIM)
            unit = slice((head * 2 + kv) * BLOCK, (head * 2 + kv + 1) * BLOCK)
            raw_ref[0:64, to] = below_ref[unit]
            raw_ref[64:192, to] = own[:, cols]
            raw_ref[192:256, to] = above_ref[unit]
            raw_ref[256:320, to] = glob_ref[unit]
            raw_ref[320:384, to] = jnp.zeros((BLOCK, HEAD_DIM), BF16)
            for slot in range(slots):
                for step in range(parts):
                    start = NEAR + slot * BLOCK + (base_rank ^ step) * part_rows
                    source = ((head * slots + slot) * 2 + kv) * part_rows
                    raw_ref[pl.ds(pl.multiple_of(start, part_rows), part_rows), to] = rand_refs[
                        step
                    ][source : source + part_rows]

        def live_rows(index):
            here_block = seq_rank * 2 + index
            listed = [here_block - 1, here_block, here_block + 1, glob_block]
            for slot in range(RAND):
                listed.append(table_ref[((base_rank * heads + head) * 2 + index) * RAND + slot])
            alive = []
            for slot, block in enumerate(listed):
                flag = (block >= 0) & (block < block_total)
                for earlier in listed[:slot]:
                    flag = flag & (block != earlier)
                alive.append(jnp.where(flag, 1.0, 0.0))
            dead = jnp.float32(0.0)
            window = [dead] * index + alive[0:3] + [dead] * (1 - index)
            ordered = window + [alive[3], dead] + alive[4:]
            return jnp.concatenate(
                [
                    jnp.where(lane < BLOCK, ordered[2 * i], ordered[2 * i + 1])
                    for i in range(len(ordered) // 2)
                ],
                axis=1,
            )

        live = jnp.concatenate([live_rows(0), live_rows(1)], axis=0) > 0.5
        cot = cot_ref[:, cols]
        ref_q = refs_ref[0, :, cols]
        ref_kv = jnp.concatenate([refs_ref[1, :, cols], refs_ref[2, :, cols]], axis=1)
        query = query_ref[:, cols].astype(F32)
        for sample in range(samples):
            notes = rand_refs[sample][note_start:].astype(F32)
            drawn = drawn_notes + head * RAND

            def hot(row):
                return jnp.where(rank == notes[row : row + 1], 1.0, 0.0).astype(BF16)

            weight = (
                notes[weight_note : weight_note + 1, 0:1]
                + notes[weight_note : weight_note + 1, 1:2]
                + notes[weight_note : weight_note + 1, 2:3]
            )
            hot_keys = jnp.concatenate([hot(0), hot(1), hot(2), hot(drawn), hot(drawn + 1)], axis=1)
            base = matmul(hot_keys, ref_kv, ((0,), (0,)))
            diff = raw_ref[...].astype(F32) - base
            mix = (base + weight * diff).astype(BF16)
            base_q = matmul(hot(own_notes), ref_q, ((0,), (0,)))
            diff_q = query - base_q
            q_mix = (base_q + weight * diff_q).astype(BF16)
            k_mix = mix[:, 0:HEAD_DIM]
            v_mix = mix[:, HEAD_DIM:]

            def over_keys(rows, keys):
                return jnp.concatenate(
                    [
                        matmul(rows, keys[0:NEAR], ((1,), (1,))),
                        jnp.concatenate(
                            [
                                matmul(rows[0:64], keys[NEAR : NEAR + 128], ((1,), (1,))),
                                matmul(rows[64:128], keys[NEAR + 128 : NEAR + 256], ((1,), (1,))),
                            ],
                            axis=0,
                        ),
                    ],
                    axis=1,
                )

            def to_rows(weights, keys):
                return matmul(weights[:, 0:NEAR], keys[0:NEAR], ((1,), (0,))) + jnp.concatenate(
                    [
                        matmul(weights[0:64, NEAR:], keys[NEAR : NEAR + 128], ((1,), (0,))),
                        matmul(weights[64:128, NEAR:], keys[NEAR + 128 : NEAR + 256], ((1,), (0,))),
                    ],
                    axis=0,
                )

            def to_keys(weights, rows):
                return jnp.concatenate(
                    [
                        matmul(weights[:, 0:NEAR], rows, ((0,), (0,))),
                        matmul(weights[0:64, NEAR:], rows[0:64], ((0,), (0,))),
                        matmul(weights[64:128, NEAR:], rows[64:128], ((0,), (0,))),
                    ],
                    axis=0,
                )

            scores = jnp.where(live, over_keys(q_mix, k_mix) * inv_root, -1e30)
            peak = jnp.max(scores, axis=1, keepdims=True)
            exponent = jnp.where(live, jnp.exp(scores - peak), 0.0)
            probs = exponent / jnp.sum(exponent, axis=1, keepdims=True)
            probs_low = probs.astype(BF16)
            attended = to_rows(probs_low, v_mix)
            row_term = jnp.sum(cot.astype(F32) * attended, axis=1, keepdims=True)
            dscore = (probs * (over_keys(cot, v_mix) - row_term)).astype(BF16)
            query_term = diff_q * (to_rows(dscore, k_mix) * inv_root)
            term = diff[:, 0:HEAD_DIM] * (to_keys(dscore, q_mix) * inv_root) + diff[
                :, HEAD_DIM:
            ] * to_keys(probs_low, cot)
            if sample == 0:
                term_ref[...] = term
                query_term_ref[...] = query_term
            else:
                term_ref[...] += term
                query_term_ref[...] += query_term
        low_rim_ref[:, here] = term_ref[0:64].astype(BF16)
        high_rim_ref[:, here] = term_ref[192:256].astype(BF16)
        local_ref[:, here] = term_ref[64:192] + query_term_ref[...]
        glob_term_ref[head * BLOCK : (head + 1) * BLOCK] = term_ref[256:320].astype(BF16)
        for slot in range(slots):
            for part in range(parts):
                start = NEAR + slot * BLOCK + part * part_rows
                rand_term_ref[part, head * slots + slot] = term_ref[
                    start : start + part_rows
                ].astype(BF16)


def attention(
    place, table, refs, query, key, value, cot, glob, below, above, rand, part_rows, heads, block_total
):
    samples = len(rand)
    slots = heads * 2 * RAND
    feat = heads * HEAD_DIM
    return pl.pallas_call(
        functools.partial(attention_kernel, samples, heads, part_rows, block_total),
        out_shape=[
            jax.ShapeDtypeStruct((2 * BLOCK, feat), F32),
            jax.ShapeDtypeStruct((heads * BLOCK, HEAD_DIM), BF16),
            jax.ShapeDtypeStruct((BLOCK, feat), BF16),
            jax.ShapeDtypeStruct((BLOCK, feat), BF16),
            jax.ShapeDtypeStruct((samples, slots, part_rows, HEAD_DIM), BF16),
        ],
        in_specs=[SMEM, SMEM] + [VMEM] * (8 + samples),
        out_specs=[VMEM] * 5,
        scratch_shapes=[
            pltpu.VMEM((10 * BLOCK, 2 * HEAD_DIM), BF16),
            pltpu.VMEM((10 * BLOCK, HEAD_DIM), F32),
            pltpu.VMEM((2 * BLOCK, HEAD_DIM), F32),
        ],
        compiler_params=pltpu.CompilerParams(vmem_limit_bytes=32 * 1024 * 1024),
        cost_estimate=pl.CostEstimate(
            flops=900_000_000, bytes_accessed=2_000_000, transcendentals=600_000
        ),
        name="attention",
    )(place, table, refs, query, key, value, cot, glob, below, above, *rand)


def collect_kernel(heads, place_ref, pick_ref, arrived_ref, *refs):
    out_refs, sum_ref, total_ref = refs[0:-2], refs[-2], refs[-1]
    bases = len(out_refs)
    part_rows = total_ref.shape[1]
    head_count = heads * bases
    total_ref[...] = jnp.zeros_like(total_ref)
    glob = arrived_ref[0, part_rows:].astype(F32)
    for slot in range(pick_ref.shape[0]):
        unit = pick_ref[slot]
        total_ref[unit] += arrived_ref[slot, 0:part_rows].astype(F32)
        if slot:
            glob = glob + arrived_ref[slot, part_rows:].astype(F32)
    for copy in range(sum_ref.shape[0]):
        sum_ref[copy] = glob.astype(BF16)
    for step, out_ref in enumerate(out_refs):
        base = place_ref[1] ^ step
        for block in range(2):
            for head in range(heads):
                out_ref[block * heads + head] = total_ref[
                    1 + block * head_count + base * heads + head
                ].astype(BF16)


def collect(place, pick, arrived, bases, part_rows, heads, copies):
    rows = arrived.shape[1] - part_rows
    return pl.pallas_call(
        functools.partial(collect_kernel, heads),
        out_shape=[jax.ShapeDtypeStruct((2 * heads, part_rows, HEAD_DIM), BF16)] * bases
        + [jax.ShapeDtypeStruct((copies, rows, HEAD_DIM), BF16)],
        in_specs=[SMEM, SMEM, VMEM],
        out_specs=[VMEM] * (bases + 1),
        scratch_shapes=[pltpu.VMEM((1 + 2 * heads * bases, part_rows, HEAD_DIM), F32)],
        cost_estimate=pl.CostEstimate(flops=0, bytes_accessed=500_000, transcendentals=0),
        name="collect",
    )(place, pick, arrived)


def finish_kernel(heads, place_ref, local_ref, low_ref, high_ref, glob_ref, *refs):
    back_refs, out_ref, total_ref = refs[0:-2], refs[-2], refs[-1]
    bases = len(back_refs)
    part_rows = back_refs[0].shape[1]
    total_ref[0:BLOCK] = local_ref[0:BLOCK] + low_ref[...].astype(F32)
    total_ref[BLOCK:] = local_ref[BLOCK:] + high_ref[...].astype(F32)
    for head in range(heads):
        here = slice(head * HEAD_DIM, (head + 1) * HEAD_DIM)
        for step, back_ref in enumerate(back_refs):
            for block in range(2):
                start = block * BLOCK + (place_ref[1] ^ step) * part_rows
                rows = pl.ds(pl.multiple_of(start, part_rows), part_rows)
                total_ref[rows, here] += back_ref[block * heads + head].astype(F32)
        glob = glob_ref[head * BLOCK : (head + 1) * BLOCK].astype(F32)
        for block in range(2):
            rows = slice(block * BLOCK, (block + 1) * BLOCK)
            mine = place_ref[0] * 2 + block == place_ref[2]
            total_ref[rows, here] += jnp.where(mine, glob, 0.0)
    out_ref[...] = (total_ref[...] * (1.0 / bases)).astype(BF16)


def finish(place, local, low, high, glob, back, heads):
    return pl.pallas_call(
        functools.partial(finish_kernel, heads),
        out_shape=jax.ShapeDtypeStruct(local.shape, BF16),
        in_specs=[SMEM] + [VMEM] * (4 + len(back)),
        out_specs=VMEM,
        scratch_shapes=[pltpu.VMEM(local.shape, F32)],
        cost_estimate=pl.CostEstimate(flops=0, bytes_accessed=400_000, transcendentals=0),
        name="finish",
    )(place, local, low, high, glob, *back)


def exchange(array, axis, groups=None):
    return lax.all_to_all(array, axis, 0, 0, axis_index_groups=groups, tiled=True)


def swapped(arrays):
    return [arrays[0]] + [
        lax.ppermute(arrays[step], "base", [(i, i ^ step) for i in range(len(arrays))])
        for step in range(1, len(arrays))
    ]


def take(array, index):
    return array.at[index].get(mode="promise_in_bounds")


def per_device(
    queries,
    key_rows,
    values,
    cotangent,
    reference_set,
    sample_ids,
    mix_weight,
    global_block,
    random_blocks,
):
    seq_count = lax.axis_size("seq")
    seq_rank = lax.axis_index("seq")
    base_count = lax.axis_size("base")
    base_rank = lax.axis_index("base")
    tok_dev, feat_dev = queries.shape
    per_dev = tok_dev // BLOCK
    head_count = feat_dev // HEAD_DIM
    heads = head_count // base_count
    feat = heads * HEAD_DIM
    block_total = per_dev * seq_count
    requests = head_count * per_dev * RAND
    part_rows = BLOCK // base_count
    global_id = global_block[0]
    owner_glob = global_id // per_dev
    place = jnp.stack([seq_rank, base_rank, global_id]).astype(jnp.int32)

    table = random_blocks.reshape(head_count, seq_count, per_dev, RAND)
    unit = (table % per_dev) * head_count + jnp.arange(head_count)[:, None, None, None]
    wanted = table // per_dev == seq_rank
    pick = jnp.sum(jnp.where(wanted, unit + 1, 0), axis=(0, 2, 3))
    my_table = lax.dynamic_index_in_dim(table, seq_rank, 1, keepdims=False).reshape(requests)
    my_owner = my_table // per_dev

    outgoing, low, high = prepare(global_block, pick, key_rows, values, part_rows, heads)

    up = [(i, (i + 1) % seq_count) for i in range(seq_count)]
    down = [((i + 1) % seq_count, i) for i in range(seq_count)]
    below = lax.ppermute(high, "seq", up)
    above = lax.ppermute(low, "seq", down)

    incoming = exchange(outgoing, "seq")
    piece = lax.dynamic_index_in_dim(incoming, owner_glob, 0, keepdims=False)[2 * part_rows :]
    glob = exchange(jnp.broadcast_to(piece[None], (seq_count,) + piece.shape), "seq")
    glob = glob[0 : low.shape[0] // PIECE].reshape(low.shape)
    ids = sample_ids.reshape(-1, HEAD_DIM)
    rand = swapped(
        gather(place, my_table, mix_weight, ids, incoming, base_count, part_rows, block_total)
    )

    local, glob_term, low_rim, high_rim, rand_term = attention(
        place,
        my_table,
        reference_set,
        queries,
        key_rows,
        values,
        cotangent,
        glob,
        below,
        above,
        rand,
        part_rows,
        heads,
        block_total,
    )

    from_above = lax.ppermute(low_rim, "seq", down)
    from_below = lax.ppermute(high_rim, "seq", up)

    terms = exchange(rand_term.reshape(-1, part_rows, HEAD_DIM), "base")
    order = jnp.arange(1, requests + 1)
    sent = jnp.sum(
        jnp.where(my_owner[None, :] == jnp.arange(seq_count)[:, None], order[None, :], 0), axis=1
    )
    major = seq_count // SEQ_MINOR
    shares = jnp.repeat(glob_term.reshape(major, -1, HEAD_DIM), SEQ_MINOR, axis=0)
    returning = jnp.concatenate([take(terms, jnp.maximum(sent - 1, 0)), shares], axis=1)
    arrived = exchange(returning, "seq")
    arrived, from_below, from_above = lax.optimization_barrier((arrived, from_below, from_above))
    *back, share = collect(place, pick, arrived, base_count, part_rows, heads, major)
    back = swapped(back)
    lines = [[i * SEQ_MINOR + j for i in range(major)] for j in range(SEQ_MINOR)]
    glob_total = exchange(share, "seq", lines).reshape(glob_term.shape)
    return finish(place, local, from_below, from_above, glob_total, back, heads)


def solution(mesh):
    placed = (
        P("seq", "head"),
        P("seq", "head"),
        P("seq", "head"),
        P("seq", "head"),
        P(None, None, "head"),
        P("base", None),
        P("base"),
        P(),
        P("head", None, None),
    )
    return jax.shard_map(
        per_device,
        mesh=mesh,
        in_specs=placed,
        out_specs=P("seq", ("head", "base")),
        check_vma=False,
    )
```

time: 192 us -> 170 us (0.89)
  the two profiles are of different devices: /device:TPU:8 before, /device:TPU:32 now
where the time goes in v2:
time: 170 us; the launch traced here: 169 us
  starting transfers between devices  85.7 us (50%)
  waiting for transfers between devices  57.2 us (34%)
  Pallas kernels  17.8 us (10%)
  local copies, waits for them, and re-layouts  4.75 us (3%)
  other arithmetic  2.25 us (1%)
  between operations  1.78 us (1%)
    all_to_all x5, starting transfers between devices, exchange(): lax.all_to_all(array, axis, 0, 0, axis_index_groups=groups, tiled=True)  48.9 us
    all_to_all x5, waiting for transfers between devices, exchange(): lax.all_to_all(array, axis, 0, 0, axis_index_groups=groups, tiled=True)  47.1 us
    ppermute x6, starting transfers between devices, swapped(): lax.ppermute(arrays[step], 'base', [(i, i ^ step) for i in range(len(arra...  20.8 us
    pallas_call x1, Pallas kernels, attention(): pl.pallas_call(functools.partial(attention_kernel, samples, heads, part_r...  9.47 us
    ppermute x6, waiting for transfers between devices, swapped(): lax.ppermute(arrays[step], 'base', [(i, i ^ step) for i in range(len(arra...  5.19 us
    ppermute x1, waiting for transfers between devices, per_device(): from_below = lax.ppermute(high_rim, 'seq', up)  4.97 us
    ppermute x1, starting transfers between devices, per_device(): above = lax.ppermute(low, 'seq', down)  4.58 us
    ppermute x1, starting transfers between devices, per_device(): from_above = lax.ppermute(low_rim, 'seq', down)  4.58 us
  transfers between devices with their start and end apart: 15, of which 7 were waited for; matrix products, arithmetic and copies ran while one was open for 1% of the time, Pallas kernels for 1%

profile of v2, /device:TPU:32, one launch (start us, length us, event | category | flops | bytes accessed | tf_op | source)
XLA Modules:
  0.0 169.5 jit_solution(8811304832819438898)
XLA Ops:
  3.9 18.5 %all-to-all-start = ((bf16[64,40,128]{2,1,0:T(8,128)(2,1)}), bf16[64,40,128]{2,1,0:T(8,128)(2,1)S(1)}, u32[]{:S(2)}, u32[]{:S(2)}) async-start(bf16[64,40,128]{2,1,0:T(8,128)(2,1)} %get-tuple-element.25), calls=%async_computation | async-start | bytes 1310720 | tf_op jit(solution)/shard_map/all_to_all | solution.py:407
  22.4 3.4 %collective-permute-start = (bf16[256,128]{1,0:T(8,128)(2,1)S(1)}, bf16[256,128]{1,0:T(8,128)(2,1)S(1)}, u32[]{:S(2)}, u32[]{:S(2)}) collective-permute-start(bf16[256,128]{1,0:T(8,128)(2,1)S(1)} %copy-done.20), channel_id=1, source_target_pairs={{0,8},{8,16},{16,24},{24,32},{32,40},{40,48},{48,56},{56,64},{64,7... | collective-permute-start | bytes 196616 | tf_op jit(solution)/shard_map/ppermute | solution.py:459
  25.8 4.6 %collective-permute-start.1 = (bf16[256,128]{1,0:T(8,128)(2,1)S(1)}, bf16[256,128]{1,0:T(8,128)(2,1)S(1)}, u32[]{:S(2)}, u32[]{:S(2)}) collective-permute-start(bf16[256,128]{1,0:T(8,128)(2,1)S(1)} %copy-done.19), channel_id=1, source_target_pairs={{8,0},{16,8},{24,16},{32,24},{40,32},{48,40},{56,48},{64,56},{72,6... | collective-permute-start | bytes 196616 | tf_op jit(solution)/shard_map/ppermute | solution.py:460
  32.1 28.3 %all-to-all-done.incoming_ref = bf16[64,40,128]{2,1,0:T(8,128)(2,1)S(1)} async-done(((bf16[64,40,128]{2,1,0:T(8,128)(2,1)}), bf16[64,40,128]{2,1,0:T(8,128)(2,1)S(1)}, u32[]{:S(2)}, u32[]{:S(2)}) %all-to-all-start) | async-done | bytes 655392 | tf_op jit(solution)/shard_map/all_to_all | solution.py:407
  61.0 6.9 %all-to-all-start.1 = ((bf16[64,8,128]{2,1,0:T(8,128)(2,1)}), bf16[64,8,128]{2,1,0:T(8,128)(2,1)S(1)}, u32[]{:S(2)}, u32[]{:S(2)}) async-start(bf16[64,8,128]{2,1,0:T(8,128)(2,1)} %broadcast_in_dim.31), calls=%async_computation.1 | async-start | bytes 262144 | tf_op jit(solution)/shard_map/all_to_all | solution.py:407
  68.1 2.4 %gather.7 = (bf16[272,128]{1,0:T(8,128)(2,1)}, bf16[272,128]{1,0:T(8,128)(2,1)}, bf16[272,128]{1,0:T(8,128)(2,1)}, bf16[272,128]{1,0:T(8,128)(2,1)}) custom-call(s32[3]{0:T(128)} %pad_add_fusion.place_ref, s32[32]{0:T(128)} %copy-done.4, f32[1]{0:T(128)S(6)} %copy.15.weight_ref, s32[64,128]{1,0:T(8,128)} %bitcast.23, bf16[64,40,128]{2,1,0:T(8,128)(2,1)} %copy-done.10), custom_call_target="tpu_custom_call" | custom-call | bytes 1000000 | tf_op jit(solution)/shard_map/gather/pallas_call | solution.py:123
  70.4 3.4 %collective-permute-start.2 = (bf16[272,128]{1,0:T(8,128)(2,1)}, bf16[272,128]{1,0:T(8,128)(2,1)S(1)}, u32[]{:S(2)}, u32[]{:S(2)}) collective-permute-start(bf16[272,128]{1,0:T(8,128)(2,1)} %get-tuple-element.29), channel_id=1, source_target_pairs={{0,1},{1,0},{2,3},{3,2},{4,5},{5,4},{6,7},{7,6},{8,9},{9,8},{10,11... | collective-permute-start | bytes 208904 | tf_op jit(solution)/shard_map/ppermute | solution.py:412
  73.8 4.6 %collective-permute-start.3 = (bf16[272,128]{1,0:T(8,128)(2,1)}, bf16[272,128]{1,0:T(8,128)(2,1)S(1)}, u32[]{:S(2)}, u32[]{:S(2)}) collective-permute-start(bf16[272,128]{1,0:T(8,128)(2,1)} %get-tuple-element.30), channel_id=1, source_target_pairs={{0,2},{1,3},{2,0},{3,1},{4,6},{5,7},{6,4},{7,5},{8,10},{9,11},{10,... | collective-permute-start | bytes 208904 | tf_op jit(solution)/shard_map/ppermute | solution.py:412
  78.5 2.4 %collective-permute-start.4 = (bf16[272,128]{1,0:T(8,128)(2,1)}, bf16[272,128]{1,0:T(8,128)(2,1)S(1)}, u32[]{:S(2)}, u32[]{:S(2)}) collective-permute-start(bf16[272,128]{1,0:T(8,128)(2,1)} %get-tuple-element.31), channel_id=1, source_target_pairs={{0,3},{1,2},{2,1},{3,0},{4,7},{5,6},{6,5},{7,4},{8,11},{9,10},{10,... | collective-permute-start | bytes 208904 | tf_op jit(solution)/shard_map/ppermute | solution.py:412
  80.9 2.8 %all-to-all-done.1 = bf16[64,8,128]{2,1,0:T(8,128)(2,1)S(1)} async-done(((bf16[64,8,128]{2,1,0:T(8,128)(2,1)}), bf16[64,8,128]{2,1,0:T(8,128)(2,1)S(1)}, u32[]{:S(2)}, u32[]{:S(2)}) %all-to-all-start.1) | async-done | bytes 131104 | tf_op jit(solution)/shard_map/all_to_all | solution.py:407
  83.7 2.4 %collective-permute-done.4.refs_3_ = bf16[272,128]{1,0:T(8,128)(2,1)S(1)} collective-permute-done((bf16[272,128]{1,0:T(8,128)(2,1)}, bf16[272,128]{1,0:T(8,128)(2,1)S(1)}, u32[]{:S(2)}, u32[]{:S(2)}) %collective-permute-start.4) | collective-permute-done | bytes 69664 | tf_op jit(solution)/shard_map/ppermute | solution.py:412
  87.0 9.5 %attention.1 = (f32[128,256]{1,0:T(8,128)S(1)}, bf16[128,128]{1,0:T(8,128)(2,1)S(1)}, bf16[64,256]{1,0:T(8,128)(2,1)S(1)}, bf16[64,256]{1,0:T(8,128)(2,1)S(1)}, bf16[4,8,16,128]{3,2,1,0:T(8,128)(2,1)}) custom-call(s32[3]{0:T(128)S(1)} %copy-done.3, s32[32]{0:T(128)S(1)} %copy-done.5, bf16[3,64,1024]{2,1,0:T(8,128)(2,1)S(1)} %copy-done.6, ...), custom_call_target="tpu_custom_call" | custom-call | flops 900000000 | bytes 2000000 | tf_op jit(solution)/shard_map/attention/pallas_call | solution.py:312
  97.2 3.3 %all-to-all-start.2 = ((bf16[32,16,128]{2,1,0:T(8,128)(2,1)}), bf16[32,16,128]{2,1,0:T(8,128)(2,1)S(1)}, u32[]{:S(2)}, u32[]{:S(2)}) async-start(bf16[32,16,128]{2,1,0:T(8,128)(2,1)} %bitcast.7), calls=%async_computation.2 | async-start | bytes 262144 | tf_op jit(solution)/shard_map/all_to_all | solution.py:407
  100.5 5.9 %all-to-all-done.2 = bf16[32,16,128]{2,1,0:T(8,128)(2,1)S(1)} async-done(((bf16[32,16,128]{2,1,0:T(8,128)(2,1)}), bf16[32,16,128]{2,1,0:T(8,128)(2,1)S(1)}, u32[]{:S(2)}, u32[]{:S(2)}) %all-to-all-start.2) | async-done | bytes 131104 | tf_op jit(solution)/shard_map/all_to_all | solution.py:407
  107.9 15.1 %all-to-all-start.3 = ((bf16[64,24,128]{2,1,0:T(8,128)(2,1)}), bf16[64,24,128]{2,1,0:T(8,128)(2,1)S(1)}, u32[]{:S(2)}, u32[]{:S(2)}) async-start(bf16[64,24,128]{2,1,0:T(8,128)(2,1)} %pad_maximum_fusion), calls=%async_computation.3 | async-start | bytes 786432 | tf_op jit(solution)/shard_map/all_to_all | solution.py:407
  123.0 3.4 %collective-permute-start.5 = (bf16[64,256]{1,0:T(8,128)(2,1)S(1)}, bf16[64,256]{1,0:T(8,128)(2,1)S(1)}, u32[]{:S(2)}, u32[]{:S(2)}) collective-permute-start(bf16[64,256]{1,0:T(8,128)(2,1)S(1)} %get-tuple-element.35), channel_id=1, source_target_pairs={{0,8},{8,16},{16,24},{24,32},{32,40},{40,48},{48,56},{56,64},{64,7... | collective-permute-start | bytes 98312 | tf_op jit(solution)/shard_map/ppermute | solution.py:489
  126.4 4.6 %collective-permute-start.6 = (bf16[64,256]{1,0:T(8,128)(2,1)S(1)}, bf16[64,256]{1,0:T(8,128)(2,1)S(1)}, u32[]{:S(2)}, u32[]{:S(2)}) collective-permute-start(bf16[64,256]{1,0:T(8,128)(2,1)S(1)} %get-tuple-element.36), channel_id=1, source_target_pairs={{8,0},{16,8},{24,16},{32,24},{40,32},{48,40},{56,48},{64,56},{72,6... | collective-permute-start | bytes 98312 | tf_op jit(solution)/shard_map/ppermute | solution.py:488
  130.9 5.0 %collective-permute-done.5.low_ref = bf16[64,256]{1,0:T(8,128)(2,1)S(1)} collective-permute-done((bf16[64,256]{1,0:T(8,128)(2,1)S(1)}, bf16[64,256]{1,0:T(8,128)(2,1)S(1)}, u32[]{:S(2)}, u32[]{:S(2)}) %collective-permute-start.5) | collective-permute-done | bytes 32800 | tf_op jit(solution)/shard_map/ppermute | solution.py:489
  135.9 10.1 %all-to-all-done.3.arrived_ref = bf16[64,24,128]{2,1,0:T(8,128)(2,1)S(1)} async-done(((bf16[64,24,128]{2,1,0:T(8,128)(2,1)}), bf16[64,24,128]{2,1,0:T(8,128)(2,1)S(1)}, u32[]{:S(2)}, u32[]{:S(2)}) %all-to-all-start.3) | async-done | bytes 393248 | tf_op jit(solution)/shard_map/all_to_all | solution.py:407
  148.7 5.1 %all-to-all-start.4 = ((bf16[16,8,128]{2,1,0:T(8,128)(2,1)}), bf16[16,8,128]{2,1,0:T(8,128)(2,1)S(1)}, u32[]{:S(2)}, u32[]{:S(2)}) async-start(bf16[16,8,128]{2,1,0:T(8,128)(2,1)} %get-tuple-element.40), calls=%async_computation.4 | async-start | bytes 65536 | tf_op jit(solution)/shard_map/all_to_all | solution.py:407
  153.9 2.5 %collective-permute-start.7 = (bf16[4,16,128]{2,1,0:T(8,128)(2,1)S(1)}, bf16[4,16,128]{2,1,0:T(8,128)(2,1)S(1)}, u32[]{:S(2)}, u32[]{:S(2)}) collective-permute-start(bf16[4,16,128]{2,1,0:T(8,128)(2,1)S(1)} %copy-done.23), channel_id=1, source_target_pairs={{0,1},{1,0},{2,3},{3,2},{4,5},{5,4},{6,7},{7,6},{8,9},{9,8},{10,11... | collective-permute-start | bytes 49160 | tf_op jit(solution)/shard_map/ppermute | solution.py:412
  156.3 4.0 %collective-permute-start.8 = (bf16[4,16,128]{2,1,0:T(8,128)(2,1)S(1)}, bf16[4,16,128]{2,1,0:T(8,128)(2,1)S(1)}, u32[]{:S(2)}, u32[]{:S(2)}) collective-permute-start(bf16[4,16,128]{2,1,0:T(8,128)(2,1)S(1)} %copy-done.22), channel_id=1, source_target_pairs={{0,2},{1,3},{2,0},{3,1},{4,6},{5,7},{6,4},{7,5},{8,10},{9,11},{10,... | collective-permute-start | bytes 49160 | tf_op jit(solution)/shard_map/ppermute | solution.py:412
  160.3 4.0 %collective-permute-start.9 = (bf16[4,16,128]{2,1,0:T(8,128)(2,1)S(1)}, bf16[4,16,128]{2,1,0:T(8,128)(2,1)S(1)}, u32[]{:S(2)}, u32[]{:S(2)}) collective-permute-start(bf16[4,16,128]{2,1,0:T(8,128)(2,1)S(1)} %copy-done.21), channel_id=1, source_target_pairs={{0,3},{1,2},{2,1},{3,0},{4,7},{5,6},{6,5},{7,4},{8,11},{9,10},{10,... | collective-permute-start | bytes 49160 | tf_op jit(solution)/shard_map/ppermute | solution.py:412
  164.4 2.8 %collective-permute-done.9.refs_3_ = bf16[4,16,128]{2,1,0:T(8,128)(2,1)S(1)} collective-permute-done((bf16[4,16,128]{2,1,0:T(8,128)(2,1)S(1)}, bf16[4,16,128]{2,1,0:T(8,128)(2,1)S(1)}, u32[]{:S(2)}, u32[]{:S(2)}) %collective-permute-start.9) | collective-permute-done | bytes 16416 | tf_op jit(solution)/shard_map/ppermute | solution.py:412
  (78 shorter events, 13.0 us)
Async XLA Ops:
  3.9 18.5 %copy-start.20 = (bf16[256,128]{1,0:T(8,128)(2,1)S(1)}, bf16[256,128]{1,0:T(8,128)(2,1)}, u32[]{:S(2)}) copy-start(bf16[256,128]{1,0:T(8,128)(2,1)} %get-tuple-element.26) | copy-start | bytes 196612
  3.9 21.9 %copy-start.19 = (bf16[256,128]{1,0:T(8,128)(2,1)S(1)}, bf16[256,128]{1,0:T(8,128)(2,1)}, u32[]{:S(2)}) copy-start(bf16[256,128]{1,0:T(8,128)(2,1)} %get-tuple-element.27) | copy-start | bytes 196612
  3.9 56.5 %all-to-all-start = ((bf16[64,40,128]{2,1,0:T(8,128)(2,1)}), bf16[64,40,128]{2,1,0:T(8,128)(2,1)S(1)}, u32[]{:S(2)}, u32[]{:S(2)}) async-start(bf16[64,40,128]{2,1,0:T(8,128)(2,1)} %get-tuple-element.25), calls=%async_computation | async-start | bytes 1310720 | tf_op jit(solution)/shard_map/all_to_all | solution.py:407
  22.4 61.3 %collective-permute-start = (bf16[256,128]{1,0:T(8,128)(2,1)S(1)}, bf16[256,128]{1,0:T(8,128)(2,1)S(1)}, u32[]{:S(2)}, u32[]{:S(2)}) collective-permute-start(bf16[256,128]{1,0:T(8,128)(2,1)S(1)} %copy-done.20), channel_id=1, source_target_pairs={{0,8},{8,16},{16,24},{24,32},{32,40},{40,48},{48,56},{56,64},{64,7... | collective-permute-start | bytes 196616 | tf_op jit(solution)/shard_map/ppermute | solution.py:459
  25.8 57.9 %collective-permute-start.1 = (bf16[256,128]{1,0:T(8,128)(2,1)S(1)}, bf16[256,128]{1,0:T(8,128)(2,1)S(1)}, u32[]{:S(2)}, u32[]{:S(2)}) collective-permute-start(bf16[256,128]{1,0:T(8,128)(2,1)S(1)} %copy-done.19), channel_id=1, source_target_pairs={{8,0},{16,8},{24,16},{32,24},{40,32},{48,40},{56,48},{64,56},{72,6... | collective-permute-start | bytes 196616 | tf_op jit(solution)/shard_map/ppermute | solution.py:460
  30.4 55.7 %copy-start.8 = (bf16[128,1024]{1,0:T(8,128)(2,1)S(1)}, bf16[128,1024]{1,0:T(8,128)(2,1)}, u32[]{:S(2)}) copy-start(bf16[128,1024]{1,0:T(8,128)(2,1)} %cot_ref.1) | copy-start | bytes 786436
  30.8 37.1 %copy-start.4 = (s32[32]{0:T(128)}, s32[32]{0:T(128)S(1)}, u32[]{:S(2)}) copy-start(s32[32]{0:T(128)S(1)} %reshape.75.table_ref) | copy-start | bytes 388
  60.4 25.8 %copy-start.7 = (bf16[128,1024]{1,0:T(8,128)(2,1)S(1)}, bf16[128,1024]{1,0:T(8,128)(2,1)}, u32[]{:S(2)}) copy-start(bf16[128,1024]{1,0:T(8,128)(2,1)} %query_ref.1) | copy-start | bytes 786436
  61.0 25.1 %copy-start.6 = (bf16[3,64,1024]{2,1,0:T(8,128)(2,1)S(1)}, bf16[3,64,1024]{2,1,0:T(8,128)(2,1)}, u32[]{:S(2)}) copy-start(bf16[3,64,1024]{2,1,0:T(8,128)(2,1)} %refs_ref.1) | copy-start | bytes 1179652
  61.0 22.7 %all-to-all-start.1 = ((bf16[64,8,128]{2,1,0:T(8,128)(2,1)}), bf16[64,8,128]{2,1,0:T(8,128)(2,1)S(1)}, u32[]{:S(2)}, u32[]{:S(2)}) async-start(bf16[64,8,128]{2,1,0:T(8,128)(2,1)} %broadcast_in_dim.31), calls=%async_computation.1 | async-start | bytes 262144 | tf_op jit(solution)/shard_map/all_to_all | solution.py:407
  68.1 18.1 %copy-start = (bf16[128,1024]{1,0:T(8,128)(2,1)S(1)}, bf16[128,1024]{1,0:T(8,128)(2,1)}, u32[]{:S(2)}) copy-start(bf16[128,1024]{1,0:T(8,128)(2,1)} %key_ref.3) | copy-start | bytes 786436
  68.1 18.1 %copy-start.1 = (bf16[128,1024]{1,0:T(8,128)(2,1)S(1)}, bf16[128,1024]{1,0:T(8,128)(2,1)}, u32[]{:S(2)}) copy-start(bf16[128,1024]{1,0:T(8,128)(2,1)} %value_ref.3) | copy-start | bytes 786436
  70.4 13.3 %collective-permute-start.2 = (bf16[272,128]{1,0:T(8,128)(2,1)}, bf16[272,128]{1,0:T(8,128)(2,1)S(1)}, u32[]{:S(2)}, u32[]{:S(2)}) collective-permute-start(bf16[272,128]{1,0:T(8,128)(2,1)} %get-tuple-element.29), channel_id=1, source_target_pairs={{0,1},{1,0},{2,3},{3,2},{4,5},{5,4},{6,7},{7,6},{8,9},{9,8},{10,11... | collective-permute-start | bytes 208904 | tf_op jit(solution)/shard_map/ppermute | solution.py:412
  73.8 9.9 %collective-permute-start.3 = (bf16[272,128]{1,0:T(8,128)(2,1)}, bf16[272,128]{1,0:T(8,128)(2,1)S(1)}, u32[]{:S(2)}, u32[]{:S(2)}) collective-permute-start(bf16[272,128]{1,0:T(8,128)(2,1)} %get-tuple-element.30), channel_id=1, source_target_pairs={{0,2},{1,3},{2,0},{3,1},{4,6},{5,7},{6,4},{7,5},{8,10},{9,11},{10,... | collective-permute-start | bytes 208904 | tf_op jit(solution)/shard_map/ppermute | solution.py:412
  78.5 7.6 %collective-permute-start.4 = (bf16[272,128]{1,0:T(8,128)(2,1)}, bf16[272,128]{1,0:T(8,128)(2,1)S(1)}, u32[]{:S(2)}, u32[]{:S(2)}) collective-permute-start(bf16[272,128]{1,0:T(8,128)(2,1)} %get-tuple-element.31), channel_id=1, source_target_pairs={{0,3},{1,2},{2,1},{3,0},{4,7},{5,6},{6,5},{7,4},{8,11},{9,10},{10,... | collective-permute-start | bytes 208904 | tf_op jit(solution)/shard_map/ppermute | solution.py:412
  97.2 9.3 %all-to-all-start.2 = ((bf16[32,16,128]{2,1,0:T(8,128)(2,1)}), bf16[32,16,128]{2,1,0:T(8,128)(2,1)S(1)}, u32[]{:S(2)}, u32[]{:S(2)}) async-start(bf16[32,16,128]{2,1,0:T(8,128)(2,1)} %bitcast.7), calls=%async_computation.2 | async-start | bytes 262144 | tf_op jit(solution)/shard_map/all_to_all | solution.py:407
  107.9 38.1 %all-to-all-start.3 = ((bf16[64,24,128]{2,1,0:T(8,128)(2,1)}), bf16[64,24,128]{2,1,0:T(8,128)(2,1)S(1)}, u32[]{:S(2)}, u32[]{:S(2)}) async-start(bf16[64,24,128]{2,1,0:T(8,128)(2,1)} %pad_maximum_fusion), calls=%async_computation.3 | async-start | bytes 786432 | tf_op jit(solution)/shard_map/all_to_all | solution.py:407
  123.0 12.9 %collective-permute-start.5 = (bf16[64,256]{1,0:T(8,128)(2,1)S(1)}, bf16[64,256]{1,0:T(8,128)(2,1)S(1)}, u32[]{:S(2)}, u32[]{:S(2)}) collective-permute-start(bf16[64,256]{1,0:T(8,128)(2,1)S(1)} %get-tuple-element.35), channel_id=1, source_target_pairs={{0,8},{8,16},{16,24},{24,32},{32,40},{40,48},{48,56},{56,64},{64,7... | collective-permute-start | bytes 98312 | tf_op jit(solution)/shard_map/ppermute | solution.py:489
  126.4 9.6 %collective-permute-start.6 = (bf16[64,256]{1,0:T(8,128)(2,1)S(1)}, bf16[64,256]{1,0:T(8,128)(2,1)S(1)}, u32[]{:S(2)}, u32[]{:S(2)}) collective-permute-start(bf16[64,256]{1,0:T(8,128)(2,1)S(1)} %get-tuple-element.36), channel_id=1, source_target_pairs={{8,0},{16,8},{24,16},{32,24},{40,32},{48,40},{56,48},{64,56},{72,6... | collective-permute-start | bytes 98312 | tf_op jit(solution)/shard_map/ppermute | solution.py:488
  135.9 12.8 %copy-start.14 = (bf16[64,256]{1,0:T(8,128)(2,1)}, bf16[64,256]{1,0:T(8,128)(2,1)S(1)}, u32[]{:S(2)}) copy-start(bf16[64,256]{1,0:T(8,128)(2,1)S(1)} %collective-permute-done.5.low_ref) | copy-start | bytes 98308
  148.7 18.4 %all-to-all-start.4 = ((bf16[16,8,128]{2,1,0:T(8,128)(2,1)}), bf16[16,8,128]{2,1,0:T(8,128)(2,1)S(1)}, u32[]{:S(2)}, u32[]{:S(2)}) async-start(bf16[16,8,128]{2,1,0:T(8,128)(2,1)} %get-tuple-element.40), calls=%async_computation.4 | async-start | bytes 65536 | tf_op jit(solution)/shard_map/all_to_all | solution.py:407
  153.9 10.5 %collective-permute-start.7 = (bf16[4,16,128]{2,1,0:T(8,128)(2,1)S(1)}, bf16[4,16,128]{2,1,0:T(8,128)(2,1)S(1)}, u32[]{:S(2)}, u32[]{:S(2)}) collective-permute-start(bf16[4,16,128]{2,1,0:T(8,128)(2,1)S(1)} %copy-done.23), channel_id=1, source_target_pairs={{0,1},{1,0},{2,3},{3,2},{4,5},{5,4},{6,7},{7,6},{8,9},{9,8},{10,11... | collective-permute-start | bytes 49160 | tf_op jit(solution)/shard_map/ppermute | solution.py:412
  156.3 8.0 %collective-permute-start.8 = (bf16[4,16,128]{2,1,0:T(8,128)(2,1)S(1)}, bf16[4,16,128]{2,1,0:T(8,128)(2,1)S(1)}, u32[]{:S(2)}, u32[]{:S(2)}) collective-permute-start(bf16[4,16,128]{2,1,0:T(8,128)(2,1)S(1)} %copy-done.22), channel_id=1, source_target_pairs={{0,2},{1,3},{2,0},{3,1},{4,6},{5,7},{6,4},{7,5},{8,10},{9,11},{10,... | collective-permute-start | bytes 49160 | tf_op jit(solution)/shard_map/ppermute | solution.py:412
  160.3 6.8 %collective-permute-start.9 = (bf16[4,16,128]{2,1,0:T(8,128)(2,1)S(1)}, bf16[4,16,128]{2,1,0:T(8,128)(2,1)S(1)}, u32[]{:S(2)}, u32[]{:S(2)}) collective-permute-start(bf16[4,16,128]{2,1,0:T(8,128)(2,1)S(1)} %copy-done.21), channel_id=1, source_target_pairs={{0,3},{1,2},{2,1},{3,0},{4,7},{5,6},{6,5},{7,4},{8,11},{9,10},{10,... | collective-permute-start | bytes 49160 | tf_op jit(solution)/shard_map/ppermute | solution.py:412
  (15 other events, 59.6 us)

commit v3 on v2

--- a/solution.py
+++ b/solution.py
@@ -11,7 +11,7 @@
 HEAD_DIM = 128
 BLOCK = 64
 RAND = 2
-SEQ_MINOR = 4
+SHARES = 16
 PIECE = 8
 NOTE_ROWS = 16
 NEAR = 6 * BLOCK
@@ -35,7 +35,8 @@
     base_rank = lax.axis_index("base")
     head_count = key_ref.shape[1] // HEAD_DIM
     glob_start = pl.multiple_of((glob_ref[0] % 2) * BLOCK, BLOCK)
-    for slot in range(pick_ref.shape[0]):
+
+    def one_slot(slot, carry):
         unit = jnp.maximum(pick_ref[slot] - 1, 0)
         rows = pl.ds(
             pl.multiple_of((unit // head_count) * BLOCK + base_rank * part_rows, part_rows),
@@ -44,6 +45,9 @@
         cols = columns((unit % head_count) * HEAD_DIM)
         outgoing_ref[slot, 0:part_rows] = key_ref[rows, cols]
         outgoing_ref[slot, part_rows : 2 * part_rows] = value_ref[rows, cols]
+        return carry
+
+    lax.fori_loop(0, pick_ref.shape[0], one_slot, 0, unroll=8)
     pieces = heads * 2 * BLOCK // PIECE
     for head in range(heads):
         cols = columns((base_rank * heads + head) * HEAD_DIM)
@@ -157,6 +161,8 @@
         raw_ref,
         term_ref,
         query_term_ref,
+        notes_ref,
+        bias_ref,
     ) = refs[samples:]
     inv_root = 1.0 / math.sqrt(HEAD_DIM)
     bank = refs_ref.shape[1]
@@ -166,140 +172,132 @@
     rank = lax.broadcasted_iota(jnp.int32, (bank, HEAD_DIM), 0).astype(F32)
     lane = lax.broadcasted_iota(jnp.int32, (BLOCK, HEAD_DIM), 1)
     note_start = rand_refs[0].shape[0] - NOTE_ROWS
+    for step in range(samples):
+        notes_ref[step] = rand_refs[step][note_start:].astype(F32)
     own_notes = 3
     drawn_notes = 4
     weight_note = drawn_notes + heads * RAND
+
+    def live_blocks(head, index):
+        here_block = seq_rank * 2 + index
+        listed = [here_block - 1, here_block, here_block + 1, glob_block]
+        for slot in range(RAND):
+            listed.append(table_ref[((base_rank * heads + head) * 2 + index) * RAND + slot])
+        alive = []
+        for slot, block in enumerate(listed):
+            flag = (block >= 0) & (block < block_total)
+            for earlier in listed[:slot]:
+                flag = flag & (block != earlier)
+            alive.append(jnp.where(flag, 0.0, -1e30))
+        dead = jnp.float32(-1e30)
+        window = [dead] * index + alive[0:3] + [dead] * (1 - index)
+        drawn = [dead] * (index * RAND) + alive[4:] + [dead] * ((1 - index) * RAND)
+        return window + [alive[3], dead] + drawn
+
+    cots, queries = [], []
     for head in range(heads):
-        first_col = (base_rank * heads + head) * HEAD_DIM
-        cols = columns(first_col)
-        here = slice(head * HEAD_DIM, (head + 1) * HEAD_DIM)
+        cols = columns((base_rank * heads + head) * HEAD_DIM)
         for kv in range(2):
             own = (key_ref, value_ref)[kv]
             to = slice(kv * HEAD_DIM, (kv + 1) * HEAD_DIM)
             unit = slice((head * 2 + kv) * BLOCK, (head * 2 + kv + 1) * BLOCK)
-            raw_ref[0:64, to] = below_ref[unit]
-            raw_ref[64:192, to] = own[:, cols]
-            raw_ref[192:256, to] = above_ref[unit]
-            raw_ref[256:320, to] = glob_ref[unit]
-            raw_ref[320:384, to] = jnp.zeros((BLOCK, HEAD_DIM), BF16)
+            raw_ref[head, 0:64, to] = below_ref[unit]
+            raw_ref[head, 64:192, to] = own[:, cols]
+            raw_ref[head, 192:256, to] = above_ref[unit]
+            raw_ref[head, 256:320, to] = glob_ref[unit]
+            raw_ref[head, 320:384, to] = jnp.zeros((BLOCK, HEAD_DIM), BF16)
+        for block, (left, right) in enumerate(zip(live_blocks(head, 0), live_blocks(head, 1))):
+            bias_ref[head, block * BLOCK : (block + 1) * BLOCK] = jnp.where(
+                lane < BLOCK, left, right
+            )
+        cots.append(cot_ref[:, cols])
+        queries.append(query_ref[:, cols].astype(F32))
+    wide = pl.ds(pl.multiple_of(base_rank * heads * HEAD_DIM, heads * HEAD_DIM), heads * HEAD_DIM)
+    ref_q = refs_ref[0, :, wide]
+    ref_kvs = [
+        jnp.concatenate(
+            [
+                refs_ref[1, :, columns((base_rank * heads + head) * HEAD_DIM)],
+                refs_ref[2, :, columns((base_rank * heads + head) * HEAD_DIM)],
+            ],
+            axis=1,
+        )
+        for head in range(heads)
+    ]
+    ref_all = jnp.concatenate(ref_kvs, axis=1)
+    for head in range(heads):
+        for kv in range(2):
+            to = slice(kv * HEAD_DIM, (kv + 1) * HEAD_DIM)
             for slot in range(slots):
                 for step in range(parts):
                     start = NEAR + slot * BLOCK + (base_rank ^ step) * part_rows
                     source = ((head * slots + slot) * 2 + kv) * part_rows
-                    raw_ref[pl.ds(pl.multiple_of(start, part_rows), part_rows), to] = rand_refs[
-                        step
-                    ][source : source + part_rows]
-
-        def live_rows(index):
-            here_block = seq_rank * 2 + index
-            listed = [here_block - 1, here_block, here_block + 1, glob_block]
-            for slot in range(RAND):
-                listed.append(table_ref[((base_rank * heads + head) * 2 + index) * RAND + slot])
-            alive = []
-            for slot, block in enumerate(listed):
-                flag = (block >= 0) & (block < block_total)
-                for earlier in listed[:slot]:
-                    flag = flag & (block != earlier)
-                alive.append(jnp.where(flag, 1.0, 0.0))
-            dead = jnp.float32(0.0)
-            window = [dead] * index + alive[0:3] + [dead] * (1 - index)
-            ordered = window + [alive[3], dead] + alive[4:]
-            return jnp.concatenate(
+                    raw_ref[head, pl.ds(pl.multiple_of(start, part_rows), part_rows), to] = (
+                        rand_refs[step][source : source + part_rows]
+                    )
+
+    term_ref[...] = jnp.zeros_like(term_ref)
+    query_term_ref[...] = jnp.zeros_like(query_term_ref)
+
+    def one_sample(sample, carry):
+        notes = notes_ref[sample]
+
+        def hot(row):
+            return jnp.where(rank == notes[row : row + 1], 1.0, 0.0).astype(BF16)
+
+        weight = (
+            notes[weight_note : weight_note + 1, 0:1]
+            + notes[weight_note : weight_note + 1, 1:2]
+            + notes[weight_note : weight_note + 1, 2:3]
+        )
+        hot_near = jnp.concatenate([hot(0), hot(1), hot(2)], axis=1)
+        base_near = matmul(hot_near, ref_all, ((0,), (0,)))
+        base_rows = matmul(hot(own_notes), ref_q, ((0,), (0,)))
+        for head in range(heads):
+            here = slice(head * HEAD_DIM, (head + 1) * HEAD_DIM)
+            drawn = drawn_notes + head * RAND
+            hot_far = jnp.concatenate([hot(drawn), hot(drawn + 1)], axis=1)
+            base = jnp.concatenate(
                 [
-                    jnp.where(lane < BLOCK, ordered[2 * i], ordered[2 * i + 1])
-                    for i in range(len(ordered) // 2)
+                    base_near[:, head * 2 * HEAD_DIM : (head + 1) * 2 * HEAD_DIM],
+                    matmul(hot_far, ref_kvs[head], ((0,), (0,))),
                 ],
-                axis=1,
+                axis=0,
             )
-
-        live = jnp.concatenate([live_rows(0), live_rows(1)], axis=0) > 0.5
-        cot = cot_ref[:, cols]
-        ref_q = refs_ref[0, :, cols]
-        ref_kv = jnp.concatenate([refs_ref[1, :, cols], refs_ref[2, :, cols]], axis=1)
-        query = query_ref[:, cols].astype(F32)
-        for sample in range(samples):
-            notes = rand_refs[sample][note_start:].astype(F32)
-            drawn = drawn_notes + head * RAND
-
-            def hot(row):
-                return jnp.where(rank == notes[row : row + 1], 1.0, 0.0).astype(BF16)
-
-            weight = (
-                notes[weight_note : weight_note + 1, 0:1]
-                + notes[weight_note : weight_note + 1, 1:2]
-                + notes[weight_note : weight_note + 1, 2:3]
-            )
-            hot_keys = jnp.concatenate([hot(0), hot(1), hot(2), hot(drawn), hot(drawn + 1)], axis=1)
-            base = matmul(hot_keys, ref_kv, ((0,), (0,)))
-            diff = raw_ref[...].astype(F32) - base
+            diff = raw_ref[head].astype(F32) - base
             mix = (base + weight * diff).astype(BF16)
-            base_q = matmul(hot(own_notes), ref_q, ((0,), (0,)))
-            diff_q = query - base_q
+            k_mix, v_mix = mix[:, 0:HEAD_DIM], mix[:, HEAD_DIM:]
+            base_q = base_rows[:, here]
+            diff_q = queries[head] - base_q
             q_mix = (base_q + weight * diff_q).astype(BF16)
-            k_mix = mix[:, 0:HEAD_DIM]
-            v_mix = mix[:, HEAD_DIM:]
-
-            def over_keys(rows, keys):
-                return jnp.concatenate(
-                    [
-                        matmul(rows, keys[0:NEAR], ((1,), (1,))),
-                        jnp.concatenate(
-                            [
-                                matmul(rows[0:64], keys[NEAR : NEAR + 128], ((1,), (1,))),
-                                matmul(rows[64:128], keys[NEAR + 128 : NEAR + 256], ((1,), (1,))),
-                            ],
-                            axis=0,
-                        ),
-                    ],
-                    axis=1,
-                )
-
-            def to_rows(weights, keys):
-                return matmul(weights[:, 0:NEAR], keys[0:NEAR], ((1,), (0,))) + jnp.concatenate(
-                    [
-                        matmul(weights[0:64, NEAR:], keys[NEAR : NEAR + 128], ((1,), (0,))),
-                        matmul(weights[64:128, NEAR:], keys[NEAR + 128 : NEAR + 256], ((1,), (0,))),
-                    ],
-                    axis=0,
-                )
-
-            def to_keys(weights, rows):
-                return jnp.concatenate(
-                    [
-                        matmul(weights[:, 0:NEAR], rows, ((0,), (0,))),
-                        matmul(weights[0:64, NEAR:], rows[0:64], ((0,), (0,))),
-                        matmul(weights[64:128, NEAR:], rows[64:128], ((0,), (0,))),
-                    ],
-                    axis=0,
-                )
-
-            scores = jnp.where(live, over_keys(q_mix, k_mix) * inv_root, -1e30)
-            peak = jnp.max(scores, axis=1, keepdims=True)
-            exponent = jnp.where(live, jnp.exp(scores - peak), 0.0)
-            probs = exponent / jnp.sum(exponent, axis=1, keepdims=True)
+            cot = cots[head]
+            scores = matmul(k_mix, q_mix, ((1,), (1,))) * inv_root + bias_ref[head]
+            exponent = jnp.exp(scores - jnp.max(scores, axis=0, keepdims=True))
+            probs = exponent * (1.0 / jnp.sum(exponent, axis=0, keepdims=True))
             probs_low = probs.astype(BF16)
-            attended = to_rows(probs_low, v_mix)
-            row_term = jnp.sum(cot.astype(F32) * attended, axis=1, keepdims=True)
-            dscore = (probs * (over_keys(cot, v_mix) - row_term)).astype(BF16)
-            query_term = diff_q * (to_rows(dscore, k_mix) * inv_root)
-            term = diff[:, 0:HEAD_DIM] * (to_keys(dscore, q_mix) * inv_root) + diff[
-                :, HEAD_DIM:
-            ] * to_keys(probs_low, cot)
-            if sample == 0:
-                term_ref[...] = term
-                query_term_ref[...] = query_term
-            else:
-                term_ref[...] += term
-                query_term_ref[...] += query_term
-        low_rim_ref[:, here] = term_ref[0:64].astype(BF16)
-        high_rim_ref[:, here] = term_ref[192:256].astype(BF16)
-        local_ref[:, here] = term_ref[64:192] + query_term_ref[...]
-        glob_term_ref[head * BLOCK : (head + 1) * BLOCK] = term_ref[256:320].astype(BF16)
+            dprobs = matmul(v_mix, cot, ((1,), (1,)))
+            row_term = jnp.sum(probs_low.astype(F32) * dprobs, axis=0, keepdims=True)
+            dscore = (probs * (dprobs - row_term)).astype(BF16)
+            query_term_ref[head] += diff_q * (matmul(dscore, k_mix, ((0,), (0,))) * inv_root)
+            grad_k = matmul(dscore, q_mix, ((1,), (0,)))
+            grad_v = matmul(probs_low, cot, ((1,), (0,)))
+            term_ref[head] += diff[:, 0:HEAD_DIM] * (grad_k * inv_root) + diff[:, HEAD_DIM:] * grad_v
+        return carry
+
+    lax.fori_loop(0, samples, one_sample, 0)
+    for head in range(heads):
+        here = slice(head * HEAD_DIM, (head + 1) * HEAD_DIM)
+        local_ref[:, here] = term_ref[head, 64:192] + query_term_ref[head]
+    for head in range(heads):
+        here = slice(head * HEAD_DIM, (head + 1) * HEAD_DIM)
+        low_rim_ref[:, here] = term_ref[head, 0:64].astype(BF16)
+        high_rim_ref[:, here] = term_ref[head, 192:256].astype(BF16)
+        glob_term_ref[head * BLOCK : (head + 1) * BLOCK] = term_ref[head, 256:320].astype(BF16)
         for slot in range(slots):
             for part in range(parts):
                 start = NEAR + slot * BLOCK + part * part_rows
                 rand_term_ref[part, head * slots + slot] = term_ref[
-                    start : start + part_rows
+                    head, start : start + part_rows
                 ].astype(BF16)
 
 
@@ -321,9 +319,11 @@
         in_specs=[SMEM, SMEM] + [VMEM] * (8 + samples),
         out_specs=[VMEM] * 5,
         scratch_shapes=[
-            pltpu.VMEM((10 * BLOCK, 2 * HEAD_DIM), BF16),
-            pltpu.VMEM((10 * BLOCK, HEAD_DIM), F32),
-            pltpu.VMEM((2 * BLOCK, HEAD_DIM), F32),
+            pltpu.VMEM((heads, 10 * BLOCK, 2 * HEAD_DIM), BF16),
+            pltpu.VMEM((heads, 10 * BLOCK, HEAD_DIM), F32),
+            pltpu.VMEM((heads, 2 * BLOCK, HEAD_DIM), F32),
+            pltpu.VMEM((samples, NOTE_ROWS, HEAD_DIM), F32),
+            pltpu.VMEM((heads, 10 * BLOCK, HEAD_DIM), F32),
         ],
         compiler_params=pltpu.CompilerParams(vmem_limit_bytes=32 * 1024 * 1024),
         cost_estimate=pl.CostEstimate(
@@ -339,12 +339,16 @@
     part_rows = total_ref.shape[1]
     head_count = heads * bases
     total_ref[...] = jnp.zeros_like(total_ref)
-    glob = arrived_ref[0, part_rows:].astype(F32)
-    for slot in range(pick_ref.shape[0]):
+
+    def one_slot(slot, glob):
         unit = pick_ref[slot]
         total_ref[unit] += arrived_ref[slot, 0:part_rows].astype(F32)
-        if slot:
-            glob = glob + arrived_ref[slot, part_rows:].astype(F32)
+        return glob + arrived_ref[slot, part_rows:].astype(F32)
+
+    rows = arrived_ref.shape[1] - part_rows
+    glob = lax.fori_loop(
+        0, pick_ref.shape[0], one_slot, jnp.zeros((rows, HEAD_DIM), F32), unroll=8
+    )
     for copy in range(sum_ref.shape[0]):
         sum_ref[copy] = glob.astype(BF16)
     for step, out_ref in enumerate(out_refs):
@@ -412,6 +416,10 @@
         lax.ppermute(arrays[step], "base", [(i, i ^ step) for i in range(len(arrays))])
         for step in range(1, len(arrays))
     ]
+
+
+def runs(count, size):
+    return [list(range(i, i + size)) for i in range(0, count, size)]
 
 
 def take(array, index):
@@ -461,8 +469,10 @@
 
     incoming = exchange(outgoing, "seq")
     piece = lax.dynamic_index_in_dim(incoming, owner_glob, 0, keepdims=False)[2 * part_rows :]
-    glob = exchange(jnp.broadcast_to(piece[None], (seq_count,) + piece.shape), "seq")
-    glob = glob[0 : low.shape[0] // PIECE].reshape(low.shape)
+    ways = low.shape[0] // PIECE
+    glob = exchange(
+        jnp.broadcast_to(piece[None], (ways,) + piece.shape), "seq", runs(seq_count, ways)
+    ).reshape(low.shape)
     ids = sample_ids.reshape(-1, HEAD_DIM)
     rand = swapped(
         gather(place, my_table, mix_weight, ids, incoming, base_count, part_rows, block_total)
@@ -493,15 +503,15 @@
     sent = jnp.sum(
         jnp.where(my_owner[None, :] == jnp.arange(seq_count)[:, None], order[None, :], 0), axis=1
     )
-    major = seq_count // SEQ_MINOR
-    shares = jnp.repeat(glob_term.reshape(major, -1, HEAD_DIM), SEQ_MINOR, axis=0)
+    shares = jnp.tile(
+        glob_term.reshape(SHARES, -1, HEAD_DIM), (seq_count // SHARES, 1, 1)
+    )
     returning = jnp.concatenate([take(terms, jnp.maximum(sent - 1, 0)), shares], axis=1)
     arrived = exchange(returning, "seq")
     arrived, from_below, from_above = lax.optimization_barrier((arrived, from_below, from_above))
-    *back, share = collect(place, pick, arrived, base_count, part_rows, heads, major)
+    *back, share = collect(place, pick, arrived, base_count, part_rows, heads, SHARES)
     back = swapped(back)
-    lines = [[i * SEQ_MINOR + j for i in range(major)] for j in range(SEQ_MINOR)]
-    glob_total = exchange(share, "seq", lines).reshape(glob_term.shape)
+    glob_total = exchange(share, "seq", runs(seq_count, SHARES)).reshape(glob_term.shape)
     return finish(place, local, from_below, from_above, glob_total, back, heads)
 
 

time: 170 us -> 169 us (level)
  the two profiles are of different devices: /device:TPU:32 before, /device:TPU:8 now
where the time goes in v3:
time: 169 us; the launch traced here: 168 us
  starting transfers between devices  78.2 us (46%)
  waiting for transfers between devices  63 us (37%)
  Pallas kernels  17.2 us (10%)
  local copies, waits for them, and re-layouts  5.85 us (3%)
  other arithmetic  2.24 us (1%)
  between operations  1.75 us (1%)
    all_to_all x5, waiting for transfers between devices, exchange(): lax.all_to_all(array, axis, 0, 0, axis_index_groups=groups, tiled=True)  51.6 us
    all_to_all x5, starting transfers between devices, exchange(): lax.all_to_all(array, axis, 0, 0, axis_index_groups=groups, tiled=True)  45.6 us
    ppermute x6, starting transfers between devices, swapped(): lax.ppermute(arrays[step], 'base', [(i, i ^ step) for i in range(len(arra...  20.8 us
    pallas_call x1, Pallas kernels, attention(): pl.pallas_call(functools.partial(attention_kernel, samples, heads, part_r...  8.78 us
    ppermute x6, waiting for transfers between devices, swapped(): lax.ppermute(arrays[step], 'base', [(i, i ^ step) for i in range(len(arra...  8.01 us
    unnamed x49, local copies, waits for them, and re-layouts  4.18 us
  transfers between devices with their start and end apart: 15, of which 7 were waited for; matrix products, arithmetic and copies ran while one was open for 1% of the time, Pallas kernels for 1%

profile of v3, /device:TPU:8, one launch (start us, length us, event | category | flops | bytes accessed | tf_op | source)
XLA Modules:
  0.0 168.1 jit_solution(13144636383651286072)
XLA Ops:
  1.6 2.4 %prepare.1 = (bf16[64,40,128]{2,1,0:T(8,128)(2,1)}, bf16[256,128]{1,0:T(8,128)(2,1)}, bf16[256,128]{1,0:T(8,128)(2,1)}) custom-call(s32[1]{0:T(128)} %copy.16.glob_ref, s32[64]{0:T(128)} %reduce_sum.27.pick_ref, bf16[128,1024]{1,0:T(8,128)(2,1)} %key_ref.3, bf16[128,1024]{1,0:T(8,128)(2,1)} %value_ref.3), custom_call_target="tpu_custom_call" | custom-call | bytes 1400000 | tf_op jit(solution)/shard_map/prepare/pallas_call | solution.py:69
  4.0 18.9 %all-to-all-start = ((bf16[64,40,128]{2,1,0:T(8,128)(2,1)}), bf16[64,40,128]{2,1,0:T(8,128)(2,1)S(1)}, u32[]{:S(2)}, u32[]{:S(2)}) async-start(bf16[64,40,128]{2,1,0:T(8,128)(2,1)} %get-tuple-element.25), calls=%async_computation | async-start | bytes 1310720 | tf_op jit(solution)/shard_map/all_to_all | solution.py:411
  22.9 3.4 %collective-permute-start = (bf16[256,128]{1,0:T(8,128)(2,1)S(1)}, bf16[256,128]{1,0:T(8,128)(2,1)S(1)}, u32[]{:S(2)}, u32[]{:S(2)}) collective-permute-start(bf16[256,128]{1,0:T(8,128)(2,1)S(1)} %copy-done.20), channel_id=1, source_target_pairs={{0,8},{8,16},{16,24},{24,32},{32,40},{40,48},{48,56},{56,64},{64,7... | collective-permute-start | bytes 196616 | tf_op jit(solution)/shard_map/ppermute | solution.py:467
  26.3 2.5 %collective-permute-start.1 = (bf16[256,128]{1,0:T(8,128)(2,1)S(1)}, bf16[256,128]{1,0:T(8,128)(2,1)S(1)}, u32[]{:S(2)}, u32[]{:S(2)}) collective-permute-start(bf16[256,128]{1,0:T(8,128)(2,1)S(1)} %copy-done.19), channel_id=1, source_target_pairs={{8,0},{16,8},{24,16},{32,24},{40,32},{48,40},{56,48},{64,56},{72,6... | collective-permute-start | bytes 196616 | tf_op jit(solution)/shard_map/ppermute | solution.py:468
  29.8 31.4 %all-to-all-done.incoming_ref = bf16[64,40,128]{2,1,0:T(8,128)(2,1)S(1)} async-done(((bf16[64,40,128]{2,1,0:T(8,128)(2,1)}), bf16[64,40,128]{2,1,0:T(8,128)(2,1)S(1)}, u32[]{:S(2)}, u32[]{:S(2)}) %all-to-all-start) | async-done | bytes 655392 | tf_op jit(solution)/shard_map/all_to_all | solution.py:411
  61.9 5.3 %all-to-all-start.1 = ((bf16[32,8,128]{2,1,0:T(8,128)(2,1)}), bf16[32,8,128]{2,1,0:T(8,128)(2,1)S(1)}, u32[]{:S(2)}, u32[]{:S(2)}) async-start(bf16[32,8,128]{2,1,0:T(8,128)(2,1)} %broadcast_in_dim.28), calls=%async_computation.1 | async-start | bytes 131072 | tf_op jit(solution)/shard_map/all_to_all | solution.py:411
  68.5 2.3 %gather.7 = (bf16[272,128]{1,0:T(8,128)(2,1)}, bf16[272,128]{1,0:T(8,128)(2,1)}, bf16[272,128]{1,0:T(8,128)(2,1)}, bf16[272,128]{1,0:T(8,128)(2,1)}) custom-call(s32[3]{0:T(128)} %pad_add_fusion.place_ref, s32[32]{0:T(128)} %copy-done.4, f32[1]{0:T(128)S(6)} %copy.15.weight_ref, s32[64,128]{1,0:T(8,128)} %bitcast.23, bf16[64,40,128]{2,1,0:T(8,128)(2,1)} %copy-done.10), custom_call_target="tpu_custom_call" | custom-call | bytes 1000000 | tf_op jit(solution)/shard_map/gather/pallas_call | solution.py:127
  70.8 3.4 %collective-permute-start.2 = (bf16[272,128]{1,0:T(8,128)(2,1)}, bf16[272,128]{1,0:T(8,128)(2,1)S(1)}, u32[]{:S(2)}, u32[]{:S(2)}) collective-permute-start(bf16[272,128]{1,0:T(8,128)(2,1)} %get-tuple-element.29), channel_id=1, source_target_pairs={{0,1},{1,0},{2,3},{3,2},{4,5},{5,4},{6,7},{7,6},{8,9},{9,8},{10,11... | collective-permute-start | bytes 208904 | tf_op jit(solution)/shard_map/ppermute | solution.py:416
  74.2 4.6 %collective-permute-start.3 = (bf16[272,128]{1,0:T(8,128)(2,1)}, bf16[272,128]{1,0:T(8,128)(2,1)S(1)}, u32[]{:S(2)}, u32[]{:S(2)}) collective-permute-start(bf16[272,128]{1,0:T(8,128)(2,1)} %get-tuple-element.30), channel_id=1, source_target_pairs={{0,2},{1,3},{2,0},{3,1},{4,6},{5,7},{6,4},{7,5},{8,10},{9,11},{10,... | collective-permute-start | bytes 208904 | tf_op jit(solution)/shard_map/ppermute | solution.py:416
  78.8 2.4 %collective-permute-start.4 = (bf16[272,128]{1,0:T(8,128)(2,1)}, bf16[272,128]{1,0:T(8,128)(2,1)S(1)}, u32[]{:S(2)}, u32[]{:S(2)}) collective-permute-start(bf16[272,128]{1,0:T(8,128)(2,1)} %get-tuple-element.31), channel_id=1, source_target_pairs={{0,3},{1,2},{2,1},{3,0},{4,7},{5,6},{6,5},{7,4},{8,11},{9,10},{10,... | collective-permute-start | bytes 208904 | tf_op jit(solution)/shard_map/ppermute | solution.py:416
  82.1 4.4 %collective-permute-done.4.refs_3_ = bf16[272,128]{1,0:T(8,128)(2,1)S(1)} collective-permute-done((bf16[272,128]{1,0:T(8,128)(2,1)}, bf16[272,128]{1,0:T(8,128)(2,1)S(1)}, u32[]{:S(2)}, u32[]{:S(2)}) %collective-permute-start.4) | collective-permute-done | bytes 69664 | tf_op jit(solution)/shard_map/ppermute | solution.py:416
  88.0 8.8 %attention.1 = (f32[128,256]{1,0:T(8,128)S(1)}, bf16[128,128]{1,0:T(8,128)(2,1)S(1)}, bf16[64,256]{1,0:T(8,128)(2,1)S(1)}, bf16[64,256]{1,0:T(8,128)(2,1)S(1)}, bf16[4,8,16,128]{3,2,1,0:T(8,128)(2,1)}) custom-call(s32[3]{0:T(128)S(1)} %copy-done.3, s32[32]{0:T(128)S(1)} %copy-done.5, bf16[3,64,1024]{2,1,0:T(8,128)(2,1)S(1)} %copy-done.6, ...), custom_call_target="tpu_custom_call" | custom-call | flops 900000000 | bytes 2000000 | tf_op jit(solution)/shard_map/attention/pallas_call | solution.py:310
  97.4 3.3 %all-to-all-start.2 = ((bf16[32,16,128]{2,1,0:T(8,128)(2,1)}), bf16[32,16,128]{2,1,0:T(8,128)(2,1)S(1)}, u32[]{:S(2)}, u32[]{:S(2)}) async-start(bf16[32,16,128]{2,1,0:T(8,128)(2,1)} %bitcast.7), calls=%async_computation.2 | async-start | bytes 262144 | tf_op jit(solution)/shard_map/all_to_all | solution.py:411
  100.7 5.9 %all-to-all-done.2 = bf16[32,16,128]{2,1,0:T(8,128)(2,1)S(1)} async-done(((bf16[32,16,128]{2,1,0:T(8,128)(2,1)}), bf16[32,16,128]{2,1,0:T(8,128)(2,1)S(1)}, u32[]{:S(2)}, u32[]{:S(2)}) %all-to-all-start.2) | async-done | bytes 131104 | tf_op jit(solution)/shard_map/all_to_all | solution.py:411
  108.1 12.9 %all-to-all-start.3 = ((bf16[64,24,128]{2,1,0:T(8,128)(2,1)}), bf16[64,24,128]{2,1,0:T(8,128)(2,1)S(1)}, u32[]{:S(2)}, u32[]{:S(2)}) async-start(bf16[64,24,128]{2,1,0:T(8,128)(2,1)} %pad_maximum_fusion), calls=%async_computation.3 | async-start | bytes 786432 | tf_op jit(solution)/shard_map/all_to_all | solution.py:411
  121.1 3.4 %collective-permute-start.5 = (bf16[64,256]{1,0:T(8,128)(2,1)S(1)}, bf16[64,256]{1,0:T(8,128)(2,1)S(1)}, u32[]{:S(2)}, u32[]{:S(2)}) collective-permute-start(bf16[64,256]{1,0:T(8,128)(2,1)S(1)} %get-tuple-element.35), channel_id=1, source_target_pairs={{0,8},{8,16},{16,24},{24,32},{32,40},{40,48},{48,56},{56,64},{64,7... | collective-permute-start | bytes 98312 | tf_op jit(solution)/shard_map/ppermute | solution.py:499
  124.5 2.5 %collective-permute-start.6 = (bf16[64,256]{1,0:T(8,128)(2,1)S(1)}, bf16[64,256]{1,0:T(8,128)(2,1)S(1)}, u32[]{:S(2)}, u32[]{:S(2)}) collective-permute-start(bf16[64,256]{1,0:T(8,128)(2,1)S(1)} %get-tuple-element.36), channel_id=1, source_target_pairs={{8,0},{16,8},{24,16},{32,24},{40,32},{48,40},{56,48},{64,56},{72,6... | collective-permute-start | bytes 98312 | tf_op jit(solution)/shard_map/ppermute | solution.py:498
  127.0 3.4 %collective-permute-done.6.high_ref = bf16[64,256]{1,0:T(8,128)(2,1)S(1)} collective-permute-done((bf16[64,256]{1,0:T(8,128)(2,1)S(1)}, bf16[64,256]{1,0:T(8,128)(2,1)S(1)}, u32[]{:S(2)}, u32[]{:S(2)}) %collective-permute-start.6) | collective-permute-done | bytes 32800 | tf_op jit(solution)/shard_map/ppermute | solution.py:498
  130.3 14.2 %all-to-all-done.3.arrived_ref = bf16[64,24,128]{2,1,0:T(8,128)(2,1)S(1)} async-done(((bf16[64,24,128]{2,1,0:T(8,128)(2,1)}), bf16[64,24,128]{2,1,0:T(8,128)(2,1)S(1)}, u32[]{:S(2)}, u32[]{:S(2)}) %all-to-all-start.3) | async-done | bytes 393248 | tf_op jit(solution)/shard_map/all_to_all | solution.py:411
  147.3 5.3 %all-to-all-start.4 = ((bf16[16,8,128]{2,1,0:T(8,128)(2,1)}), bf16[16,8,128]{2,1,0:T(8,128)(2,1)S(1)}, u32[]{:S(2)}, u32[]{:S(2)}) async-start(bf16[16,8,128]{2,1,0:T(8,128)(2,1)} %get-tuple-element.40), calls=%async_computation.4 | async-start | bytes 65536 | tf_op jit(solution)/shard_map/all_to_all | solution.py:411
  152.5 2.5 %collective-permute-start.7 = (bf16[4,16,128]{2,1,0:T(8,128)(2,1)S(1)}, bf16[4,16,128]{2,1,0:T(8,128)(2,1)S(1)}, u32[]{:S(2)}, u32[]{:S(2)}) collective-permute-start(bf16[4,16,128]{2,1,0:T(8,128)(2,1)S(1)} %copy-done.23), channel_id=1, source_target_pairs={{0,1},{1,0},{2,3},{3,2},{4,5},{5,4},{6,7},{7,6},{8,9},{9,8},{10,11... | collective-permute-start | bytes 49160 | tf_op jit(solution)/shard_map/ppermute | solution.py:416
  155.0 4.0 %collective-permute-start.8 = (bf16[4,16,128]{2,1,0:T(8,128)(2,1)S(1)}, bf16[4,16,128]{2,1,0:T(8,128)(2,1)S(1)}, u32[]{:S(2)}, u32[]{:S(2)}) collective-permute-start(bf16[4,16,128]{2,1,0:T(8,128)(2,1)S(1)} %copy-done.22), channel_id=1, source_target_pairs={{0,2},{1,3},{2,0},{3,1},{4,6},{5,7},{6,4},{7,5},{8,10},{9,11},{10,... | collective-permute-start | bytes 49160 | tf_op jit(solution)/shard_map/ppermute | solution.py:416
  159.0 4.0 %collective-permute-start.9 = (bf16[4,16,128]{2,1,0:T(8,128)(2,1)S(1)}, bf16[4,16,128]{2,1,0:T(8,128)(2,1)S(1)}, u32[]{:S(2)}, u32[]{:S(2)}) collective-permute-start(bf16[4,16,128]{2,1,0:T(8,128)(2,1)S(1)} %copy-done.21), channel_id=1, source_target_pairs={{0,3},{1,2},{2,1},{3,0},{4,7},{5,6},{6,5},{7,4},{8,11},{9,10},{10,... | collective-permute-start | bytes 49160 | tf_op jit(solution)/shard_map/ppermute | solution.py:416
  163.0 2.8 %collective-permute-done.9.refs_3_ = bf16[4,16,128]{2,1,0:T(8,128)(2,1)S(1)} collective-permute-done((bf16[4,16,128]{2,1,0:T(8,128)(2,1)S(1)}, bf16[4,16,128]{2,1,0:T(8,128)(2,1)S(1)}, u32[]{:S(2)}, u32[]{:S(2)}) %collective-permute-start.9) | collective-permute-done | bytes 16416 | tf_op jit(solution)/shard_map/ppermute | solution.py:416
  (77 shorter events, 12.6 us)
Async XLA Ops:
  4.0 18.9 %copy-start.20 = (bf16[256,128]{1,0:T(8,128)(2,1)S(1)}, bf16[256,128]{1,0:T(8,128)(2,1)}, u32[]{:S(2)}) copy-start(bf16[256,128]{1,0:T(8,128)(2,1)} %get-tuple-element.26) | copy-start | bytes 196612
  4.0 22.3 %copy-start.19 = (bf16[256,128]{1,0:T(8,128)(2,1)S(1)}, bf16[256,128]{1,0:T(8,128)(2,1)}, u32[]{:S(2)}) copy-start(bf16[256,128]{1,0:T(8,128)(2,1)} %get-tuple-element.27) | copy-start | bytes 196612
  4.0 82.4 %copy-start.7 = (bf16[128,1024]{1,0:T(8,128)(2,1)S(1)}, bf16[128,1024]{1,0:T(8,128)(2,1)}, u32[]{:S(2)}) copy-start(bf16[128,1024]{1,0:T(8,128)(2,1)} %query_ref.1) | copy-start | bytes 786436
  4.0 82.4 %copy-start.8 = (bf16[128,1024]{1,0:T(8,128)(2,1)S(1)}, bf16[128,1024]{1,0:T(8,128)(2,1)}, u32[]{:S(2)}) copy-start(bf16[128,1024]{1,0:T(8,128)(2,1)} %cot_ref.1) | copy-start | bytes 786436
  4.0 57.2 %all-to-all-start = ((bf16[64,40,128]{2,1,0:T(8,128)(2,1)}), bf16[64,40,128]{2,1,0:T(8,128)(2,1)S(1)}, u32[]{:S(2)}, u32[]{:S(2)}) async-start(bf16[64,40,128]{2,1,0:T(8,128)(2,1)} %get-tuple-element.25), calls=%async_computation | async-start | bytes 1310720 | tf_op jit(solution)/shard_map/all_to_all | solution.py:411
  22.9 58.3 %collective-permute-start = (bf16[256,128]{1,0:T(8,128)(2,1)S(1)}, bf16[256,128]{1,0:T(8,128)(2,1)S(1)}, u32[]{:S(2)}, u32[]{:S(2)}) collective-permute-start(bf16[256,128]{1,0:T(8,128)(2,1)S(1)} %copy-done.20), channel_id=1, source_target_pairs={{0,8},{8,16},{16,24},{24,32},{32,40},{40,48},{48,56},{56,64},{64,7... | collective-permute-start | bytes 196616 | tf_op jit(solution)/shard_map/ppermute | solution.py:467
  26.3 54.9 %collective-permute-start.1 = (bf16[256,128]{1,0:T(8,128)(2,1)S(1)}, bf16[256,128]{1,0:T(8,128)(2,1)S(1)}, u32[]{:S(2)}, u32[]{:S(2)}) collective-permute-start(bf16[256,128]{1,0:T(8,128)(2,1)S(1)} %copy-done.19), channel_id=1, source_target_pairs={{8,0},{16,8},{24,16},{32,24},{40,32},{48,40},{56,48},{64,56},{72,6... | collective-permute-start | bytes 196616 | tf_op jit(solution)/shard_map/ppermute | solution.py:468
  29.7 56.8 %copy-start.6 = (bf16[3,64,1024]{2,1,0:T(8,128)(2,1)S(1)}, bf16[3,64,1024]{2,1,0:T(8,128)(2,1)}, u32[]{:S(2)}) copy-start(bf16[3,64,1024]{2,1,0:T(8,128)(2,1)} %refs_ref.1) | copy-start | bytes 1179652
  61.9 24.5 %all-to-all-start.1 = ((bf16[32,8,128]{2,1,0:T(8,128)(2,1)}), bf16[32,8,128]{2,1,0:T(8,128)(2,1)S(1)}, u32[]{:S(2)}, u32[]{:S(2)}) async-start(bf16[32,8,128]{2,1,0:T(8,128)(2,1)} %broadcast_in_dim.28), calls=%async_computation.1 | async-start | bytes 131072 | tf_op jit(solution)/shard_map/all_to_all | solution.py:411
  68.4 18.1 %copy-start = (bf16[128,1024]{1,0:T(8,128)(2,1)S(1)}, bf16[128,1024]{1,0:T(8,128)(2,1)}, u32[]{:S(2)}) copy-start(bf16[128,1024]{1,0:T(8,128)(2,1)} %key_ref.3) | copy-start | bytes 786436
  68.4 18.1 %copy-start.1 = (bf16[128,1024]{1,0:T(8,128)(2,1)S(1)}, bf16[128,1024]{1,0:T(8,128)(2,1)}, u32[]{:S(2)}) copy-start(bf16[128,1024]{1,0:T(8,128)(2,1)} %value_ref.3) | copy-start | bytes 786436
  70.8 10.5 %collective-permute-start.2 = (bf16[272,128]{1,0:T(8,128)(2,1)}, bf16[272,128]{1,0:T(8,128)(2,1)S(1)}, u32[]{:S(2)}, u32[]{:S(2)}) collective-permute-start(bf16[272,128]{1,0:T(8,128)(2,1)} %get-tuple-element.29), channel_id=1, source_target_pairs={{0,1},{1,0},{2,3},{3,2},{4,5},{5,4},{6,7},{7,6},{8,9},{9,8},{10,11... | collective-permute-start | bytes 208904 | tf_op jit(solution)/shard_map/ppermute | solution.py:416
  74.2 7.9 %collective-permute-start.3 = (bf16[272,128]{1,0:T(8,128)(2,1)}, bf16[272,128]{1,0:T(8,128)(2,1)S(1)}, u32[]{:S(2)}, u32[]{:S(2)}) collective-permute-start(bf16[272,128]{1,0:T(8,128)(2,1)} %get-tuple-element.30), channel_id=1, source_target_pairs={{0,2},{1,3},{2,0},{3,1},{4,6},{5,7},{6,4},{7,5},{8,10},{9,11},{10,... | collective-permute-start | bytes 208904 | tf_op jit(solution)/shard_map/ppermute | solution.py:416
  78.8 7.6 %collective-permute-start.4 = (bf16[272,128]{1,0:T(8,128)(2,1)}, bf16[272,128]{1,0:T(8,128)(2,1)S(1)}, u32[]{:S(2)}, u32[]{:S(2)}) collective-permute-start(bf16[272,128]{1,0:T(8,128)(2,1)} %get-tuple-element.31), channel_id=1, source_target_pairs={{0,3},{1,2},{2,1},{3,0},{4,7},{5,6},{6,5},{7,4},{8,11},{9,10},{10,... | collective-permute-start | bytes 208904 | tf_op jit(solution)/shard_map/ppermute | solution.py:416
  97.4 9.3 %all-to-all-start.2 = ((bf16[32,16,128]{2,1,0:T(8,128)(2,1)}), bf16[32,16,128]{2,1,0:T(8,128)(2,1)S(1)}, u32[]{:S(2)}, u32[]{:S(2)}) async-start(bf16[32,16,128]{2,1,0:T(8,128)(2,1)} %bitcast.7), calls=%async_computation.2 | async-start | bytes 262144 | tf_op jit(solution)/shard_map/all_to_all | solution.py:411
  108.1 36.4 %all-to-all-start.3 = ((bf16[64,24,128]{2,1,0:T(8,128)(2,1)}), bf16[64,24,128]{2,1,0:T(8,128)(2,1)S(1)}, u32[]{:S(2)}, u32[]{:S(2)}) async-start(bf16[64,24,128]{2,1,0:T(8,128)(2,1)} %pad_maximum_fusion), calls=%async_computation.3 | async-start | bytes 786432 | tf_op jit(solution)/shard_map/all_to_all | solution.py:411
  121.1 5.9 %collective-permute-start.5 = (bf16[64,256]{1,0:T(8,128)(2,1)S(1)}, bf16[64,256]{1,0:T(8,128)(2,1)S(1)}, u32[]{:S(2)}, u32[]{:S(2)}) collective-permute-start(bf16[64,256]{1,0:T(8,128)(2,1)S(1)} %get-tuple-element.35), channel_id=1, source_target_pairs={{0,8},{8,16},{16,24},{24,32},{32,40},{40,48},{48,56},{56,64},{64,7... | collective-permute-start | bytes 98312 | tf_op jit(solution)/shard_map/ppermute | solution.py:499
  124.5 5.9 %collective-permute-start.6 = (bf16[64,256]{1,0:T(8,128)(2,1)S(1)}, bf16[64,256]{1,0:T(8,128)(2,1)S(1)}, u32[]{:S(2)}, u32[]{:S(2)}) collective-permute-start(bf16[64,256]{1,0:T(8,128)(2,1)S(1)} %get-tuple-element.36), channel_id=1, source_target_pairs={{8,0},{16,8},{24,16},{32,24},{40,32},{48,40},{56,48},{64,56},{72,6... | collective-permute-start | bytes 98312 | tf_op jit(solution)/shard_map/ppermute | solution.py:498
  127.0 20.3 %copy-start.14 = (bf16[64,256]{1,0:T(8,128)(2,1)}, bf16[64,256]{1,0:T(8,128)(2,1)S(1)}, u32[]{:S(2)}) copy-start(bf16[64,256]{1,0:T(8,128)(2,1)S(1)} %collective-permute-done.5.low_ref) | copy-start | bytes 98308
  130.3 16.9 %copy-start.15 = (bf16[64,256]{1,0:T(8,128)(2,1)}, bf16[64,256]{1,0:T(8,128)(2,1)S(1)}, u32[]{:S(2)}) copy-start(bf16[64,256]{1,0:T(8,128)(2,1)S(1)} %collective-permute-done.6.high_ref) | copy-start | bytes 98308
  147.3 18.6 %all-to-all-start.4 = ((bf16[16,8,128]{2,1,0:T(8,128)(2,1)}), bf16[16,8,128]{2,1,0:T(8,128)(2,1)S(1)}, u32[]{:S(2)}, u32[]{:S(2)}) async-start(bf16[16,8,128]{2,1,0:T(8,128)(2,1)} %get-tuple-element.40), calls=%async_computation.4 | async-start | bytes 65536 | tf_op jit(solution)/shard_map/all_to_all | solution.py:411
  152.5 10.5 %collective-permute-start.7 = (bf16[4,16,128]{2,1,0:T(8,128)(2,1)S(1)}, bf16[4,16,128]{2,1,0:T(8,128)(2,1)S(1)}, u32[]{:S(2)}, u32[]{:S(2)}) collective-permute-start(bf16[4,16,128]{2,1,0:T(8,128)(2,1)S(1)} %copy-done.23), channel_id=1, source_target_pairs={{0,1},{1,0},{2,3},{3,2},{4,5},{5,4},{6,7},{7,6},{8,9},{9,8},{10,11... | collective-permute-start | bytes 49160 | tf_op jit(solution)/shard_map/ppermute | solution.py:416
  155.0 8.0 %collective-permute-start.8 = (bf16[4,16,128]{2,1,0:T(8,128)(2,1)S(1)}, bf16[4,16,128]{2,1,0:T(8,128)(2,1)S(1)}, u32[]{:S(2)}, u32[]{:S(2)}) collective-permute-start(bf16[4,16,128]{2,1,0:T(8,128)(2,1)S(1)} %copy-done.22), channel_id=1, source_target_pairs={{0,2},{1,3},{2,0},{3,1},{4,6},{5,7},{6,4},{7,5},{8,10},{9,11},{10,... | collective-permute-start | bytes 49160 | tf_op jit(solution)/shard_map/ppermute | solution.py:416
  159.0 6.8 %collective-permute-start.9 = (bf16[4,16,128]{2,1,0:T(8,128)(2,1)S(1)}, bf16[4,16,128]{2,1,0:T(8,128)(2,1)S(1)}, u32[]{:S(2)}, u32[]{:S(2)}) collective-permute-start(bf16[4,16,128]{2,1,0:T(8,128)(2,1)S(1)} %copy-done.21), channel_id=1, source_target_pairs={{0,3},{1,2},{2,1},{3,0},{4,7},{5,6},{6,5},{7,4},{8,11},{9,10},{10,... | collective-permute-start | bytes 49160 | tf_op jit(solution)/shard_map/ppermute | solution.py:416
  (15 other events, 43.6 us)

commit v4 on v3

--- a/solution.py
+++ b/solution.py
@@ -81,9 +81,17 @@
 
 
 def gather_kernel(
-    part_rows, block_total, place_ref, table_ref, weight_ref, ids_ref, incoming_ref, *out_refs
+    steps,
+    requests,
+    part_rows,
+    block_total,
+    glob_ref,
+    table_ref,
+    weight_ref,
+    ids_ref,
+    incoming_ref,
+    *out_refs,
 ):
-    requests = table_ref.shape[0] // len(out_refs)
     lane = lax.broadcasted_iota(jnp.int32, (1, HEAD_DIM), 1)
 
     def block_row(block, half):
@@ -93,8 +101,8 @@
     def pair_row(left, right):
         return jnp.where(lane < BLOCK, block_row(left, 0), block_row(right, 1))
 
-    first = place_ref[0] * 2
-    glob = place_ref[2]
+    first = lax.axis_index("seq") * 2
+    glob = glob_ref[0]
     below = jnp.maximum(first - 1, 0)
     above = jnp.minimum(first + 2, block_total - 1)
     shared = [pair_row(below, first), pair_row(first + 1, above), pair_row(glob, glob)]
@@ -105,8 +113,8 @@
     middle = rest.astype(BF16).astype(F32)
     pieces = jnp.where(lane == 0, high, jnp.where(lane == 1, middle, rest - middle))
     blank = jnp.zeros((NOTE_ROWS - 5 - requests // 2, HEAD_DIM), F32)
-    for step, out_ref in enumerate(out_refs):
-        base = place_ref[1] ^ step
+    for step, out_ref in zip(steps, out_refs):
+        base = lax.axis_index("base") ^ step
         for request in range(requests):
             owner = table_ref[base * requests + request] // 2
             out_ref[request * 2 * part_rows : (request + 1) * 2 * part_rows] = incoming_ref[
@@ -122,16 +130,17 @@
         out_ref[requests * 2 * part_rows :] = notes.astype(BF16)
 
 
-def gather(place, table, weight, ids, incoming, bases, part_rows, block_total):
-    rows = table.shape[0] // bases * 2 * part_rows + NOTE_ROWS
+def gather(glob_block, table, weight, ids, incoming, steps, bases, part_rows, block_total):
+    requests = table.shape[0] // bases
+    rows = requests * 2 * part_rows + NOTE_ROWS
     return pl.pallas_call(
-        functools.partial(gather_kernel, part_rows, block_total),
-        out_shape=[jax.ShapeDtypeStruct((rows, HEAD_DIM), BF16)] * bases,
+        functools.partial(gather_kernel, steps, requests, part_rows, block_total),
+        out_shape=[jax.ShapeDtypeStruct((rows, HEAD_DIM), BF16)] * len(steps),
         in_specs=[SMEM, SMEM, SMEM, VMEM, VMEM],
-        out_specs=[VMEM] * bases,
+        out_specs=[VMEM] * len(steps),
         cost_estimate=pl.CostEstimate(flops=0, bytes_accessed=1_000_000, transcendentals=0),
         name="gather",
-    )(place, table, weight, ids, incoming)
+    )(glob_block, table, weight, ids, incoming)
 
 
 def attention_kernel(
@@ -474,9 +483,10 @@
         jnp.broadcast_to(piece[None], (ways,) + piece.shape), "seq", runs(seq_count, ways)
     ).reshape(low.shape)
     ids = sample_ids.reshape(-1, HEAD_DIM)
-    rand = swapped(
-        gather(place, my_table, mix_weight, ids, incoming, base_count, part_rows, block_total)
-    )
+    sources = (global_block, my_table, mix_weight, ids, incoming)
+    sizes = (base_count, part_rows, block_total)
+    others = gather(*sources, range(1, base_count), *sizes)
+    rand = swapped(gather(*sources, range(1), *sizes) + others)
 
     local, glob_term, low_rim, high_rim, rand_term = attention(
         place,

time: 169 us -> 167 us (0.988)
  waiting for transfers between devices: 63 us -> 60.8 us
  Pallas kernels: 17.2 us -> 19 us
    ppermute x6, waiting for transfers between devices: 8.01 us -> 5.96 us  [swapped(): lax.ppermute(arrays[step], 'base', [(i, i ^ step) for i in range(len(arra...]
    pallas_call x1 -> x2, Pallas kernels: 2.34 us -> 4.21 us  [gather(): pl.pallas_call(functools.partial(gather_kernel, steps, requests, part_row...]
  transfers between devices with their start and end apart: 15 -> 15, of which waited for: 7 -> 6; matrix products, arithmetic and copies ran while one was open for 1% -> 1% of each run, Pallas kernels for 1% -> 3%
where the time goes in v4:
time: 167 us; the launch traced here: 166 us
  starting transfers between devices  78.2 us (47%)
  waiting for transfers between devices  60.8 us (36%)
  Pallas kernels  19 us (11%)
  local copies, waits for them, and re-layouts  4.77 us (3%)
  between operations  1.77 us (1%)
    all_to_all x5, waiting for transfers between devices, exchange(): lax.all_to_all(array, axis, 0, 0, axis_index_groups=groups, tiled=True)  51.4 us
    all_to_all x5, starting transfers between devices, exchange(): lax.all_to_all(array, axis, 0, 0, axis_index_groups=groups, tiled=True)  45.7 us
    ppermute x6, starting transfers between devices, swapped(): lax.ppermute(arrays[step], 'base', [(i, i ^ step) for i in range(len(arra...  20.8 us
    pallas_call x1, Pallas kernels, attention(): pl.pallas_call(functools.partial(attention_kernel, samples, heads, part_r...  8.78 us
    ppermute x6, waiting for transfers between devices, swapped(): lax.ppermute(arrays[step], 'base', [(i, i ^ step) for i in range(len(arra...  5.96 us
    pallas_call x2, Pallas kernels, gather(): pl.pallas_call(functools.partial(gather_kernel, steps, requests, part_row...  4.21 us
    ppermute x1, starting transfers between devices, per_device(): below = lax.ppermute(high, 'seq', up)  3.37 us
    ppermute x1, starting transfers between devices, per_device(): from_below = lax.ppermute(high_rim, 'seq', up)  3.37 us
  transfers between devices with their start and end apart: 15, of which 6 were waited for; matrix products, arithmetic and copies ran while one was open for 1% of the time, Pallas kernels for 3%

profile of v4, /device:TPU:8, one launch (start us, length us, event | category | flops | bytes accessed | tf_op | source)
XLA Modules:
  0.0 166.2 jit_solution(18205428288540703707)
XLA Ops:
  1.5 2.4 %prepare.1 = (bf16[64,40,128]{2,1,0:T(8,128)(2,1)}, bf16[256,128]{1,0:T(8,128)(2,1)}, bf16[256,128]{1,0:T(8,128)(2,1)}) custom-call(s32[1]{0:T(128)} %copy.16.glob_ref, s32[64]{0:T(128)} %reduce_sum.27.pick_ref, bf16[128,1024]{1,0:T(8,128)(2,1)} %key_ref.3, bf16[128,1024]{1,0:T(8,128)(2,1)} %value_ref.3), custom_call_target="tpu_custom_call" | custom-call | bytes 1400000 | tf_op jit(solution)/shard_map/prepare/pallas_call | solution.py:69
  3.9 18.9 %all-to-all-start = ((bf16[64,40,128]{2,1,0:T(8,128)(2,1)}), bf16[64,40,128]{2,1,0:T(8,128)(2,1)S(1)}, u32[]{:S(2)}, u32[]{:S(2)}) async-start(bf16[64,40,128]{2,1,0:T(8,128)(2,1)} %get-tuple-element.24), calls=%async_computation | async-start | bytes 1310720 | tf_op jit(solution)/shard_map/all_to_all | solution.py:420
  22.8 3.4 %collective-permute-start = (bf16[256,128]{1,0:T(8,128)(2,1)S(1)}, bf16[256,128]{1,0:T(8,128)(2,1)S(1)}, u32[]{:S(2)}, u32[]{:S(2)}) collective-permute-start(bf16[256,128]{1,0:T(8,128)(2,1)S(1)} %copy-done.20), channel_id=1, source_target_pairs={{0,8},{8,16},{16,24},{24,32},{32,40},{40,48},{48,56},{56,64},{64,7... | collective-permute-start | bytes 196616 | tf_op jit(solution)/shard_map/ppermute | solution.py:476
  26.2 2.5 %collective-permute-start.1 = (bf16[256,128]{1,0:T(8,128)(2,1)S(1)}, bf16[256,128]{1,0:T(8,128)(2,1)S(1)}, u32[]{:S(2)}, u32[]{:S(2)}) collective-permute-start(bf16[256,128]{1,0:T(8,128)(2,1)S(1)} %copy-done.19), channel_id=1, source_target_pairs={{8,0},{16,8},{24,16},{32,24},{40,32},{48,40},{56,48},{64,56},{72,6... | collective-permute-start | bytes 196616 | tf_op jit(solution)/shard_map/ppermute | solution.py:477
  29.8 31.3 %all-to-all-done.incoming_ref = bf16[64,40,128]{2,1,0:T(8,128)(2,1)S(1)} async-done(((bf16[64,40,128]{2,1,0:T(8,128)(2,1)}), bf16[64,40,128]{2,1,0:T(8,128)(2,1)S(1)}, u32[]{:S(2)}, u32[]{:S(2)}) %all-to-all-start) | async-done | bytes 655392 | tf_op jit(solution)/shard_map/all_to_all | solution.py:420
  61.8 5.3 %all-to-all-start.1 = ((bf16[32,8,128]{2,1,0:T(8,128)(2,1)}), bf16[32,8,128]{2,1,0:T(8,128)(2,1)S(1)}, u32[]{:S(2)}, u32[]{:S(2)}) async-start(bf16[32,8,128]{2,1,0:T(8,128)(2,1)} %broadcast_in_dim.28), calls=%async_computation.1 | async-start | bytes 131072 | tf_op jit(solution)/shard_map/all_to_all | solution.py:420
  67.1 2.2 %gather.9 = (bf16[272,128]{1,0:T(8,128)(2,1)}, bf16[272,128]{1,0:T(8,128)(2,1)}, bf16[272,128]{1,0:T(8,128)(2,1)}) custom-call(s32[1]{0:T(128)} %copy.16.glob_ref, s32[32]{0:T(128)} %copy-done.5, f32[1]{0:T(128)S(6)} %copy.15.weight_ref, s32[64,128]{1,0:T(8,128)} %bitcast.23, bf16[64,40,128]{2,1,0:T(8,128)(2,1)} %copy-done.10), custom_call_target="tpu_custom_call" | custom-call | bytes 1000000 | tf_op jit(solution)/shard_map/gather/pallas_call | solution.py:136
  69.3 3.4 %collective-permute-start.2 = (bf16[272,128]{1,0:T(8,128)(2,1)}, bf16[272,128]{1,0:T(8,128)(2,1)S(1)}, u32[]{:S(2)}, u32[]{:S(2)}) collective-permute-start(bf16[272,128]{1,0:T(8,128)(2,1)} %get-tuple-element.27), channel_id=1, source_target_pairs={{0,1},{1,0},{2,3},{3,2},{4,5},{5,4},{6,7},{7,6},{8,9},{9,8},{10,11... | collective-permute-start | bytes 208904 | tf_op jit(solution)/shard_map/ppermute | solution.py:425
  72.7 4.6 %collective-permute-start.3 = (bf16[272,128]{1,0:T(8,128)(2,1)}, bf16[272,128]{1,0:T(8,128)(2,1)S(1)}, u32[]{:S(2)}, u32[]{:S(2)}) collective-permute-start(bf16[272,128]{1,0:T(8,128)(2,1)} %get-tuple-element.28), channel_id=1, source_target_pairs={{0,2},{1,3},{2,0},{3,1},{4,6},{5,7},{6,4},{7,5},{8,10},{9,11},{10,... | collective-permute-start | bytes 208904 | tf_op jit(solution)/shard_map/ppermute | solution.py:425
  77.4 2.4 %collective-permute-start.4 = (bf16[272,128]{1,0:T(8,128)(2,1)}, bf16[272,128]{1,0:T(8,128)(2,1)S(1)}, u32[]{:S(2)}, u32[]{:S(2)}) collective-permute-start(bf16[272,128]{1,0:T(8,128)(2,1)} %get-tuple-element.29), channel_id=1, source_target_pairs={{0,3},{1,2},{2,1},{3,0},{4,7},{5,6},{6,5},{7,4},{8,11},{9,10},{10,... | collective-permute-start | bytes 208904 | tf_op jit(solution)/shard_map/ppermute | solution.py:425
  81.9 3.1 %collective-permute-done.4.refs_3_ = bf16[272,128]{1,0:T(8,128)(2,1)S(1)} collective-permute-done((bf16[272,128]{1,0:T(8,128)(2,1)}, bf16[272,128]{1,0:T(8,128)(2,1)S(1)}, u32[]{:S(2)}, u32[]{:S(2)}) %collective-permute-start.4) | collective-permute-done | bytes 69664 | tf_op jit(solution)/shard_map/ppermute | solution.py:425
  86.0 8.8 %attention.1 = (f32[128,256]{1,0:T(8,128)S(1)}, bf16[128,128]{1,0:T(8,128)(2,1)S(1)}, bf16[64,256]{1,0:T(8,128)(2,1)S(1)}, bf16[64,256]{1,0:T(8,128)(2,1)S(1)}, bf16[4,8,16,128]{3,2,1,0:T(8,128)(2,1)}) custom-call(s32[3]{0:T(128)S(1)} %pad_add_fusion.place_ref, s32[32]{0:T(128)S(1)} %copy-done.6, bf16[3,64,1024]{2,1,0:T(8,128)(2,1)S(1)} %copy-done.7, ...), custom_call_target="tpu_custom_call" | custom-call | flops 900000000 | bytes 2000000 | tf_op jit(solution)/shard_map/attention/pallas_call | solution.py:319
  95.4 3.3 %all-to-all-start.2 = ((bf16[32,16,128]{2,1,0:T(8,128)(2,1)}), bf16[32,16,128]{2,1,0:T(8,128)(2,1)S(1)}, u32[]{:S(2)}, u32[]{:S(2)}) async-start(bf16[32,16,128]{2,1,0:T(8,128)(2,1)} %bitcast.7), calls=%async_computation.2 | async-start | bytes 262144 | tf_op jit(solution)/shard_map/all_to_all | solution.py:420
  98.7 5.9 %all-to-all-done.2 = bf16[32,16,128]{2,1,0:T(8,128)(2,1)S(1)} async-done(((bf16[32,16,128]{2,1,0:T(8,128)(2,1)}), bf16[32,16,128]{2,1,0:T(8,128)(2,1)S(1)}, u32[]{:S(2)}, u32[]{:S(2)}) %all-to-all-start.2) | async-done | bytes 131104 | tf_op jit(solution)/shard_map/all_to_all | solution.py:420
  106.1 12.9 %all-to-all-start.3 = ((bf16[64,24,128]{2,1,0:T(8,128)(2,1)}), bf16[64,24,128]{2,1,0:T(8,128)(2,1)S(1)}, u32[]{:S(2)}, u32[]{:S(2)}) async-start(bf16[64,24,128]{2,1,0:T(8,128)(2,1)} %pad_maximum_fusion), calls=%async_computation.3 | async-start | bytes 786432 | tf_op jit(solution)/shard_map/all_to_all | solution.py:420
  119.1 3.4 %collective-permute-start.5 = (bf16[64,256]{1,0:T(8,128)(2,1)S(1)}, bf16[64,256]{1,0:T(8,128)(2,1)S(1)}, u32[]{:S(2)}, u32[]{:S(2)}) collective-permute-start(bf16[64,256]{1,0:T(8,128)(2,1)S(1)} %get-tuple-element.33), channel_id=1, source_target_pairs={{0,8},{8,16},{16,24},{24,32},{32,40},{40,48},{48,56},{56,64},{64,7... | collective-permute-start | bytes 98312 | tf_op jit(solution)/shard_map/ppermute | solution.py:509
  122.5 2.5 %collective-permute-start.6 = (bf16[64,256]{1,0:T(8,128)(2,1)S(1)}, bf16[64,256]{1,0:T(8,128)(2,1)S(1)}, u32[]{:S(2)}, u32[]{:S(2)}) collective-permute-start(bf16[64,256]{1,0:T(8,128)(2,1)S(1)} %get-tuple-element.34), channel_id=1, source_target_pairs={{8,0},{16,8},{24,16},{32,24},{40,32},{48,40},{56,48},{64,56},{72,6... | collective-permute-start | bytes 98312 | tf_op jit(solution)/shard_map/ppermute | solution.py:508
  125.0 3.4 %collective-permute-done.6.high_ref = bf16[64,256]{1,0:T(8,128)(2,1)S(1)} collective-permute-done((bf16[64,256]{1,0:T(8,128)(2,1)S(1)}, bf16[64,256]{1,0:T(8,128)(2,1)S(1)}, u32[]{:S(2)}, u32[]{:S(2)}) %collective-permute-start.6) | collective-permute-done | bytes 32800 | tf_op jit(solution)/shard_map/ppermute | solution.py:508
  128.3 14.2 %all-to-all-done.3.arrived_ref = bf16[64,24,128]{2,1,0:T(8,128)(2,1)S(1)} async-done(((bf16[64,24,128]{2,1,0:T(8,128)(2,1)}), bf16[64,24,128]{2,1,0:T(8,128)(2,1)S(1)}, u32[]{:S(2)}, u32[]{:S(2)}) %all-to-all-start.3) | async-done | bytes 393248 | tf_op jit(solution)/shard_map/all_to_all | solution.py:420
  145.3 5.3 %all-to-all-start.4 = ((bf16[16,8,128]{2,1,0:T(8,128)(2,1)}), bf16[16,8,128]{2,1,0:T(8,128)(2,1)S(1)}, u32[]{:S(2)}, u32[]{:S(2)}) async-start(bf16[16,8,128]{2,1,0:T(8,128)(2,1)} %get-tuple-element.38), calls=%async_computation.4 | async-start | bytes 65536 | tf_op jit(solution)/shard_map/all_to_all | solution.py:420
  150.5 2.5 %collective-permute-start.7 = (bf16[4,16,128]{2,1,0:T(8,128)(2,1)S(1)}, bf16[4,16,128]{2,1,0:T(8,128)(2,1)S(1)}, u32[]{:S(2)}, u32[]{:S(2)}) collective-permute-start(bf16[4,16,128]{2,1,0:T(8,128)(2,1)S(1)} %copy-done.23), channel_id=1, source_target_pairs={{0,1},{1,0},{2,3},{3,2},{4,5},{5,4},{6,7},{7,6},{8,9},{9,8},{10,11... | collective-permute-start | bytes 49160 | tf_op jit(solution)/shard_map/ppermute | solution.py:425
  153.0 4.0 %collective-permute-start.8 = (bf16[4,16,128]{2,1,0:T(8,128)(2,1)S(1)}, bf16[4,16,128]{2,1,0:T(8,128)(2,1)S(1)}, u32[]{:S(2)}, u32[]{:S(2)}) collective-permute-start(bf16[4,16,128]{2,1,0:T(8,128)(2,1)S(1)} %copy-done.22), channel_id=1, source_target_pairs={{0,2},{1,3},{2,0},{3,1},{4,6},{5,7},{6,4},{7,5},{8,10},{9,11},{10,... | collective-permute-start | bytes 49160 | tf_op jit(solution)/shard_map/ppermute | solution.py:425
  157.0 4.0 %collective-permute-start.9 = (bf16[4,16,128]{2,1,0:T(8,128)(2,1)S(1)}, bf16[4,16,128]{2,1,0:T(8,128)(2,1)S(1)}, u32[]{:S(2)}, u32[]{:S(2)}) collective-permute-start(bf16[4,16,128]{2,1,0:T(8,128)(2,1)S(1)} %copy-done.21), channel_id=1, source_target_pairs={{0,3},{1,2},{2,1},{3,0},{4,7},{5,6},{6,5},{7,4},{8,11},{9,10},{10,... | collective-permute-start | bytes 49160 | tf_op jit(solution)/shard_map/ppermute | solution.py:425
  161.0 2.8 %collective-permute-done.9.refs_3_ = bf16[4,16,128]{2,1,0:T(8,128)(2,1)S(1)} collective-permute-done((bf16[4,16,128]{2,1,0:T(8,128)(2,1)S(1)}, bf16[4,16,128]{2,1,0:T(8,128)(2,1)S(1)}, u32[]{:S(2)}, u32[]{:S(2)}) %collective-permute-start.9) | collective-permute-done | bytes 16416 | tf_op jit(solution)/shard_map/ppermute | solution.py:425
  (78 shorter events, 12.1 us)
Async XLA Ops:
  3.9 18.9 %copy-start.20 = (bf16[256,128]{1,0:T(8,128)(2,1)S(1)}, bf16[256,128]{1,0:T(8,128)(2,1)}, u32[]{:S(2)}) copy-start(bf16[256,128]{1,0:T(8,128)(2,1)} %get-tuple-element.25) | copy-start | bytes 196612
  3.9 22.3 %copy-start.19 = (bf16[256,128]{1,0:T(8,128)(2,1)S(1)}, bf16[256,128]{1,0:T(8,128)(2,1)}, u32[]{:S(2)}) copy-start(bf16[256,128]{1,0:T(8,128)(2,1)} %get-tuple-element.26) | copy-start | bytes 196612
  3.9 57.2 %all-to-all-start = ((bf16[64,40,128]{2,1,0:T(8,128)(2,1)}), bf16[64,40,128]{2,1,0:T(8,128)(2,1)S(1)}, u32[]{:S(2)}, u32[]{:S(2)}) async-start(bf16[64,40,128]{2,1,0:T(8,128)(2,1)} %get-tuple-element.24), calls=%async_computation | async-start | bytes 1310720 | tf_op jit(solution)/shard_map/all_to_all | solution.py:420
  22.8 59.1 %collective-permute-start = (bf16[256,128]{1,0:T(8,128)(2,1)S(1)}, bf16[256,128]{1,0:T(8,128)(2,1)S(1)}, u32[]{:S(2)}, u32[]{:S(2)}) collective-permute-start(bf16[256,128]{1,0:T(8,128)(2,1)S(1)} %copy-done.20), channel_id=1, source_target_pairs={{0,8},{8,16},{16,24},{24,32},{32,40},{40,48},{48,56},{56,64},{64,7... | collective-permute-start | bytes 196616 | tf_op jit(solution)/shard_map/ppermute | solution.py:476
  26.2 55.7 %collective-permute-start.1 = (bf16[256,128]{1,0:T(8,128)(2,1)S(1)}, bf16[256,128]{1,0:T(8,128)(2,1)S(1)}, u32[]{:S(2)}, u32[]{:S(2)}) collective-permute-start(bf16[256,128]{1,0:T(8,128)(2,1)S(1)} %copy-done.19), channel_id=1, source_target_pairs={{8,0},{16,8},{24,16},{32,24},{40,32},{48,40},{56,48},{64,56},{72,6... | collective-permute-start | bytes 196616 | tf_op jit(solution)/shard_map/ppermute | solution.py:477
  61.8 23.2 %all-to-all-start.1 = ((bf16[32,8,128]{2,1,0:T(8,128)(2,1)}), bf16[32,8,128]{2,1,0:T(8,128)(2,1)S(1)}, u32[]{:S(2)}, u32[]{:S(2)}) async-start(bf16[32,8,128]{2,1,0:T(8,128)(2,1)} %broadcast_in_dim.28), calls=%async_computation.1 | async-start | bytes 131072 | tf_op jit(solution)/shard_map/all_to_all | solution.py:420
  67.1 17.9 %copy-start.7 = (bf16[3,64,1024]{2,1,0:T(8,128)(2,1)S(1)}, bf16[3,64,1024]{2,1,0:T(8,128)(2,1)}, u32[]{:S(2)}) copy-start(bf16[3,64,1024]{2,1,0:T(8,128)(2,1)} %refs_ref.1) | copy-start | bytes 1179652
  67.1 17.9 %copy-start.8 = (bf16[128,1024]{1,0:T(8,128)(2,1)S(1)}, bf16[128,1024]{1,0:T(8,128)(2,1)}, u32[]{:S(2)}) copy-start(bf16[128,1024]{1,0:T(8,128)(2,1)} %query_ref.1) | copy-start | bytes 786436
  67.1 17.9 %copy-start.9 = (bf16[128,1024]{1,0:T(8,128)(2,1)S(1)}, bf16[128,1024]{1,0:T(8,128)(2,1)}, u32[]{:S(2)}) copy-start(bf16[128,1024]{1,0:T(8,128)(2,1)} %cot_ref.1) | copy-start | bytes 786436
  69.3 12.5 %collective-permute-start.2 = (bf16[272,128]{1,0:T(8,128)(2,1)}, bf16[272,128]{1,0:T(8,128)(2,1)S(1)}, u32[]{:S(2)}, u32[]{:S(2)}) collective-permute-start(bf16[272,128]{1,0:T(8,128)(2,1)} %get-tuple-element.27), channel_id=1, source_target_pairs={{0,1},{1,0},{2,3},{3,2},{4,5},{5,4},{6,7},{7,6},{8,9},{9,8},{10,11... | collective-permute-start | bytes 208904 | tf_op jit(solution)/shard_map/ppermute | solution.py:425
  72.7 9.1 %collective-permute-start.3 = (bf16[272,128]{1,0:T(8,128)(2,1)}, bf16[272,128]{1,0:T(8,128)(2,1)S(1)}, u32[]{:S(2)}, u32[]{:S(2)}) collective-permute-start(bf16[272,128]{1,0:T(8,128)(2,1)} %get-tuple-element.28), channel_id=1, source_target_pairs={{0,2},{1,3},{2,0},{3,1},{4,6},{5,7},{6,4},{7,5},{8,10},{9,11},{10,... | collective-permute-start | bytes 208904 | tf_op jit(solution)/shard_map/ppermute | solution.py:425
  77.4 7.6 %collective-permute-start.4 = (bf16[272,128]{1,0:T(8,128)(2,1)}, bf16[272,128]{1,0:T(8,128)(2,1)S(1)}, u32[]{:S(2)}, u32[]{:S(2)}) collective-permute-start(bf16[272,128]{1,0:T(8,128)(2,1)} %get-tuple-element.29), channel_id=1, source_target_pairs={{0,3},{1,2},{2,1},{3,0},{4,7},{5,6},{6,5},{7,4},{8,11},{9,10},{10,... | collective-permute-start | bytes 208904 | tf_op jit(solution)/shard_map/ppermute | solution.py:425
  95.4 9.3 %all-to-all-start.2 = ((bf16[32,16,128]{2,1,0:T(8,128)(2,1)}), bf16[32,16,128]{2,1,0:T(8,128)(2,1)S(1)}, u32[]{:S(2)}, u32[]{:S(2)}) async-start(bf16[32,16,128]{2,1,0:T(8,128)(2,1)} %bitcast.7), calls=%async_computation.2 | async-start | bytes 262144 | tf_op jit(solution)/shard_map/all_to_all | solution.py:420
  106.1 36.4 %all-to-all-start.3 = ((bf16[64,24,128]{2,1,0:T(8,128)(2,1)}), bf16[64,24,128]{2,1,0:T(8,128)(2,1)S(1)}, u32[]{:S(2)}, u32[]{:S(2)}) async-start(bf16[64,24,128]{2,1,0:T(8,128)(2,1)} %pad_maximum_fusion), calls=%async_computation.3 | async-start | bytes 786432 | tf_op jit(solution)/shard_map/all_to_all | solution.py:420
  119.1 5.9 %collective-permute-start.5 = (bf16[64,256]{1,0:T(8,128)(2,1)S(1)}, bf16[64,256]{1,0:T(8,128)(2,1)S(1)}, u32[]{:S(2)}, u32[]{:S(2)}) collective-permute-start(bf16[64,256]{1,0:T(8,128)(2,1)S(1)} %get-tuple-element.33), channel_id=1, source_target_pairs={{0,8},{8,16},{16,24},{24,32},{32,40},{40,48},{48,56},{56,64},{64,7... | collective-permute-start | bytes 98312 | tf_op jit(solution)/shard_map/ppermute | solution.py:509
  122.5 5.9 %collective-permute-start.6 = (bf16[64,256]{1,0:T(8,128)(2,1)S(1)}, bf16[64,256]{1,0:T(8,128)(2,1)S(1)}, u32[]{:S(2)}, u32[]{:S(2)}) collective-permute-start(bf16[64,256]{1,0:T(8,128)(2,1)S(1)} %get-tuple-element.34), channel_id=1, source_target_pairs={{8,0},{16,8},{24,16},{32,24},{40,32},{48,40},{56,48},{64,56},{72,6... | collective-permute-start | bytes 98312 | tf_op jit(solution)/shard_map/ppermute | solution.py:508
  125.0 20.3 %copy-start.14 = (bf16[64,256]{1,0:T(8,128)(2,1)}, bf16[64,256]{1,0:T(8,128)(2,1)S(1)}, u32[]{:S(2)}) copy-start(bf16[64,256]{1,0:T(8,128)(2,1)S(1)} %collective-permute-done.5.low_ref) | copy-start | bytes 98308
  128.3 16.9 %copy-start.15 = (bf16[64,256]{1,0:T(8,128)(2,1)}, bf16[64,256]{1,0:T(8,128)(2,1)S(1)}, u32[]{:S(2)}) copy-start(bf16[64,256]{1,0:T(8,128)(2,1)S(1)} %collective-permute-done.6.high_ref) | copy-start | bytes 98308
  145.2 7.8 %copy-start.22 = (bf16[4,16,128]{2,1,0:T(8,128)(2,1)S(1)}, bf16[4,16,128]{2,1,0:T(8,128)(2,1)}, u32[]{:S(2)}) copy-start(bf16[4,16,128]{2,1,0:T(8,128)(2,1)} %get-tuple-element.41) | copy-start | bytes 49156
  145.2 11.8 %copy-start.21 = (bf16[4,16,128]{2,1,0:T(8,128)(2,1)S(1)}, bf16[4,16,128]{2,1,0:T(8,128)(2,1)}, u32[]{:S(2)}) copy-start(bf16[4,16,128]{2,1,0:T(8,128)(2,1)} %get-tuple-element.42) | copy-start | bytes 49156
  145.3 18.6 %all-to-all-start.4 = ((bf16[16,8,128]{2,1,0:T(8,128)(2,1)}), bf16[16,8,128]{2,1,0:T(8,128)(2,1)S(1)}, u32[]{:S(2)}, u32[]{:S(2)}) async-start(bf16[16,8,128]{2,1,0:T(8,128)(2,1)} %get-tuple-element.38), calls=%async_computation.4 | async-start | bytes 65536 | tf_op jit(solution)/shard_map/all_to_all | solution.py:420
  150.5 10.5 %collective-permute-start.7 = (bf16[4,16,128]{2,1,0:T(8,128)(2,1)S(1)}, bf16[4,16,128]{2,1,0:T(8,128)(2,1)S(1)}, u32[]{:S(2)}, u32[]{:S(2)}) collective-permute-start(bf16[4,16,128]{2,1,0:T(8,128)(2,1)S(1)} %copy-done.23), channel_id=1, source_target_pairs={{0,1},{1,0},{2,3},{3,2},{4,5},{5,4},{6,7},{7,6},{8,9},{9,8},{10,11... | collective-permute-start | bytes 49160 | tf_op jit(solution)/shard_map/ppermute | solution.py:425
  153.0 8.0 %collective-permute-start.8 = (bf16[4,16,128]{2,1,0:T(8,128)(2,1)S(1)}, bf16[4,16,128]{2,1,0:T(8,128)(2,1)S(1)}, u32[]{:S(2)}, u32[]{:S(2)}) collective-permute-start(bf16[4,16,128]{2,1,0:T(8,128)(2,1)S(1)} %copy-done.22), channel_id=1, source_target_pairs={{0,2},{1,3},{2,0},{3,1},{4,6},{5,7},{6,4},{7,5},{8,10},{9,11},{10,... | collective-permute-start | bytes 49160 | tf_op jit(solution)/shard_map/ppermute | solution.py:425
  157.0 6.8 %collective-permute-start.9 = (bf16[4,16,128]{2,1,0:T(8,128)(2,1)S(1)}, bf16[4,16,128]{2,1,0:T(8,128)(2,1)S(1)}, u32[]{:S(2)}, u32[]{:S(2)}) collective-permute-start(bf16[4,16,128]{2,1,0:T(8,128)(2,1)S(1)} %copy-done.21), channel_id=1, source_target_pairs={{0,3},{1,2},{2,1},{3,0},{4,7},{5,6},{6,5},{7,4},{8,11},{9,10},{10,... | collective-permute-start | bytes 49160 | tf_op jit(solution)/shard_map/ppermute | solution.py:425
  (15 other events, 40.6 us)
